TPU v7x, 256 devices: a whole 4x4x8 slice. The times are simulated.
256 devices in a mesh: ka: 64 (over z, x_lo, y), ba: 4 (over x_hi, core).
Axes of the slice: x: 4 (x_hi: 2, x_lo: 2; x = x_hi * 2 + x_lo), y: 4, z: 8, core: 2. Of those that a mesh axis runs over, the one named last changes fastest.
Arguments:
- orbitals: bfloat16 [64, 4, 2, 32, 1024], P('ka', 'ba'), may hold values from -6 to 6
- kpoints: int32 [64, 3], replicated, may hold values from 0 to 7, as said below
- occupied: int32 [64], replicated, may hold values from 1 to 4, as said below
Outputs:
- exchange_terms: float32 [64, 4, 2, 32, 1024], P('ka', 'ba')
Inputs may be any that keep to these rules, and one draw needn't show every extreme that they name: `kpoints`: distinct points of the 8 x 8 x 8 k-mesh; the point (0, 0, 0) and the far corner are among them. Some k-point has all 4 bands occupied and some only one.
All inputs are finite; a program needn't handle non-finite values.
Results may differ from a plain program's by a relative error of at most 0.008.
Values may be sent and summed in bfloat16 or wider, within the bound.
No kernel may reach another device: no remote copies, remote signals or barrier semaphores. Data moves between devices by JAX's collectives and lax.ppermute only.
A program may use at most 64 MiB of HBM per device.

v0:
```python
import functools
import math

import jax
import jax.numpy as jnp
import numpy as np
from jax import lax
from jax.experimental import pallas as pl
from jax.experimental.pallas import tpu as pltpu
from jax.sharding import PartitionSpec as P

KMESH = 8
STEPS = 3
GRID = 32
LANES = 128
CELL = 20.52
SCREENING = 0.05


def complex_table(angle):
    cosine, sine = np.cos(angle), np.sin(angle)
    return np.block([[cosine, sine], [-sine, cosine]])


def first_tables():
    a, x = [v.reshape(-1) for v in np.meshgrid(np.arange(4), np.arange(32), indexing="ij")]
    tables = []
    for b in range(2):
        turns = x[:, None] * x[None, :] + 8 * a[:, None] * a[None, :] + 4 * b * a[:, None]
        tables.append(complex_table(2 * math.pi / 32 * (turns % 32)))
    return np.stack(tables).astype(jnp.bfloat16)


def second_tables():
    low, z = [v.reshape(-1) for v in np.meshgrid(np.arange(4), np.arange(32), indexing="ij")]
    tables = []
    for k1 in range(8):
        turns = low[:, None] * (k1 + 8 * low[None, :]) + z[:, None] * z[None, :]
        tables.append(complex_table(2 * math.pi / 32 * (turns % 32).T).T)
    return np.stack(tables).astype(jnp.bfloat16)


def block(index):
    return slice(index * LANES, (index + 1) * LANES)


def rows(index):
    return slice(index * GRID, (index + 1) * GRID)


def dot(left, right, dims=((1,), (0,))):
    return lax.dot_general(left, right, (dims, ((), ())), preferred_element_type=jnp.float32)


def pair_kernel(step, n_count, first, kpoints, occupied, spot, mate, *refs):
    bands = refs[:n_count]
    refs = refs[n_count:]
    sums_in = None if first else refs[0]
    refs = refs if first else refs[1:]
    forward_x, inverse_x, forward_yz, inverse_yz, mate_out, sums, wide, mid, back = refs

    count = kpoints.shape[0]
    own = spot[0]
    slot = spot[1]
    other = lax.rem(own - step + count, count)
    along = []
    for i in range(3):
        apart = lax.rem(kpoints[own, i] - kpoints[other, i] + KMESH // 2 + KMESH, KMESH)
        along.append((apart - KMESH // 2).astype(jnp.float32) / KMESH)
    mate_weight = jnp.where(slot < occupied[other], -1.0, 0.0)
    unit = 2 * math.pi / CELL

    def centred(index):
        return jnp.bitwise_and(index + GRID // 2, GRID - 1) - GRID // 2

    shape = (GRID, LANES)
    lane = lax.broadcasted_iota(jnp.int32, shape, 1)
    at_x = (centred(lax.broadcasted_iota(jnp.int32, shape, 0)).astype(jnp.float32) + along[0]) * unit
    at_z = (centred(jnp.bitwise_and(lane, GRID - 1)).astype(jnp.float32) + along[2]) * unit
    high = lax.shift_right_logical(lane, 5) * 8

    for b in range(2):
        for a in range(4):
            cut = block(2 * a + b)
            mate_re = mate[0, :, cut].astype(jnp.float32)
            mate_im = mate[1, :, cut].astype(jnp.float32)
            for n in range(n_count):
                band_re = bands[n][0, :, cut].astype(jnp.float32)
                band_im = bands[n][1, :, cut].astype(jnp.float32)
                wide[b, rows(a), block(n)] = (mate_re * band_re + mate_im * band_im).astype(jnp.bfloat16)
                wide[b, rows(4 + a), block(n)] = (mate_re * band_im - mate_im * band_re).astype(jnp.bfloat16)

    for n in range(0, n_count, 2):
        pair = slice(n * LANES, (n + 2) * LANES)
        even = dot(forward_x[0], wide[0, :, pair])
        odd = dot(forward_x[1], wide[1, :, pair])
        plus = (even + odd).astype(jnp.bfloat16)
        minus = (even - odd).astype(jnp.bfloat16)
        for i in range(2):
            for e in range(4):
                for c in range(2):
                    mid[e, rows(n + i), block(c)] = plus[rows(4 * c + e), block(i)]
                    mid[e + 4, rows(n + i), block(c)] = minus[rows(4 * c + e), block(i)]

    for e in range(4):
        halves = []
        for k1 in (e, e + 4):
            third = dot(mid[k1], forward_yz[k1])
            at_y = (centred(high + k1).astype(jnp.float32) + along[1]) * unit
            squared = at_x * at_x + at_y * at_y + at_z * at_z
            screened = (math.pi / GRID**3) / (squared + SCREENING)
            screened = jnp.concatenate([screened, screened], axis=1)
            screened = jnp.concatenate([screened] * n_count, axis=0)
            halves.append(dot((third * screened).astype(jnp.bfloat16), inverse_yz[k1]))
        for b in range(2):
            joined = (halves[0] + halves[1] if b == 0 else halves[0] - halves[1]).astype(jnp.bfloat16)
            for n in range(n_count):
                for c in range(2):
                    back[b, rows(4 * c + e), block(n)] = joined[rows(n), block(c)]

    for b in range(2):
        for n in range(0, n_count, 2):
            pair = slice(n * LANES, (n + 2) * LANES)
            wide_out = dot(inverse_x[b], back[b, :, pair])
            for a in range(4):
                cut = block(2 * a + b)
                mate_re = mate[0, :, cut].astype(jnp.float32) * mate_weight
                mate_im = mate[1, :, cut].astype(jnp.float32) * mate_weight
                total_re = total_im = None
                for i in range(2):
                    band = slot ^ (n + i)
                    weight = jnp.where(band < occupied[own], -1.0, 0.0)
                    wave_re = wide_out[rows(a), block(i)]
                    wave_im = wide_out[rows(4 + a), block(i)]
                    term_re = mate_re * wave_re - mate_im * wave_im
                    term_im = mate_re * wave_im + mate_im * wave_re
                    if not first:
                        term_re = term_re + sums_in[n + i, 0, :, cut]
                        term_im = term_im + sums_in[n + i, 1, :, cut]
                    sums[n + i, 0, :, cut] = term_re
                    sums[n + i, 1, :, cut] = term_im
                    band_re = bands[n + i][0, :, cut].astype(jnp.float32) * weight
                    band_im = bands[n + i][1, :, cut].astype(jnp.float32) * weight
                    back_re = band_re * wave_re + band_im * wave_im
                    back_im = band_im * wave_re - band_re * wave_im
                    total_re = back_re if total_re is None else total_re + back_re
                    total_im = back_im if total_im is None else total_im + back_im
                if n == 0:
                    mate_out[0, :, cut] = total_re
                    mate_out[1, :, cut] = total_im
                else:
                    mate_out[0, :, cut] += total_re
                    mate_out[1, :, cut] += total_im


def pair_terms(step, kpoints, occupied, spot, mate, bands, sums, tables):
    n_count = len(bands)
    smem = pl.BlockSpec(memory_space=pltpu.SMEM)
    vmem = pl.BlockSpec(memory_space=pltpu.VMEM)
    first = sums is None
    field = mate.shape
    operands = [mate, *bands] + ([] if first else [sums]) + list(tables)
    return pl.pallas_call(
        functools.partial(pair_kernel, step, n_count, first),
        out_shape=[
            jax.ShapeDtypeStruct(field, jnp.float32),
            jax.ShapeDtypeStruct((n_count,) + field, jnp.float32),
        ],
        in_specs=[smem] * 3 + [vmem] * len(operands),
        out_specs=[vmem, vmem],
        scratch_shapes=[
            pltpu.VMEM((2, 256, n_count * LANES), jnp.bfloat16),
            pltpu.VMEM((8, n_count * GRID, 256), jnp.bfloat16),
            pltpu.VMEM((2, 256, n_count * LANES), jnp.bfloat16),
        ],
        compiler_params=pltpu.CompilerParams(vmem_limit_bytes=32 * 1024 * 1024),
        cost_estimate=pl.CostEstimate(flops=2 * 10**9, bytes_accessed=6 * 10**6, transcendentals=0),
    )(kpoints, occupied, spot, *operands)


def passed_along(value, by):
    count = lax.axis_size("ka")
    return lax.ppermute(value, "ka", [(i, (i + by) % count) for i in range(count)])


def swapped(value, flip):
    return lax.ppermute(value, "ba", [(i, i ^ flip) for i in range(lax.axis_size("ba"))])


def on_device(orbitals, kpoints, occupied):
    own = orbitals[0, 0]
    spot = jnp.stack([lax.axis_index("ka"), lax.axis_index("ba")])
    forward_x = first_tables()
    forward_yz = second_tables()
    tables = (
        jnp.asarray(forward_x),
        jnp.asarray(forward_x.transpose(0, 2, 1)),
        jnp.asarray(forward_yz),
        jnp.asarray(forward_yz.transpose(0, 2, 1)),
    )
    mates = [passed_along(own, step) for step in range(1, STEPS + 1)]
    bands = [own] + [swapped(own, flip) for flip in (1, 2, 3)]
    sums = None
    total = None
    for step in range(1, STEPS + 1):
        mate_term, sums = pair_terms(
            step, kpoints, occupied, spot, mates[step - 1], bands, sums, tables
        )
        returned = passed_along(mate_term.astype(jnp.bfloat16), -step).astype(jnp.float32)
        total = returned if total is None else total + returned
    total = total + sums[0]
    for flip in (1, 2, 3):
        total = total + swapped(sums[flip].astype(jnp.bfloat16), flip).astype(jnp.float32)
    return total[None, None]


def solution(mesh):
    in_specs = (P("ka", "ba", None, None, None), P(), P())
    out_specs = P("ka", "ba", None, None, None)
    return jax.shard_map(
        on_device, mesh=mesh, in_specs=in_specs, out_specs=out_specs, check_vma=False
    )
```

profile of v0, /device:TPU:6, one launch (start us, length us, event | category | flops | bytes accessed | tf_op | source)
XLA Modules:
  0.0 54.5 jit_solution(15246482681694900885)
XLA Ops:
  0.0 0.8 %collective-permute-start.3 = (bf16[2,32,1024]{2,1,0:T(8,128)(2,1)}, bf16[2,32,1024]{2,1,0:T(8,128)(2,1)S(1)}, u32[]{:S(2)}, u32[]{:S(2)}) collective-permute-start(bf16[2,32,1024]{2,1,0:T(8,128)(2,1)} %bitcast.21), channel_id=1, source_target_pairs={{0,3},{1,2},{2,1},{3,0},{4,7},{5,6},{6,5},{7,4},{8,11},{9,10},{10,... | collective-permute-start | bytes 393224 | tf_op jit(solution)/shard_map/ppermute | solution.py:187
  0.8 2.1 %collective-permute-start.2 = (bf16[2,32,1024]{2,1,0:T(8,128)(2,1)}, bf16[2,32,1024]{2,1,0:T(8,128)(2,1)S(1)}, u32[]{:S(2)}, u32[]{:S(2)}) collective-permute-start(bf16[2,32,1024]{2,1,0:T(8,128)(2,1)} %bitcast.22), channel_id=1, source_target_pairs={{0,2},{1,3},{2,0},{3,1},{4,6},{5,7},{6,4},{7,5},{8,10},{9,11},{10,... | collective-permute-start | bytes 393224 | tf_op jit(solution)/shard_map/ppermute | solution.py:187
  3.0 0.4 collective-permute-start.1
  3.4 1.6 %collective-permute-start = (bf16[2,32,1024]{2,1,0:T(8,128)(2,1)}, bf16[2,32,1024]{2,1,0:T(8,128)(2,1)S(1)}, u32[]{:S(2)}, u32[]{:S(2)}) collective-permute-start(bf16[2,32,1024]{2,1,0:T(8,128)(2,1)} %bitcast.24), channel_id=1, source_target_pairs={{0,4},{4,8},{8,12},{12,16},{16,20},{20,24},{24,28},{28,32},{32,36}... | collective-permute-start | bytes 393224 | tf_op jit(solution)/shard_map/ppermute | solution.py:183
  4.9 3.3 %collective-permute-start.7 = (bf16[2,32,1024]{2,1,0:T(8,128)(2,1)}, bf16[2,32,1024]{2,1,0:T(8,128)(2,1)S(1)}, u32[]{:S(2)}, u32[]{:S(2)}) collective-permute-start(bf16[2,32,1024]{2,1,0:T(8,128)(2,1)} %bitcast.25), channel_id=1, source_target_pairs={{0,12},{4,16},{8,20},{12,24},{16,28},{20,32},{24,36},{28,40},{32,4... | collective-permute-start | bytes 393224 | tf_op jit(solution)/shard_map/ppermute | solution.py:183
  8.2 0.0 copy-start.8
  8.2 0.7 %copy-done.8 = s32[64,3]{0,1:T(4,128)S(1)} copy-done((s32[64,3]{0,1:T(4,128)S(1)}, s32[64,3]{0,1:T(4,128)}, u32[]{:S(2)}) %copy-start.8) | copy-done | bytes 792
  8.9 0.1 copy.8.kpoints
  9.0 0.0 copy-start.2
  9.0 0.1 pad_add_fusion.spot
  9.1 0.0 collective-permute-done.3.refs_3_
  9.1 2.0 %collective-permute-start.5 = (bf16[2,32,1024]{2,1,0:T(8,128)(2,1)}, bf16[2,32,1024]{2,1,0:T(8,128)(2,1)S(1)}, u32[]{:S(2)}, u32[]{:S(2)}) collective-permute-start(bf16[2,32,1024]{2,1,0:T(8,128)(2,1)} %bitcast.26), channel_id=1, source_target_pairs={{0,8},{4,12},{8,16},{12,20},{16,24},{20,28},{24,32},{28,36},{32,40... | collective-permute-start | bytes 393224 | tf_op jit(solution)/shard_map/ppermute | solution.py:183
  11.1 0.0 collective-permute-done.2.refs_2_
  11.1 0.0 collective-permute-done.1.refs_1_
  11.1 2.5 %collective-permute-done.mate = bf16[2,32,1024]{2,1,0:T(8,128)(2,1)S(1)} collective-permute-done((bf16[2,32,1024]{2,1,0:T(8,128)(2,1)}, bf16[2,32,1024]{2,1,0:T(8,128)(2,1)S(1)}, u32[]{:S(2)}, u32[]{:S(2)}) %collective-permute-start) | collective-permute-done | bytes 131104 | tf_op jit(solution)/shard_map/ppermute | solution.py:183
  13.6 0.0 copy-done.2
  13.6 0.0 copy-start
  13.6 0.9 %copy-done = bf16[1,1,2,32,1024]{4,3,2,1,0:T(8,128)(2,1)S(1)} copy-done((bf16[1,1,2,32,1024]{4,3,2,1,0:T(8,128)(2,1)S(1)}, bf16[1,1,2,32,1024]{4,3,2,1,0:T(8,128)(2,1)}, u32[]{:S(2)}) %copy-start) | copy-done | bytes 131096
  14.5 0.0 copy-start.3
  14.5 1.2 %copy-done.3 = bf16[8,256,256]{2,1,0:T(8,128)(2,1)S(1)} copy-done((bf16[8,256,256]{2,1,0:T(8,128)(2,1)S(1)}, bf16[8,256,256]{2,1,0:T(8,128)(2,1)}, u32[]{:S(2)}) %copy-start.3) | copy-done | bytes 1048600
  15.7 0.0 copy-start.5
  15.7 1.2 %copy-done.5 = bf16[8,256,256]{2,1,0:T(8,128)(2,1)S(1)} copy-done((bf16[8,256,256]{2,1,0:T(8,128)(2,1)S(1)}, bf16[8,256,256]{2,1,0:T(8,128)(2,1)}, u32[]{:S(2)}) %copy-start.5) | copy-done | bytes 1048600
  17.0 0.0 copy-start.6
  17.0 0.9 %copy-done.6 = bf16[2,256,256]{2,1,0:T(8,128)(2,1)S(1)} copy-done((bf16[2,256,256]{2,1,0:T(8,128)(2,1)S(1)}, bf16[2,256,256]{2,1,0:T(8,128)(2,1)}, u32[]{:S(2)}) %copy-start.6) | copy-done | bytes 262168
  17.9 0.0 copy-start.7
  17.9 0.9 %copy-done.7 = bf16[2,256,256]{2,1,0:T(8,128)(2,1)S(1)} copy-done((bf16[2,256,256]{2,1,0:T(8,128)(2,1)S(1)}, bf16[2,256,256]{2,1,0:T(8,128)(2,1)}, u32[]{:S(2)}) %copy-start.7) | copy-done | bytes 262168
  18.9 2.6 %shard_map.73 = (f32[2,32,1024]{2,1,0:T(8,128)S(1)}, f32[4,2,32,1024]{3,2,1,0:T(8,128)S(1)}) custom-call(s32[64,3]{1,0:T(8,128)S(1)} %copy.8.kpoints, s32[64]{0:T(128)S(1)} %copy-done.2, s32[2]{0:T(128)S(1)} %pad_add_fusion.spot, bf16[2,32,1024]{2,1,0:T(8,128)(2,1)S(1)} %collective-permute-done.mate, bf16[2,32,1024]{2,1,0:T(8,128)(2,1)S(1)} %bitcast.27, ...), custom_call_target="tpu_custom_call" | custom-call | flops 2000000000 | bytes 6000000 | tf_op jit(solution)/shard_map/pallas_call | solution.py:163
  21.5 0.0 copy-start.1
  21.5 0.1 collective-permute-start.4
  21.6 0.0 collective-permute-done.5.mate
  21.6 0.0 copy-done.4
  21.7 0.8 %copy-done.1 = bf16[1,1,2,32,1024]{4,3,2,1,0:T(8,128)(2,1)S(1)} copy-done((bf16[1,1,2,32,1024]{4,3,2,1,0:T(8,128)(2,1)S(1)}, bf16[1,1,2,32,1024]{4,3,2,1,0:T(8,128)(2,1)}, u32[]{:S(2)}) %copy-start.1) | copy-done | bytes 131096
  22.4 2.7 %shard_map.74 = (f32[2,32,1024]{2,1,0:T(8,128)S(1)}, f32[4,2,32,1024]{3,2,1,0:T(8,128)S(1)}) custom-call(s32[64,3]{1,0:T(8,128)S(1)} %copy.8.kpoints, s32[64]{0:T(128)S(1)} %copy-done.2, s32[2]{0:T(128)S(1)} %pad_add_fusion.spot, bf16[2,32,1024]{2,1,0:T(8,128)(2,1)S(1)} %collective-permute-done.5.mate, bf16[2,32,1024]{2,1,0:T(8,128)(2,1)S(1)} %bitcast.28, ...), custom_call_target="tpu_custom_call" | custom-call | flops 2000000000 | bytes 6000000 | tf_op jit(solution)/shard_map/pallas_call | solution.py:163
  25.2 0.3 collective-permute-start.6
  25.4 0.0 collective-permute-done.7.mate
  25.5 2.7 %shard_map.75 = (f32[2,32,1024]{2,1,0:T(8,128)S(1)}, f32[4,2,32,1024]{3,2,1,0:T(8,128)S(1)}) custom-call(s32[64,3]{1,0:T(8,128)S(1)} %copy.8.kpoints, s32[64]{0:T(128)S(1)} %copy-done.2, s32[2]{0:T(128)S(1)} %pad_add_fusion.spot, bf16[2,32,1024]{2,1,0:T(8,128)(2,1)S(1)} %collective-permute-done.7.mate, bf16[2,32,1024]{2,1,0:T(8,128)(2,1)S(1)} %bitcast.29, ...), custom_call_target="tpu_custom_call" | custom-call | flops 2000000000 | bytes 6000000 | tf_op jit(solution)/shard_map/pallas_call | solution.py:163
  28.2 15.1 %collective-permute-start.8 = (bf16[2,32,1024]{2,1,0:T(8,128)(2,1)S(1)}, bf16[2,32,1024]{2,1,0:T(8,128)(2,1)S(1)}, u32[]{:S(2)}, u32[]{:S(2)}) collective-permute-start(bf16[2,32,1024]{2,1,0:T(8,128)(2,1)S(1)} %convert_element_type.43), channel_id=1, source_target_pairs={{0,244},{4,248},{8,252},{12,0},{16,4},{20,8},{24,12},{28,16},{32,2... | collective-permute-start | bytes 393224 | tf_op jit(solution)/shard_map/ppermute | solution.py:183
  43.3 0.1 convert.5
  43.4 0.1 collective-permute-start.9
  43.5 0.1 collective-permute-start.11
  43.6 0.0 collective-permute-done.4
  43.6 3.5 %collective-permute-start.10 = (bf16[2,32,1024]{2,1,0:T(8,128)(2,1)S(1)}, bf16[2,32,1024]{2,1,0:T(8,128)(2,1)S(1)}, u32[]{:S(2)}, u32[]{:S(2)}) collective-permute-start(bf16[2,32,1024]{2,1,0:T(8,128)(2,1)S(1)} %get-tuple-element.19), channel_id=1, source_target_pairs={{0,2},{1,3},{2,0},{3,1},{4,6},{5,7},{6,4},{7,5},{8,10},{9,11},{10,... | collective-permute-start | bytes 393224 | tf_op jit(solution)/shard_map/ppermute | solution.py:187
  47.2 0.0 collective-permute-done.6
  47.2 0.0 collective-permute-done.8
  47.2 0.0 collective-permute-done.9
  47.2 3.1 %collective-permute-done.11 = bf16[2,32,1024]{2,1,0:T(8,128)(2,1)S(1)} collective-permute-done((bf16[2,32,1024]{2,1,0:T(8,128)(2,1)S(1)}, bf16[2,32,1024]{2,1,0:T(8,128)(2,1)S(1)}, u32[]{:S(2)}, u32[]{:S(2)}) %collective-permute-start.11) | collective-permute-done | bytes 131104 | tf_op jit(solution)/shard_map/ppermute | solution.py:187
  50.4 3.4 %collective-permute-done.10 = bf16[2,32,1024]{2,1,0:T(8,128)(2,1)S(1)} collective-permute-done((bf16[2,32,1024]{2,1,0:T(8,128)(2,1)S(1)}, bf16[2,32,1024]{2,1,0:T(8,128)(2,1)S(1)}, u32[]{:S(2)}, u32[]{:S(2)}) %collective-permute-start.10) | collective-permute-done | bytes 131104 | tf_op jit(solution)/shard_map/ppermute | solution.py:187
  53.7 0.8 %fusion.3 = f32[1,1,2,32,1024]{4,3,2,1,0:T(8,128)} fusion(bf16[2,32,1024]{2,1,0:T(8,128)(2,1)S(1)} %collective-permute-done.11, bf16[2,32,1024]{2,1,0:T(8,128)(2,1)S(1)} %collective-permute-done.10, bf16[2,32,1024]{2,1,0:T(8,128)(2,1)S(1)} %collective-permute-done.9, f32[4,2,32,1024]{3,2,1,0:T(8,128)S(1)} %get-tuple-element.16, ...), kind=kLoop, calls=%fused_computation.4 | loop fusion | flops 786432 | bytes 1310720 | tf_op jit(solution)/shard_map/broadcast_in_dim | solution.py:214
  (5 shorter events, 0.1 us)
Async XLA Ops:
  0.0 9.1 %collective-permute-start.3 = (bf16[2,32,1024]{2,1,0:T(8,128)(2,1)}, bf16[2,32,1024]{2,1,0:T(8,128)(2,1)S(1)}, u32[]{:S(2)}, u32[]{:S(2)}) collective-permute-start(bf16[2,32,1024]{2,1,0:T(8,128)(2,1)} %bitcast.21), channel_id=1, source_target_pairs={{0,3},{1,2},{2,1},{3,0},{4,7},{5,6},{6,5},{7,4},{8,11},{9,10},{10,... | collective-permute-start | bytes 393224 | tf_op jit(solution)/shard_map/ppermute | solution.py:187
  0.8 10.2 %collective-permute-start.2 = (bf16[2,32,1024]{2,1,0:T(8,128)(2,1)}, bf16[2,32,1024]{2,1,0:T(8,128)(2,1)S(1)}, u32[]{:S(2)}, u32[]{:S(2)}) collective-permute-start(bf16[2,32,1024]{2,1,0:T(8,128)(2,1)} %bitcast.22), channel_id=1, source_target_pairs={{0,2},{1,3},{2,0},{3,1},{4,6},{5,7},{6,4},{7,5},{8,10},{9,11},{10,... | collective-permute-start | bytes 393224 | tf_op jit(solution)/shard_map/ppermute | solution.py:187
  3.0 8.1 %collective-permute-start.1 = (bf16[2,32,1024]{2,1,0:T(8,128)(2,1)}, bf16[2,32,1024]{2,1,0:T(8,128)(2,1)S(1)}, u32[]{:S(2)}, u32[]{:S(2)}) collective-permute-start(bf16[2,32,1024]{2,1,0:T(8,128)(2,1)} %bitcast.23), channel_id=1, source_target_pairs={{0,1},{1,0},{2,3},{3,2},{4,5},{5,4},{6,7},{7,6},{8,9},{9,8},{10,11... | collective-permute-start | bytes 393224 | tf_op jit(solution)/shard_map/ppermute | solution.py:187
  3.4 10.2 %collective-permute-start = (bf16[2,32,1024]{2,1,0:T(8,128)(2,1)}, bf16[2,32,1024]{2,1,0:T(8,128)(2,1)S(1)}, u32[]{:S(2)}, u32[]{:S(2)}) collective-permute-start(bf16[2,32,1024]{2,1,0:T(8,128)(2,1)} %bitcast.24), channel_id=1, source_target_pairs={{0,4},{4,8},{8,12},{12,16},{16,20},{20,24},{24,28},{28,32},{32,36}... | collective-permute-start | bytes 393224 | tf_op jit(solution)/shard_map/ppermute | solution.py:183
  4.9 20.5 %collective-permute-start.7 = (bf16[2,32,1024]{2,1,0:T(8,128)(2,1)}, bf16[2,32,1024]{2,1,0:T(8,128)(2,1)S(1)}, u32[]{:S(2)}, u32[]{:S(2)}) collective-permute-start(bf16[2,32,1024]{2,1,0:T(8,128)(2,1)} %bitcast.25), channel_id=1, source_target_pairs={{0,12},{4,16},{8,20},{12,24},{16,28},{20,32},{24,36},{28,40},{32,4... | collective-permute-start | bytes 393224 | tf_op jit(solution)/shard_map/ppermute | solution.py:183
  8.2 0.7 %copy-start.8 = (s32[64,3]{0,1:T(4,128)S(1)}, s32[64,3]{0,1:T(4,128)}, u32[]{:S(2)}) copy-start(s32[64,3]{0,1:T(4,128)} %param.8) | copy-start | bytes 2308
  9.0 4.6 %copy-start.2 = (s32[64]{0:T(128)S(1)}, s32[64]{0:T(128)}, u32[]{:S(2)}) copy-start(s32[64]{0:T(128)} %occupied.5) | copy-start | bytes 772
  9.1 12.6 %collective-permute-start.5 = (bf16[2,32,1024]{2,1,0:T(8,128)(2,1)}, bf16[2,32,1024]{2,1,0:T(8,128)(2,1)S(1)}, u32[]{:S(2)}, u32[]{:S(2)}) collective-permute-start(bf16[2,32,1024]{2,1,0:T(8,128)(2,1)} %bitcast.26), channel_id=1, source_target_pairs={{0,8},{4,12},{8,16},{12,20},{16,24},{20,28},{24,32},{28,36},{32,40... | collective-permute-start | bytes 393224 | tf_op jit(solution)/shard_map/ppermute | solution.py:183
  13.6 0.9 %copy-start = (bf16[1,1,2,32,1024]{4,3,2,1,0:T(8,128)(2,1)S(1)}, bf16[1,1,2,32,1024]{4,3,2,1,0:T(8,128)(2,1)}, u32[]{:S(2)}) copy-start(bf16[1,1,2,32,1024]{4,3,2,1,0:T(8,128)(2,1)} %param.7) | copy-start | bytes 393220
  14.5 1.2 %copy-start.3 = (bf16[8,256,256]{2,1,0:T(8,128)(2,1)S(1)}, bf16[8,256,256]{2,1,0:T(8,128)(2,1)}, u32[]{:S(2)}) copy-start(bf16[8,256,256]{2,1,0:T(8,128)(2,1)} %constant.20.clone.refs_7_.refs_8_) | copy-start | bytes 3145732
  15.7 1.2 %copy-start.5 = (bf16[8,256,256]{2,1,0:T(8,128)(2,1)S(1)}, bf16[8,256,256]{2,1,0:T(8,128)(2,1)}, u32[]{:S(2)}) copy-start(bf16[8,256,256]{2,1,0:T(8,128)(2,1)} %constant.19.clone.refs_6_.refs_7_) | copy-start | bytes 3145732
  17.0 0.9 %copy-start.6 = (bf16[2,256,256]{2,1,0:T(8,128)(2,1)S(1)}, bf16[2,256,256]{2,1,0:T(8,128)(2,1)}, u32[]{:S(2)}) copy-start(bf16[2,256,256]{2,1,0:T(8,128)(2,1)} %constant.18.clone.refs_5_.refs_6_) | copy-start | bytes 786436
  17.9 0.9 %copy-start.7 = (bf16[2,256,256]{2,1,0:T(8,128)(2,1)S(1)}, bf16[2,256,256]{2,1,0:T(8,128)(2,1)}, u32[]{:S(2)}) copy-start(bf16[2,256,256]{2,1,0:T(8,128)(2,1)} %constant.17.clone.refs_4_.refs_5_) | copy-start | bytes 786436
  18.9 2.8 %copy-start.4 = (bf16[8,256,256]{2,1,0:T(8,128)(2,1)S(1)}, bf16[8,256,256]{2,1,0:T(8,128)(2,1)}, u32[]{:S(2)}) copy-start(bf16[8,256,256]{2,1,0:T(8,128)(2,1)} %constant.20.clone.refs_7_.refs_8_) | copy-start | bytes 3145732
  21.5 0.9 %copy-start.1 = (bf16[1,1,2,32,1024]{4,3,2,1,0:T(8,128)(2,1)S(1)}, bf16[1,1,2,32,1024]{4,3,2,1,0:T(8,128)(2,1)}, u32[]{:S(2)}) copy-start(bf16[1,1,2,32,1024]{4,3,2,1,0:T(8,128)(2,1)} %param.7) | copy-start | bytes 393220
  21.5 22.1 %collective-permute-start.4 = (bf16[2,32,1024]{2,1,0:T(8,128)(2,1)S(1)}, bf16[2,32,1024]{2,1,0:T(8,128)(2,1)S(1)}, u32[]{:S(2)}, u32[]{:S(2)}) collective-permute-start(bf16[2,32,1024]{2,1,0:T(8,128)(2,1)S(1)} %convert_element_type.39), channel_id=1, source_target_pairs={{0,252},{4,0},{8,4},{12,8},{16,12},{20,16},{24,20},{28,24},{32,28}... | collective-permute-start | bytes 393224 | tf_op jit(solution)/shard_map/ppermute | solution.py:183
  25.2 22.0 %collective-permute-start.6 = (bf16[2,32,1024]{2,1,0:T(8,128)(2,1)S(1)}, bf16[2,32,1024]{2,1,0:T(8,128)(2,1)S(1)}, u32[]{:S(2)}, u32[]{:S(2)}) collective-permute-start(bf16[2,32,1024]{2,1,0:T(8,128)(2,1)S(1)} %convert_element_type.41), channel_id=1, source_target_pairs={{0,248},{4,252},{8,0},{12,4},{16,8},{20,12},{24,16},{28,20},{32,24... | collective-permute-start | bytes 393224 | tf_op jit(solution)/shard_map/ppermute | solution.py:183
  28.2 19.0 %collective-permute-start.8 = (bf16[2,32,1024]{2,1,0:T(8,128)(2,1)S(1)}, bf16[2,32,1024]{2,1,0:T(8,128)(2,1)S(1)}, u32[]{:S(2)}, u32[]{:S(2)}) collective-permute-start(bf16[2,32,1024]{2,1,0:T(8,128)(2,1)S(1)} %convert_element_type.43), channel_id=1, source_target_pairs={{0,244},{4,248},{8,252},{12,0},{16,4},{20,8},{24,12},{28,16},{32,2... | collective-permute-start | bytes 393224 | tf_op jit(solution)/shard_map/ppermute | solution.py:183
  43.4 3.8 %collective-permute-start.9 = (bf16[2,32,1024]{2,1,0:T(8,128)(2,1)S(1)}, bf16[2,32,1024]{2,1,0:T(8,128)(2,1)S(1)}, u32[]{:S(2)}, u32[]{:S(2)}) collective-permute-start(bf16[2,32,1024]{2,1,0:T(8,128)(2,1)S(1)} %get-tuple-element.17), channel_id=1, source_target_pairs={{0,1},{1,0},{2,3},{3,2},{4,5},{5,4},{6,7},{7,6},{8,9},{9,8},{10,11... | collective-permute-start | bytes 393224 | tf_op jit(solution)/shard_map/ppermute | solution.py:187
  43.5 6.8 %collective-permute-start.11 = (bf16[2,32,1024]{2,1,0:T(8,128)(2,1)S(1)}, bf16[2,32,1024]{2,1,0:T(8,128)(2,1)S(1)}, u32[]{:S(2)}, u32[]{:S(2)}) collective-permute-start(bf16[2,32,1024]{2,1,0:T(8,128)(2,1)S(1)} %get-tuple-element.18), channel_id=1, source_target_pairs={{0,3},{1,2},{2,1},{3,0},{4,7},{5,6},{6,5},{7,4},{8,11},{9,10},{10,... | collective-permute-start | bytes 393224 | tf_op jit(solution)/shard_map/ppermute | solution.py:187
  43.6 10.1 %collective-permute-start.10 = (bf16[2,32,1024]{2,1,0:T(8,128)(2,1)S(1)}, bf16[2,32,1024]{2,1,0:T(8,128)(2,1)S(1)}, u32[]{:S(2)}, u32[]{:S(2)}) collective-permute-start(bf16[2,32,1024]{2,1,0:T(8,128)(2,1)S(1)} %get-tuple-element.19), channel_id=1, source_target_pairs={{0,2},{1,3},{2,0},{3,1},{4,6},{5,7},{6,4},{7,5},{8,10},{9,11},{10,... | collective-permute-start | bytes 393224 | tf_op jit(solution)/shard_map/ppermute | solution.py:187
where the time goes:
time: 55.4 us; the launch traced here: 54.5 us
  starting transfers between devices  29.4 us (53%)
  waiting for transfers between devices  9.07 us (16%)
  Pallas kernels  8.1 us (15%)
  local copies, waits for them, and re-layouts  6.83 us (12%)
  other arithmetic  1 us (2%)
    ppermute x6, starting transfers between devices, passed_along(): lax.ppermute(value, 'ka', [(i, (i + by) % count) for i in range(count)])  22.3 us
    pallas_call x3, Pallas kernels, pair_terms(): pl.pallas_call(functools.partial(pair_kernel, step, n_count, first), out_...  8.1 us
    ppermute x6, starting transfers between devices, swapped(): lax.ppermute(value, 'ba', [(i, i ^ flip) for i in range(lax.axis_size('ba...  7.09 us
    unnamed x19, local copies, waits for them, and re-layouts  6.8 us
    ppermute x6, waiting for transfers between devices, swapped(): lax.ppermute(value, 'ba', [(i, i ^ flip) for i in range(lax.axis_size('ba...  6.5 us
    ppermute x6, waiting for transfers between devices, passed_along(): lax.ppermute(value, 'ka', [(i, (i + by) % count) for i in range(count)])  2.57 us
  transfers between devices with their start and end apart: 12, of which 3 were waited for; matrix products, arithmetic and copies ran while one was open for 1% of the time, Pallas kernels for 15%

commit v1 on v0

v1 whole, which is shorter than its diff:
```python
import functools
import math

import jax
import jax.numpy as jnp
import numpy as np
from jax import lax
from jax.experimental import pallas as pl
from jax.experimental.pallas import tpu as pltpu
from jax.sharding import PartitionSpec as P

KMESH = 8
SHIFTS = (1, 3, -2)
GRID = 32
LANES = 128
CELL = 20.52
SCREENING = 0.05
VMEM_BYTES = 32 * 1024 * 1024


def complex_table(angle):
    cosine, sine = np.cos(angle), np.sin(angle)
    return np.block([[cosine, sine], [-sine, cosine]])


def first_tables():
    a, x = [v.reshape(-1) for v in np.meshgrid(np.arange(4), np.arange(32), indexing="ij")]
    tables = []
    for b in range(2):
        turns = x[:, None] * x[None, :] + 8 * a[:, None] * a[None, :] + 4 * b * a[:, None]
        tables.append(complex_table(2 * math.pi / 32 * (turns % 32)))
    return np.stack(tables).astype(jnp.bfloat16)


def second_tables():
    low, z = [v.reshape(-1) for v in np.meshgrid(np.arange(4), np.arange(32), indexing="ij")]
    tables = []
    for k1 in range(8):
        turns = low[:, None] * (k1 + 8 * low[None, :]) + z[:, None] * z[None, :]
        tables.append(complex_table(2 * math.pi / 32 * (turns % 32).T).T)
    return np.stack(tables).astype(jnp.bfloat16)


def block(index):
    return slice(index * LANES, (index + 1) * LANES)


def rows(index):
    return slice(index * GRID, (index + 1) * GRID)


def dot(left, right, dims=((1,), (0,))):
    return lax.dot_general(left, right, (dims, ((), ())), preferred_element_type=jnp.float32)


def stage_kernel(kpoints, spot, *refs):
    tables = refs[:4]
    staged = refs[4:8]
    screened, sems = refs[8:]
    copies = [pltpu.make_async_copy(tables[i], staged[i], sems.at[i]) for i in range(4)]
    for copy in copies:
        copy.start()

    count = kpoints.shape[1]
    own = spot[0]
    unit = 2 * math.pi / CELL
    shape = (GRID, LANES)
    lane = lax.broadcasted_iota(jnp.int32, shape, 1)
    high = lax.shift_right_logical(lane, 5) * 8

    def centred(index):
        return (jnp.bitwise_and(index + GRID // 2, GRID - 1) - GRID // 2).astype(jnp.float32)

    grid_x = centred(lax.broadcasted_iota(jnp.int32, shape, 0))
    grid_z = centred(jnp.bitwise_and(lane, GRID - 1))
    for at, step in enumerate(SHIFTS):
        other = lax.rem(own - step + count, count)
        later, earlier = (own, other) if step > 0 else (other, own)
        along = []
        for i in range(3):
            apart = lax.rem(kpoints[i, later] - kpoints[i, earlier] + KMESH // 2 + KMESH, KMESH)
            along.append((apart - KMESH // 2).astype(jnp.float32) / KMESH)
        at_x = (grid_x + along[0]) * unit
        at_z = (grid_z + along[2]) * unit
        flat = at_x * at_x + at_z * at_z + SCREENING
        for k1 in range(8):
            at_y = (centred(high + k1) + along[1]) * unit
            screened[at, k1] = (math.pi / GRID**3) / (flat + at_y * at_y)
    for copy in copies:
        copy.wait()


def staged(kpoints, spot, tables):
    smem = pl.BlockSpec(memory_space=pltpu.SMEM)
    vmem = pl.BlockSpec(memory_space=pltpu.VMEM)
    return pl.pallas_call(
        stage_kernel,
        out_shape=[jax.ShapeDtypeStruct(t.shape, t.dtype) for t in tables]
        + [jax.ShapeDtypeStruct((len(SHIFTS), 8, GRID, LANES), jnp.float32)],
        in_specs=[smem] * 2 + [pl.BlockSpec(memory_space=pl.ANY)] * 4,
        out_specs=[vmem] * 5,
        scratch_shapes=[pltpu.SemaphoreType.DMA((4,))],
        compiler_params=pltpu.CompilerParams(vmem_limit_bytes=VMEM_BYTES),
        cost_estimate=pl.CostEstimate(flops=10**6, bytes_accessed=6 * 10**6, transcendentals=0),
    )(kpoints, spot, *tables)


def pair_kernel(at, flips, has_sums, has_mate, occupied, spot, mate, *refs):
    groups = len(flips)
    refs = list(refs)

    def take(n):
        taken = refs[:n]
        del refs[:n]
        return taken

    bands = take(groups)
    sums_in = take(groups) if has_sums else None
    mate_in = take(1)[0] if has_mate else None
    forward_x, inverse_x, forward_yz, inverse_yz, screened, mate_out = take(6)
    sums = take(groups)
    wide, mid, back = refs

    step = SHIFTS[at]
    turned = step < 0
    count = occupied.shape[0]
    own = spot[0]
    slot = spot[1]
    other = lax.rem(own - step + count, count)
    mate_weight = jnp.where(slot < occupied[other], -1.0, 0.0)

    for b in range(2):
        for a in range(4):
            cut = block(2 * a + b)
            mate_re = mate[0, :, cut].astype(jnp.float32)
            mate_im = mate[1, :, cut].astype(jnp.float32)
            for g in range(groups):
                for i in range(2):
                    band_re = bands[g][i, 0, :, cut].astype(jnp.float32)
                    band_im = bands[g][i, 1, :, cut].astype(jnp.float32)
                    value_re = mate_re * band_re + mate_im * band_im
                    if turned:
                        value_im = mate_im * band_re - mate_re * band_im
                    else:
                        value_im = mate_re * band_im - mate_im * band_re
                    wide[b, g, rows(a), block(i)] = value_re.astype(jnp.bfloat16)
                    wide[b, g, rows(4 + a), block(i)] = value_im.astype(jnp.bfloat16)

    for g in range(groups):
        even = dot(forward_x[0], wide[0, g])
        odd = dot(forward_x[1], wide[1, g])
        plus = (even + odd).astype(jnp.bfloat16)
        minus = (even - odd).astype(jnp.bfloat16)
        for i in range(2):
            for e in range(4):
                for c in range(2):
                    mid[e, rows(2 * g + i), block(c)] = plus[rows(4 * c + e), block(i)]
                    mid[e + 4, rows(2 * g + i), block(c)] = minus[rows(4 * c + e), block(i)]

    for e in range(4):
        halves = []
        for k1 in (e, e + 4):
            third = dot(mid[k1], forward_yz[k1])
            factor = screened[at, k1]
            factor = jnp.concatenate([factor, factor], axis=1)
            factor = jnp.concatenate([factor] * (2 * groups), axis=0)
            halves.append(dot((third * factor).astype(jnp.bfloat16), inverse_yz[k1]))
        for b in range(2):
            joined = (halves[0] - halves[1] if b else halves[0] + halves[1]).astype(jnp.bfloat16)
            for g in range(groups):
                for i in range(2):
                    for c in range(2):
                        back[b, g, rows(4 * c + e), block(i)] = joined[rows(2 * g + i), block(c)]

    for b in range(2):
        waves = [dot(inverse_x[b], back[b, g]) for g in range(groups)]
        for a in range(4):
            cut = block(2 * a + b)
            mate_re = mate[0, :, cut].astype(jnp.float32) * mate_weight
            mate_im = mate[1, :, cut].astype(jnp.float32) * mate_weight
            total_re = mate_in[0, :, cut] if has_mate else 0.0
            total_im = mate_in[1, :, cut] if has_mate else 0.0
            for g in range(groups):
                for i in range(2):
                    weight = jnp.where((slot ^ flips[g][i]) < occupied[own], -1.0, 0.0)
                    wave_re = waves[g][rows(a), block(i)]
                    wave_im = waves[g][rows(4 + a), block(i)]
                    band_re = bands[g][i, 0, :, cut].astype(jnp.float32) * weight
                    band_im = bands[g][i, 1, :, cut].astype(jnp.float32) * weight
                    if turned:
                        term_re = mate_re * wave_re + mate_im * wave_im
                        term_im = mate_im * wave_re - mate_re * wave_im
                        total_re = total_re + (band_re * wave_re - band_im * wave_im)
                        total_im = total_im + (band_re * wave_im + band_im * wave_re)
                    else:
                        term_re = mate_re * wave_re - mate_im * wave_im
                        term_im = mate_re * wave_im + mate_im * wave_re
                        total_re = total_re + (band_re * wave_re + band_im * wave_im)
                        total_im = total_im + (band_im * wave_re - band_re * wave_im)
                    if has_sums:
                        term_re = term_re + sums_in[g][i, 0, :, cut]
                        term_im = term_im + sums_in[g][i, 1, :, cut]
                    sums[g][i, 0, :, cut] = term_re.astype(sums[g].dtype)
                    sums[g][i, 1, :, cut] = term_im.astype(sums[g].dtype)
            mate_out[0, :, cut] = total_re.astype(mate_out.dtype)
            mate_out[1, :, cut] = total_im.astype(mate_out.dtype)


def pair_terms(at, flips, occupied, spot, mate, bands, tables, sums=(), mate_sum=(), types=None):
    groups = len(bands)
    mate_type, sums_type = types or (jnp.bfloat16, jnp.float32)
    smem = pl.BlockSpec(memory_space=pltpu.SMEM)
    vmem = pl.BlockSpec(memory_space=pltpu.VMEM)
    operands = [mate, *bands, *sums, *mate_sum, *tables]
    return pl.pallas_call(
        functools.partial(pair_kernel, at, flips, len(sums) > 0, len(mate_sum) > 0),
        out_shape=[jax.ShapeDtypeStruct(mate.shape, mate_type)]
        + [jax.ShapeDtypeStruct(band.shape, sums_type) for band in bands],
        in_specs=[smem] * 2 + [vmem] * len(operands),
        out_specs=[vmem] * (1 + groups),
        scratch_shapes=[
            pltpu.VMEM((2, groups, 256, 256), jnp.bfloat16),
            pltpu.VMEM((8, groups * 2 * GRID, 256), jnp.bfloat16),
            pltpu.VMEM((2, groups, 256, 256), jnp.bfloat16),
        ],
        compiler_params=pltpu.CompilerParams(vmem_limit_bytes=VMEM_BYTES),
        cost_estimate=pl.CostEstimate(
            flops=groups * 10**9, bytes_accessed=groups * 10**6, transcendentals=0
        ),
    )(occupied, spot, *operands)


def passed_along(value, by):
    count = lax.axis_size("ka")
    return lax.ppermute(value, "ka", [(i, (i + by) % count) for i in range(count)])


def swapped(value, flip):
    return lax.ppermute(value, "ba", [(i, i ^ flip) for i in range(lax.axis_size("ba"))])


def on_device(orbitals, kpoints, occupied):
    own = orbitals[0, 0]
    spot = jnp.stack([lax.axis_index("ka"), lax.axis_index("ba")])
    forward_x = first_tables()
    forward_yz = second_tables()
    tables = staged(
        kpoints.T,
        spot,
        (forward_x, forward_x.transpose(0, 2, 1), forward_yz, forward_yz.transpose(0, 2, 1)),
    )
    near = jnp.stack([own, swapped(own, 2)])
    mates = [passed_along(own, step) for step in SHIFTS]
    far = swapped(near, 1)
    near_flips, far_flips = (0, 2), (1, 3)
    both = (near_flips, far_flips)

    term, *sums = pair_terms(0, both, occupied, spot, mates[0], (near, far), tables)
    back = [passed_along(term, -SHIFTS[0])]
    term, *sums = pair_terms(1, both, occupied, spot, mates[1], (near, far), tables, sums=sums)
    back.append(passed_along(term, -SHIFTS[1]))
    part, far_sum = pair_terms(
        2, (far_flips,), occupied, spot, mates[2], (far,), tables,
        sums=sums[1:], types=(jnp.float32, jnp.bfloat16),
    )
    from_core = swapped(far_sum, 1)
    term, near_sum = pair_terms(
        2, (near_flips,), occupied, spot, mates[2], (near,), tables, sums=sums[:1], mate_sum=(part,)
    )
    across = swapped((near_sum[1] + from_core[1].astype(jnp.float32)).astype(jnp.bfloat16), 2)
    back.append(passed_along(term, -SHIFTS[2]))
    total = near_sum[0] + from_core[0].astype(jnp.float32) + across.astype(jnp.float32)
    for returned in back:
        total = total + returned.astype(jnp.float32)
    return total[None, None]


def solution(mesh):
    in_specs = (P("ka", "ba", None, None, None), P(), P())
    out_specs = P("ka", "ba", None, None, None)
    return jax.shard_map(
        on_device, mesh=mesh, in_specs=in_specs, out_specs=out_specs, check_vma=False
    )
```

time: 55.4 us -> 46.6 us (0.84)
  the two profiles are of different devices: /device:TPU:6 before, /device:TPU:96 now
where the time goes in v1:
time: 46.6 us; the launch traced here: 46.4 us
  starting transfers between devices  18.6 us (40%)
  waiting for transfers between devices  13.4 us (29%)
  Pallas kernels  8.68 us (19%)
  local copies, waits for them, and re-layouts  3.71 us (8%)
  other arithmetic  1.89 us (4%)
    ppermute x6, starting transfers between devices, passed_along(): lax.ppermute(value, 'ka', [(i, (i + by) % count) for i in range(count)])  12.3 us
    ppermute x4, waiting for transfers between devices, swapped(): lax.ppermute(value, 'ba', [(i, i ^ flip) for i in range(lax.axis_size('ba...  11.4 us
    pallas_call x4, Pallas kernels, pair_terms(): pl.pallas_call(functools.partial(pair_kernel, at, flips, len(sums) > 0, l...  7.8 us
    ppermute x4, starting transfers between devices, swapped(): lax.ppermute(value, 'ba', [(i, i ^ flip) for i in range(lax.axis_size('ba...  6.32 us
    unnamed x12, local copies, waits for them, and re-layouts  3.71 us
    ppermute x6, waiting for transfers between devices, passed_along(): lax.ppermute(value, 'ka', [(i, (i + by) % count) for i in range(count)])  2.01 us
    another operation x1, other arithmetic, on_device(): near = jnp.stack([own, swapped(own, 2)])  0.99 us
  transfers between devices with their start and end apart: 10, of which 4 were waited for; matrix products, arithmetic and copies ran while one was open for 0% of the time, Pallas kernels for 15%

profile of v1, /device:TPU:96, one launch (start us, length us, event | category | flops | bytes accessed | tf_op | source)
XLA Modules:
  0.0 46.4 jit_solution(5513042560663434361)
XLA Ops:
  0.0 3.0 %collective-permute-start.1 = (bf16[2,32,1024]{2,1,0:T(8,128)(2,1)}, bf16[2,32,1024]{2,1,0:T(8,128)(2,1)S(1)}, u32[]{:S(2)}, u32[]{:S(2)}) collective-permute-start(bf16[2,32,1024]{2,1,0:T(8,128)(2,1)} %bitcast.21), channel_id=1, source_target_pairs={{0,2},{1,3},{2,0},{3,1},{4,6},{5,7},{6,4},{7,5},{8,10},{9,11},{10,... | collective-permute-start | bytes 393224 | tf_op jit(solution)/shard_map/ppermute | solution.py:239
  3.0 3.9 %collective-permute-done.1 = bf16[2,32,1024]{2,1,0:T(8,128)(2,1)S(1)} collective-permute-done((bf16[2,32,1024]{2,1,0:T(8,128)(2,1)}, bf16[2,32,1024]{2,1,0:T(8,128)(2,1)S(1)}, u32[]{:S(2)}, u32[]{:S(2)}) %collective-permute-start.1) | collective-permute-done | bytes 131104 | tf_op jit(solution)/shard_map/ppermute | solution.py:239
  7.0 0.0 copy-start.2
  7.0 0.0 copy-start.3
  7.0 1.0 %pad_maximum_fusion.refs_0_ = bf16[2,2,32,1024]{3,2,1,0:T(8,128)(2,1)S(1)} fusion(bf16[1,2,32,1024]{3,2,1,0:T(8,128)(2,1)S(1)} %bitcast.26, bf16[1,2,32,1024]{3,2,1,0:T(8,128)(2,1)} %bitcast.22), kind=kLoop, calls=%fused_computation | loop fusion | flops 131072 | bytes 524288 | tf_op jit(solution)/shard_map/stack | solution.py:252
  7.9 0.1 collective-permute-start.3
  8.0 1.7 %collective-permute-start.4 = (bf16[2,32,1024]{2,1,0:T(8,128)(2,1)}, bf16[2,32,1024]{2,1,0:T(8,128)(2,1)S(1)}, u32[]{:S(2)}, u32[]{:S(2)}) collective-permute-start(bf16[2,32,1024]{2,1,0:T(8,128)(2,1)} %bitcast.23), channel_id=1, source_target_pairs={{0,4},{4,8},{8,12},{12,16},{16,20},{20,24},{24,28},{28,32},{32,36}... | collective-permute-start | bytes 393224 | tf_op jit(solution)/shard_map/ppermute | solution.py:235
  9.7 2.6 %collective-permute-start.2 = (bf16[2,32,1024]{2,1,0:T(8,128)(2,1)}, bf16[2,32,1024]{2,1,0:T(8,128)(2,1)S(1)}, u32[]{:S(2)}, u32[]{:S(2)}) collective-permute-start(bf16[2,32,1024]{2,1,0:T(8,128)(2,1)} %bitcast.24), channel_id=1, source_target_pairs={{0,12},{4,16},{8,20},{12,24},{16,28},{20,32},{24,36},{28,40},{32,4... | collective-permute-start | bytes 393224 | tf_op jit(solution)/shard_map/ppermute | solution.py:235
  12.3 2.9 %collective-permute-start = (bf16[2,32,1024]{2,1,0:T(8,128)(2,1)}, bf16[2,32,1024]{2,1,0:T(8,128)(2,1)S(1)}, u32[]{:S(2)}, u32[]{:S(2)}) collective-permute-start(bf16[2,32,1024]{2,1,0:T(8,128)(2,1)} %bitcast.25), channel_id=1, source_target_pairs={{0,248},{4,252},{8,0},{12,4},{16,8},{20,12},{24,16},{28,20},{32,24... | collective-permute-start | bytes 393224 | tf_op jit(solution)/shard_map/ppermute | solution.py:235
  15.1 0.0 copy-start.4
  15.1 0.1 pad_add_fusion.spot
  15.2 0.0 copy-done.2
  15.2 0.0 copy-done.3
  15.2 0.6 %copy-done.4 = s32[64,3]{0,1:T(4,128)S(1)} copy-done((s32[64,3]{0,1:T(4,128)S(1)}, s32[64,3]{0,1:T(4,128)}, u32[]{:S(2)}) %copy-start.4) | copy-done | bytes 792
  15.8 0.0 copy-start
  15.8 1.2 %copy-done = bf16[8,256,256]{2,1,0:T(8,128)(2,1)S(1)} copy-done((bf16[8,256,256]{2,1,0:T(8,128)(2,1)S(1)}, bf16[8,256,256]{2,1,0:T(8,128)(2,1)}, u32[]{:S(2)}) %copy-start) | copy-done | bytes 1048600
  17.1 0.0 copy-start.1
  17.1 1.2 %copy-done.1 = bf16[8,256,256]{2,1,0:T(8,128)(2,1)S(1)} copy-done((bf16[8,256,256]{2,1,0:T(8,128)(2,1)S(1)}, bf16[8,256,256]{2,1,0:T(8,128)(2,1)}, u32[]{:S(2)}) %copy-start.1) | copy-done | bytes 1048600
  18.3 0.9 %shard_map.73 = (bf16[2,256,256]{2,1,0:T(8,128)(2,1)S(1)}, bf16[2,256,256]{2,1,0:T(8,128)(2,1)S(1)}, bf16[8,256,256]{2,1,0:T(8,128)(2,1)S(1)}, bf16[8,256,256]{2,1,0:T(8,128)(2,1)S(1)}, f32[3,8,32,128]{3,2,1,0:T(8,128)S(1)}) custom-call(s32[3,64]{1,0:T(4,128)S(1)} %bitcast.20, s32[2]{0:T(128)S(1)} %pad_add_fusion.spot, bf16[2,256,256]{2,1,0:T(8,128)(2,1)S(1)} %copy-done.2, ...), custom_call_target="tpu_custom_call" | custom-call | flops 1000000 | bytes 6000000 | tf_op jit(solution)/shard_map/pallas_call | solution.py:96
  19.2 0.0 collective-permute-done.4.mate
  19.2 0.0 collective-permute-done.3.refs_1_.refs_0_
  19.2 0.0 copy-start.5
  19.2 0.6 %copy-done.5 = s32[64]{0:T(128)S(1)} copy-done((s32[64]{0:T(128)S(1)}, s32[64]{0:T(128)}, u32[]{:S(2)}) %copy-start.5) | copy-done | bytes 280
  19.8 2.1 %shard_map.74 = (bf16[2,32,1024]{2,1,0:T(8,128)(2,1)S(1)}, f32[2,2,32,1024]{3,2,1,0:T(8,128)S(1)}, f32[2,2,32,1024]{3,2,1,0:T(8,128)S(1)}) custom-call(s32[64]{0:T(128)S(1)} %copy-done.5, s32[2]{0:T(128)S(1)} %pad_add_fusion.spot, bf16[2,32,1024]{2,1,0:T(8,128)(2,1)S(1)} %collective-permute-done.4.mate, ...), custom_call_target="tpu_custom_call" | custom-call | flops 2000000000 | bytes 2000000 | tf_op jit(solution)/shard_map/pallas_call | solution.py:215
  21.9 0.0 collective-permute-done.2.mate
  21.9 2.1 %shard_map.75 = (bf16[2,32,1024]{2,1,0:T(8,128)(2,1)S(1)}, f32[2,2,32,1024]{3,2,1,0:T(8,128)S(1)}, f32[2,2,32,1024]{3,2,1,0:T(8,128)S(1)}) custom-call(s32[64]{0:T(128)S(1)} %copy-done.5, s32[2]{0:T(128)S(1)} %pad_add_fusion.spot, bf16[2,32,1024]{2,1,0:T(8,128)(2,1)S(1)} %collective-permute-done.2.mate, ...), custom_call_target="tpu_custom_call" | custom-call | flops 2000000000 | bytes 2000000 | tf_op jit(solution)/shard_map/pallas_call | solution.py:215
  24.1 0.0 collective-permute-done.mate
  24.1 1.8 %shard_map.76 = (f32[2,32,1024]{2,1,0:T(8,128)S(1)}, bf16[2,2,32,1024]{3,2,1,0:T(8,128)(2,1)S(1)}) custom-call(s32[64]{0:T(128)S(1)} %copy-done.5, s32[2]{0:T(128)S(1)} %pad_add_fusion.spot, bf16[2,32,1024]{2,1,0:T(8,128)(2,1)S(1)} %collective-permute-done.mate, bf16[2,2,32,1024]{3,2,1,0:T(8,128)(2,1)S(1)} %collective-permute-done.3.refs_1_.refs_0_, ...), custom_call_target="tpu_custom_call" | custom-call | flops 1000000000 | bytes 1000000 | tf_op jit(solution)/shard_map/pallas_call | solution.py:215
  25.9 0.1 collective-permute-start.5
  26.0 1.8 %shard_map.77 = (bf16[2,32,1024]{2,1,0:T(8,128)(2,1)S(1)}, f32[2,2,32,1024]{3,2,1,0:T(8,128)S(1)}) custom-call(s32[64]{0:T(128)S(1)} %copy-done.5, s32[2]{0:T(128)S(1)} %pad_add_fusion.spot, bf16[2,32,1024]{2,1,0:T(8,128)(2,1)S(1)} %collective-permute-done.mate, bf16[2,2,32,1024]{3,2,1,0:T(8,128)(2,1)S(1)} %pad_maximum_fusion.refs_0_, ...), custom_call_target="tpu_custom_call" | custom-call | flops 1000000000 | bytes 1000000 | tf_op jit(solution)/shard_map/pallas_call | solution.py:215
  27.8 0.7 %collective-permute-start.9 = (bf16[2,32,1024]{2,1,0:T(8,128)(2,1)S(1)}, bf16[2,32,1024]{2,1,0:T(8,128)(2,1)S(1)}, u32[]{:S(2)}, u32[]{:S(2)}) collective-permute-start(bf16[2,32,1024]{2,1,0:T(8,128)(2,1)S(1)} %get-tuple-element.34), channel_id=1, source_target_pairs={{0,8},{4,12},{8,16},{12,20},{16,24},{20,28},{24,32},{28,36},{32,40... | collective-permute-start | bytes 393224 | tf_op jit(solution)/shard_map/ppermute | solution.py:235
  28.5 1.2 %collective-permute-start.8 = (bf16[2,32,1024]{2,1,0:T(8,128)(2,1)S(1)}, bf16[2,32,1024]{2,1,0:T(8,128)(2,1)S(1)}, u32[]{:S(2)}, u32[]{:S(2)}) collective-permute-start(bf16[2,32,1024]{2,1,0:T(8,128)(2,1)S(1)} %get-tuple-element.33), channel_id=1, source_target_pairs={{0,244},{4,248},{8,252},{12,0},{16,4},{20,8},{24,12},{28,16},{32,2... | collective-permute-start | bytes 393224 | tf_op jit(solution)/shard_map/ppermute | solution.py:235
  29.8 3.2 %collective-permute-start.7 = (bf16[2,32,1024]{2,1,0:T(8,128)(2,1)S(1)}, bf16[2,32,1024]{2,1,0:T(8,128)(2,1)S(1)}, u32[]{:S(2)}, u32[]{:S(2)}) collective-permute-start(bf16[2,32,1024]{2,1,0:T(8,128)(2,1)S(1)} %get-tuple-element.32), channel_id=1, source_target_pairs={{0,252},{4,0},{8,4},{12,8},{16,12},{20,16},{24,20},{28,24},{32,28}... | collective-permute-start | bytes 393224 | tf_op jit(solution)/shard_map/ppermute | solution.py:235
  33.0 0.0 collective-permute-done.5
  33.0 3.1 %collective-permute-start.6 = (bf16[2,32,1024]{2,1,0:T(8,128)(2,1)S(1)}, bf16[2,32,1024]{2,1,0:T(8,128)(2,1)S(1)}, u32[]{:S(2)}, u32[]{:S(2)}) collective-permute-start(bf16[2,32,1024]{2,1,0:T(8,128)(2,1)S(1)} %fusion.4), channel_id=1, source_target_pairs={{0,2},{1,3},{2,0},{3,1},{4,6},{5,7},{6,4},{7,5},{8,10},{9,11},{10,... | collective-permute-start | bytes 393224 | tf_op jit(solution)/shard_map/ppermute | solution.py:239
  36.2 1.0 %collective-permute-done.9 = bf16[2,32,1024]{2,1,0:T(8,128)(2,1)S(1)} collective-permute-done((bf16[2,32,1024]{2,1,0:T(8,128)(2,1)S(1)}, bf16[2,32,1024]{2,1,0:T(8,128)(2,1)S(1)}, u32[]{:S(2)}, u32[]{:S(2)}) %collective-permute-start.9) | collective-permute-done | bytes 131104 | tf_op jit(solution)/shard_map/ppermute | solution.py:235
  37.2 1.0 %collective-permute-done.8 = bf16[2,32,1024]{2,1,0:T(8,128)(2,1)S(1)} collective-permute-done((bf16[2,32,1024]{2,1,0:T(8,128)(2,1)S(1)}, bf16[2,32,1024]{2,1,0:T(8,128)(2,1)S(1)}, u32[]{:S(2)}, u32[]{:S(2)}) %collective-permute-start.8) | collective-permute-done | bytes 131104 | tf_op jit(solution)/shard_map/ppermute | solution.py:235
  38.2 0.0 collective-permute-done.7
  38.2 7.4 %collective-permute-done.6 = bf16[2,32,1024]{2,1,0:T(8,128)(2,1)S(1)} collective-permute-done((bf16[2,32,1024]{2,1,0:T(8,128)(2,1)S(1)}, bf16[2,32,1024]{2,1,0:T(8,128)(2,1)S(1)}, u32[]{:S(2)}, u32[]{:S(2)}) %collective-permute-start.6) | collective-permute-done | bytes 131104 | tf_op jit(solution)/shard_map/ppermute | solution.py:239
  45.6 0.8 %fusion.3 = f32[1,1,2,32,1024]{4,3,2,1,0:T(8,128)} fusion(bf16[2,32,1024]{2,1,0:T(8,128)(2,1)S(1)} %collective-permute-done.9, bf16[2,32,1024]{2,1,0:T(8,128)(2,1)S(1)} %collective-permute-done.8, bf16[2,32,1024]{2,1,0:T(8,128)(2,1)S(1)} %collective-permute-done.7, bf16[2,32,1024]{2,1,0:T(8,128)(2,1)S(1)} %collective-permute-done.6, ...), kind=kLoop, calls=%fused_computation.5 | loop fusion | flops 655360 | bytes 1179648 | tf_op jit(solution)/shard_map/broadcast_in_dim | solution.py:275
  (1 shorter events, 0.0 us)
Async XLA Ops:
  0.0 7.0 %collective-permute-start.1 = (bf16[2,32,1024]{2,1,0:T(8,128)(2,1)}, bf16[2,32,1024]{2,1,0:T(8,128)(2,1)S(1)}, u32[]{:S(2)}, u32[]{:S(2)}) collective-permute-start(bf16[2,32,1024]{2,1,0:T(8,128)(2,1)} %bitcast.21), channel_id=1, source_target_pairs={{0,2},{1,3},{2,0},{3,1},{4,6},{5,7},{6,4},{7,5},{8,10},{9,11},{10,... | collective-permute-start | bytes 393224 | tf_op jit(solution)/shard_map/ppermute | solution.py:239
  7.0 8.3 %copy-start.2 = (bf16[2,256,256]{2,1,0:T(8,128)(2,1)S(1)}, bf16[2,256,256]{2,1,0:T(8,128)(2,1)}, u32[]{:S(2)}) copy-start(bf16[2,256,256]{2,1,0:T(8,128)(2,1)} %constant.17.clone.refs_0_) | copy-start | bytes 786436
  7.0 8.3 %copy-start.3 = (bf16[2,256,256]{2,1,0:T(8,128)(2,1)S(1)}, bf16[2,256,256]{2,1,0:T(8,128)(2,1)}, u32[]{:S(2)}) copy-start(bf16[2,256,256]{2,1,0:T(8,128)(2,1)} %constant.18.clone.refs_1_) | copy-start | bytes 786436
  7.9 11.2 %collective-permute-start.3 = (bf16[2,2,32,1024]{3,2,1,0:T(8,128)(2,1)S(1)}, bf16[2,2,32,1024]{3,2,1,0:T(8,128)(2,1)S(1)}, u32[]{:S(2)}, u32[]{:S(2)}) collective-permute-start(bf16[2,2,32,1024]{3,2,1,0:T(8,128)(2,1)S(1)} %pad_maximum_fusion.refs_0_), channel_id=1, source_target_pairs={{0,1},{1,0},{2,3},{3,2},{4,5},{5,4},{6,7},{7,6},{8,9},{9,8},{10,11... | collective-permute-start | bytes 786440 | tf_op jit(solution)/shard_map/ppermute | solution.py:239
  8.0 11.1 %collective-permute-start.4 = (bf16[2,32,1024]{2,1,0:T(8,128)(2,1)}, bf16[2,32,1024]{2,1,0:T(8,128)(2,1)S(1)}, u32[]{:S(2)}, u32[]{:S(2)}) collective-permute-start(bf16[2,32,1024]{2,1,0:T(8,128)(2,1)} %bitcast.23), channel_id=1, source_target_pairs={{0,4},{4,8},{8,12},{12,16},{16,20},{20,24},{24,28},{28,32},{32,36}... | collective-permute-start | bytes 393224 | tf_op jit(solution)/shard_map/ppermute | solution.py:235
  9.7 12.2 %collective-permute-start.2 = (bf16[2,32,1024]{2,1,0:T(8,128)(2,1)}, bf16[2,32,1024]{2,1,0:T(8,128)(2,1)S(1)}, u32[]{:S(2)}, u32[]{:S(2)}) collective-permute-start(bf16[2,32,1024]{2,1,0:T(8,128)(2,1)} %bitcast.24), channel_id=1, source_target_pairs={{0,12},{4,16},{8,20},{12,24},{16,28},{20,32},{24,36},{28,40},{32,4... | collective-permute-start | bytes 393224 | tf_op jit(solution)/shard_map/ppermute | solution.py:235
  12.3 11.8 %collective-permute-start = (bf16[2,32,1024]{2,1,0:T(8,128)(2,1)}, bf16[2,32,1024]{2,1,0:T(8,128)(2,1)S(1)}, u32[]{:S(2)}, u32[]{:S(2)}) collective-permute-start(bf16[2,32,1024]{2,1,0:T(8,128)(2,1)} %bitcast.25), channel_id=1, source_target_pairs={{0,248},{4,252},{8,0},{12,4},{16,8},{20,12},{24,16},{28,20},{32,24... | collective-permute-start | bytes 393224 | tf_op jit(solution)/shard_map/ppermute | solution.py:235
  15.1 0.7 %copy-start.4 = (s32[64,3]{0,1:T(4,128)S(1)}, s32[64,3]{0,1:T(4,128)}, u32[]{:S(2)}) copy-start(s32[64,3]{0,1:T(4,128)} %param.8) | copy-start | bytes 2308
  15.8 1.2 %copy-start = (bf16[8,256,256]{2,1,0:T(8,128)(2,1)S(1)}, bf16[8,256,256]{2,1,0:T(8,128)(2,1)}, u32[]{:S(2)}) copy-start(bf16[8,256,256]{2,1,0:T(8,128)(2,1)} %constant.19.clone.refs_2_) | copy-start | bytes 3145732
  17.1 1.2 %copy-start.1 = (bf16[8,256,256]{2,1,0:T(8,128)(2,1)S(1)}, bf16[8,256,256]{2,1,0:T(8,128)(2,1)}, u32[]{:S(2)}) copy-start(bf16[8,256,256]{2,1,0:T(8,128)(2,1)} %constant.20.clone.refs_3_) | copy-start | bytes 3145732
  19.2 0.7 %copy-start.5 = (s32[64]{0:T(128)S(1)}, s32[64]{0:T(128)}, u32[]{:S(2)}) copy-start(s32[64]{0:T(128)} %occupied.7) | copy-start | bytes 772
  25.9 7.1 %collective-permute-start.5 = (bf16[2,2,32,1024]{3,2,1,0:T(8,128)(2,1)S(1)}, bf16[2,2,32,1024]{3,2,1,0:T(8,128)(2,1)S(1)}, u32[]{:S(2)}, u32[]{:S(2)}) collective-permute-start(bf16[2,2,32,1024]{3,2,1,0:T(8,128)(2,1)S(1)} %get-tuple-element.31), channel_id=1, source_target_pairs={{0,1},{1,0},{2,3},{3,2},{4,5},{5,4},{6,7},{7,6},{8,9},{9,8},{10,11... | collective-permute-start | bytes 786440 | tf_op jit(solution)/shard_map/ppermute | solution.py:239
  27.8 9.4 %collective-permute-start.9 = (bf16[2,32,1024]{2,1,0:T(8,128)(2,1)S(1)}, bf16[2,32,1024]{2,1,0:T(8,128)(2,1)S(1)}, u32[]{:S(2)}, u32[]{:S(2)}) collective-permute-start(bf16[2,32,1024]{2,1,0:T(8,128)(2,1)S(1)} %get-tuple-element.34), channel_id=1, source_target_pairs={{0,8},{4,12},{8,16},{12,20},{16,24},{20,28},{24,32},{28,36},{32,40... | collective-permute-start | bytes 393224 | tf_op jit(solution)/shard_map/ppermute | solution.py:235
  28.5 9.6 %collective-permute-start.8 = (bf16[2,32,1024]{2,1,0:T(8,128)(2,1)S(1)}, bf16[2,32,1024]{2,1,0:T(8,128)(2,1)S(1)}, u32[]{:S(2)}, u32[]{:S(2)}) collective-permute-start(bf16[2,32,1024]{2,1,0:T(8,128)(2,1)S(1)} %get-tuple-element.33), channel_id=1, source_target_pairs={{0,244},{4,248},{8,252},{12,0},{16,4},{20,8},{24,12},{28,16},{32,2... | collective-permute-start | bytes 393224 | tf_op jit(solution)/shard_map/ppermute | solution.py:235
  29.8 8.4 %collective-permute-start.7 = (bf16[2,32,1024]{2,1,0:T(8,128)(2,1)S(1)}, bf16[2,32,1024]{2,1,0:T(8,128)(2,1)S(1)}, u32[]{:S(2)}, u32[]{:S(2)}) collective-permute-start(bf16[2,32,1024]{2,1,0:T(8,128)(2,1)S(1)} %get-tuple-element.32), channel_id=1, source_target_pairs={{0,252},{4,0},{8,4},{12,8},{16,12},{20,16},{24,20},{28,24},{32,28}... | collective-permute-start | bytes 393224 | tf_op jit(solution)/shard_map/ppermute | solution.py:235
  33.0 12.5 %collective-permute-start.6 = (bf16[2,32,1024]{2,1,0:T(8,128)(2,1)S(1)}, bf16[2,32,1024]{2,1,0:T(8,128)(2,1)S(1)}, u32[]{:S(2)}, u32[]{:S(2)}) collective-permute-start(bf16[2,32,1024]{2,1,0:T(8,128)(2,1)S(1)} %fusion.4), channel_id=1, source_target_pairs={{0,2},{1,3},{2,0},{3,1},{4,6},{5,7},{6,4},{7,5},{8,10},{9,11},{10,... | collective-permute-start | bytes 393224 | tf_op jit(solution)/shard_map/ppermute | solution.py:239

commit v2 on v1

v2 whole, which is shorter than its diff:
```python
import functools
import math

import jax
import jax.numpy as jnp
from jax import lax
from jax.experimental import pallas as pl
from jax.experimental.pallas import tpu as pltpu
from jax.sharding import PartitionSpec as P

KMESH = 8
SHIFTS = (1, 3, -2)
GRID = 32
LANES = 128
CELL = 20.52
SCREENING = 0.05
VMEM_BYTES = 32 * 1024 * 1024


def block(index):
    return slice(index * LANES, (index + 1) * LANES)


def rows(index):
    return slice(index * GRID, (index + 1) * GRID)


def dot(left, right, dims=((1,), (0,))):
    return lax.dot_general(left, right, (dims, ((), ())), preferred_element_type=jnp.float32)


def stage_kernel(kpoints, occupied, spot, forward_x, inverse_x, forward_yz, inverse_yz, screened, weights):
    turn = 2 * math.pi / GRID
    square = (LANES, LANES)
    row = lax.broadcasted_iota(jnp.int32, square, 0)
    column = lax.broadcasted_iota(jnp.int32, square, 1)
    row_high, column_high = lax.shift_right_logical(row, 5), lax.shift_right_logical(column, 5)

    def wave(turns):
        turns = (jnp.bitwise_and(turns + GRID // 2, GRID - 1) - GRID // 2).astype(jnp.float32) * turn
        return jnp.cos(turns), jnp.sin(turns)

    def put(table, at, upper, lower):
        table[at, :LANES] = jnp.concatenate(upper, axis=1).astype(table.dtype)
        table[at, LANES:] = jnp.concatenate(lower, axis=1).astype(table.dtype)

    low = jnp.bitwise_and(row, GRID - 1) * jnp.bitwise_and(column, GRID - 1)
    cosine, sine = wave(8 * row_high * column_high + low)
    row_cosine, row_sine = wave(row_high)
    column_cosine, column_sine = wave(column_high)
    down = across = (cosine, sine)
    for k1 in range(8):
        put(forward_yz, k1, (down[0], -down[1]), (down[1], down[0]))
        put(inverse_yz, k1, (across[0], across[1]), (-across[1], across[0]))
        if k1 % 4 == 0:
            put(forward_x, k1 // 4, (down[0], down[1]), (-down[1], down[0]))
            put(inverse_x, k1 // 4, (across[0], -across[1]), (across[1], across[0]))
        down = (
            down[0] * row_cosine - down[1] * row_sine,
            down[0] * row_sine + down[1] * row_cosine,
        )
        across = (
            across[0] * column_cosine - across[1] * column_sine,
            across[0] * column_sine + across[1] * column_cosine,
        )

    count = kpoints.shape[1]
    own = spot[0]
    slot = spot[1]
    unit = 2 * math.pi / CELL
    shape = (GRID, LANES)
    lane = lax.broadcasted_iota(jnp.int32, shape, 1)
    high = lax.shift_right_logical(lane, 5) * 8

    def centred(index):
        return (jnp.bitwise_and(index + GRID // 2, GRID - 1) - GRID // 2).astype(jnp.float32)

    def occupancy(point, band):
        return jnp.full((1, LANES), jnp.where(band < occupied[point], -1.0, 0.0), jnp.float32)

    grid_x = centred(lax.broadcasted_iota(jnp.int32, shape, 0))
    grid_z = centred(jnp.bitwise_and(lane, GRID - 1))
    for at, step in enumerate(SHIFTS):
        other = lax.rem(own - step + count, count)
        later, earlier = (own, other) if step > 0 else (other, own)
        along = []
        for i in range(3):
            apart = lax.rem(kpoints[i, later] - kpoints[i, earlier] + KMESH // 2 + KMESH, KMESH)
            along.append((apart - KMESH // 2).astype(jnp.float32) / KMESH)
        at_x = (grid_x + along[0]) * unit
        at_z = (grid_z + along[2]) * unit
        flat = at_x * at_x + at_z * at_z + SCREENING
        for k1 in range(8):
            at_y = (centred(high + k1) + along[1]) * unit
            screened[at, k1] = (math.pi / GRID**3) / (flat + at_y * at_y)
        weights[4 + at] = occupancy(other, slot)
    for flip in range(4):
        weights[flip] = occupancy(own, slot ^ flip)


def staged(kpoints, occupied, spot):
    smem = pl.BlockSpec(memory_space=pltpu.SMEM)
    vmem = pl.BlockSpec(memory_space=pltpu.VMEM)
    return pl.pallas_call(
        stage_kernel,
        out_shape=[
            jax.ShapeDtypeStruct((2, 256, 256), jnp.bfloat16),
            jax.ShapeDtypeStruct((2, 256, 256), jnp.bfloat16),
            jax.ShapeDtypeStruct((8, 256, 256), jnp.bfloat16),
            jax.ShapeDtypeStruct((8, 256, 256), jnp.bfloat16),
            jax.ShapeDtypeStruct((len(SHIFTS), 8, GRID, LANES), jnp.float32),
            jax.ShapeDtypeStruct((4 + len(SHIFTS), 1, LANES), jnp.float32),
        ],
        in_specs=[smem] * 3,
        out_specs=[vmem] * 6,
        compiler_params=pltpu.CompilerParams(vmem_limit_bytes=VMEM_BYTES),
        cost_estimate=pl.CostEstimate(flops=10**6, bytes_accessed=6 * 10**6, transcendentals=0),
    )(kpoints, occupied, spot)


def pair_kernel(ats, flips, has_sums, has_mates, *refs):
    groups = len(flips)
    refs = list(refs)

    def take(n):
        taken = refs[:n]
        del refs[:n]
        return taken

    mates = take(len(ats))
    bands = [take(2) for _ in range(groups)]
    sums_in = take(groups) if has_sums else None
    mates_in = take(len(ats)) if has_mates else None
    forward_x, inverse_x, forward_yz, inverse_yz, screened, weights = take(6)
    mates_out = take(len(ats))
    sums = take(groups)
    wide, mid, back = refs
    jobs = [(m, g) for m in range(len(ats)) for g in range(groups)]

    for b in range(2):
        for a in range(4):
            cut = block(2 * a + b)
            for job, (m, g) in enumerate(jobs):
                mate_re = mates[m][0, :, cut].astype(jnp.float32)
                mate_im = mates[m][1, :, cut].astype(jnp.float32)
                for i in range(2):
                    band_re = bands[g][i][0, :, cut].astype(jnp.float32)
                    band_im = bands[g][i][1, :, cut].astype(jnp.float32)
                    value_re = mate_re * band_re + mate_im * band_im
                    if SHIFTS[ats[m]] < 0:
                        value_im = mate_im * band_re - mate_re * band_im
                    else:
                        value_im = mate_re * band_im - mate_im * band_re
                    wide[b, job, rows(a), block(i)] = value_re.astype(jnp.bfloat16)
                    wide[b, job, rows(4 + a), block(i)] = value_im.astype(jnp.bfloat16)

    for job in range(len(jobs)):
        even = dot(forward_x[0], wide[0, job])
        odd = dot(forward_x[1], wide[1, job])
        plus = (even + odd).astype(jnp.bfloat16)
        minus = (even - odd).astype(jnp.bfloat16)
        for i in range(2):
            for e in range(4):
                for c in range(2):
                    mid[e, rows(2 * job + i), block(c)] = plus[rows(4 * c + e), block(i)]
                    mid[e + 4, rows(2 * job + i), block(c)] = minus[rows(4 * c + e), block(i)]

    for e in range(4):
        halves = []
        for k1 in (e, e + 4):
            third = dot(mid[k1], forward_yz[k1])
            factor = []
            for at in ats:
                factor += [jnp.concatenate([screened[at, k1]] * 2, axis=1)] * (2 * groups)
            factor = jnp.concatenate(factor, axis=0)
            halves.append(dot((third * factor).astype(jnp.bfloat16), inverse_yz[k1]))
        for b in range(2):
            joined = (halves[0] - halves[1] if b else halves[0] + halves[1]).astype(jnp.bfloat16)
            for job in range(len(jobs)):
                for i in range(2):
                    for c in range(2):
                        back[b, job, rows(4 * c + e), block(i)] = joined[rows(2 * job + i), block(c)]

    for b in range(2):
        waves = [dot(inverse_x[b], back[b, job]) for job in range(len(jobs))]
        for a in range(4):
            cut = block(2 * a + b)
            mate_total = [[m[0, :, cut], m[1, :, cut]] if has_mates else [0.0, 0.0] for m in mates_in or ats]
            band_total = [[[s[i, 0, :, cut], s[i, 1, :, cut]] if has_sums else [0.0, 0.0] for i in range(2)] for s in sums_in or flips]
            for job, (m, g) in enumerate(jobs):
                mate_weight = weights[4 + ats[m]]
                mate_re = mates[m][0, :, cut].astype(jnp.float32) * mate_weight
                mate_im = mates[m][1, :, cut].astype(jnp.float32) * mate_weight
                for i in range(2):
                    weight = weights[flips[g][i]]
                    wave_re = waves[job][rows(a), block(i)]
                    wave_im = waves[job][rows(4 + a), block(i)]
                    band_re = bands[g][i][0, :, cut].astype(jnp.float32) * weight
                    band_im = bands[g][i][1, :, cut].astype(jnp.float32) * weight
                    to_mate, to_band = mate_total[m], band_total[g][i]
                    if SHIFTS[ats[m]] < 0:
                        to_band[0] += mate_re * wave_re + mate_im * wave_im
                        to_band[1] += mate_im * wave_re - mate_re * wave_im
                        to_mate[0] += band_re * wave_re - band_im * wave_im
                        to_mate[1] += band_re * wave_im + band_im * wave_re
                    else:
                        to_band[0] += mate_re * wave_re - mate_im * wave_im
                        to_band[1] += mate_re * wave_im + mate_im * wave_re
                        to_mate[0] += band_re * wave_re + band_im * wave_im
                        to_mate[1] += band_im * wave_re - band_re * wave_im
            for c in range(2):
                for m in range(len(ats)):
                    mates_out[m][c, :, cut] = mate_total[m][c].astype(mates_out[m].dtype)
                for g in range(groups):
                    for i in range(2):
                        sums[g][i, c, :, cut] = band_total[g][i][c].astype(sums[g].dtype)


def pair_terms(ats, flips, mates, bands, tables, sums=(), mate_sums=(), types=(jnp.bfloat16, jnp.float32)):
    groups = len(bands)
    jobs = len(ats) * groups
    vmem = pl.BlockSpec(memory_space=pltpu.VMEM)
    field = mates[0].shape
    operands = [*mates, *[band for group in bands for band in group], *sums, *mate_sums, *tables]
    out_shape = [jax.ShapeDtypeStruct(field, types[0])] * len(ats)
    out_shape += [jax.ShapeDtypeStruct((2,) + field, types[1])] * groups
    return pl.pallas_call(
        functools.partial(pair_kernel, ats, flips, len(sums) > 0, len(mate_sums) > 0),
        out_shape=out_shape,
        in_specs=[vmem] * len(operands),
        out_specs=[vmem] * len(out_shape),
        scratch_shapes=[
            pltpu.VMEM((2, jobs, 256, 256), jnp.bfloat16),
            pltpu.VMEM((8, jobs * 2 * GRID, 256), jnp.bfloat16),
            pltpu.VMEM((2, jobs, 256, 256), jnp.bfloat16),
        ],
        compiler_params=pltpu.CompilerParams(vmem_limit_bytes=VMEM_BYTES),
        cost_estimate=pl.CostEstimate(flops=jobs * 10**9, bytes_accessed=jobs * 10**6, transcendentals=0),
    )(*operands)


def passed_along(value, by):
    count = lax.axis_size("ka")
    return lax.ppermute(value, "ka", [(i, (i + by) % count) for i in range(count)])


def swapped(value, flip):
    return lax.ppermute(value, "ba", [(i, i ^ flip) for i in range(lax.axis_size("ba"))])


def on_device(orbitals, kpoints, occupied):
    own = orbitals[0, 0]
    spot = jnp.stack([lax.axis_index("ka"), lax.axis_index("ba")])
    tables = staged(kpoints.T, occupied, spot)
    near = (own, swapped(own, 2))
    far = (swapped(own, 1), swapped(near[1], 1))
    mates = [passed_along(own, step) for step in SHIFTS]
    near_flips, far_flips = (0, 2), (1, 3)
    *terms, near_sum, far_sum = pair_terms((0, 1, 2), (near_flips, far_flips), mates, (near, far), tables)
    from_core = swapped(far_sum.astype(jnp.bfloat16), 1)
    across = swapped((near_sum[1] + from_core[1].astype(jnp.float32)).astype(jnp.bfloat16), 2)
    back = [passed_along(term, -step) for term, step in zip(terms, SHIFTS)]
    total = near_sum[0] + from_core[0].astype(jnp.float32) + across.astype(jnp.float32)
    for returned in back:
        total = total + returned.astype(jnp.float32)
    return total[None, None]


def solution(mesh):
    in_specs = (P("ka", "ba", None, None, None), P(), P())
    out_specs = P("ka", "ba", None, None, None)
    return jax.shard_map(
        on_device, mesh=mesh, in_specs=in_specs, out_specs=out_specs, check_vma=False
    )
```

time: 46.6 us -> 39.5 us (0.85)
  the two profiles are of different devices: /device:TPU:96 before, /device:TPU:1 now
where the time goes in v2:
time: 39.5 us; the launch traced here: 39.4 us
  starting transfers between devices  21.3 us (54%)
  waiting for transfers between devices  10.4 us (26%)
  Pallas kernels  5.19 us (13%)
  local copies, waits for them, and re-layouts  1.56 us (4%)
  other arithmetic  0.93 us (2%)
    ppermute x6, starting transfers between devices, passed_along(): lax.ppermute(value, 'ka', [(i, (i + by) % count) for i in range(count)])  13.2 us
    ppermute x6, waiting for transfers between devices, passed_along(): lax.ppermute(value, 'ka', [(i, (i + by) % count) for i in range(count)])  10.4 us
    ppermute x5, starting transfers between devices, swapped(): lax.ppermute(value, 'ba', [(i, i ^ flip) for i in range(lax.axis_size('ba...  8.1 us
    pallas_call x1, Pallas kernels, pair_terms(): pl.pallas_call(functools.partial(pair_kernel, ats, flips, len(sums) > 0,...  3.69 us
    unnamed x6, local copies, waits for them, and re-layouts  1.56 us
    pallas_call x1, Pallas kernels, staged(): pl.pallas_call(stage_kernel, out_shape=[jax.ShapeDtypeStruct((2, 256, 256...  1.5 us
    broadcast_in_dim x1, other arithmetic, on_device(): return total[None, None]  0.8 us
  transfers between devices with their start and end apart: 11, of which 4 were waited for; matrix products, arithmetic and copies ran while one was open for 0% of the time, Pallas kernels for 4%

profile of v2, /device:TPU:1, one launch (start us, length us, event | category | flops | bytes accessed | tf_op | source)
XLA Modules:
  0.0 39.4 jit_solution(15118853938131756929)
XLA Ops:
  0.0 3.6 %collective-permute-start.3 = (bf16[2,32,1024]{2,1,0:T(8,128)(2,1)}, bf16[2,32,1024]{2,1,0:T(8,128)(2,1)S(1)}, u32[]{:S(2)}, u32[]{:S(2)}) collective-permute-start(bf16[2,32,1024]{2,1,0:T(8,128)(2,1)} %bitcast.18), channel_id=1, source_target_pairs={{0,2},{1,3},{2,0},{3,1},{4,6},{5,7},{6,4},{7,5},{8,10},{9,11},{10,... | collective-permute-start | bytes 393224 | tf_op jit(solution)/shard_map/ppermute | solution.py:248
  3.6 1.0 %collective-permute-start.4 = (bf16[2,32,1024]{2,1,0:T(8,128)(2,1)}, bf16[2,32,1024]{2,1,0:T(8,128)(2,1)S(1)}, u32[]{:S(2)}, u32[]{:S(2)}) collective-permute-start(bf16[2,32,1024]{2,1,0:T(8,128)(2,1)} %bitcast.19), channel_id=1, source_target_pairs={{0,1},{1,0},{2,3},{3,2},{4,5},{5,4},{6,7},{7,6},{8,9},{9,8},{10,11... | collective-permute-start | bytes 393224 | tf_op jit(solution)/shard_map/ppermute | solution.py:248
  4.5 8.2 %collective-permute-start.2 = (bf16[2,32,1024]{2,1,0:T(8,128)(2,1)}, bf16[2,32,1024]{2,1,0:T(8,128)(2,1)S(1)}, u32[]{:S(2)}, u32[]{:S(2)}) collective-permute-start(bf16[2,32,1024]{2,1,0:T(8,128)(2,1)} %bitcast.20), channel_id=1, source_target_pairs={{0,248},{4,252},{8,0},{12,4},{16,8},{20,12},{24,16},{28,20},{32,24... | collective-permute-start | bytes 393224 | tf_op jit(solution)/shard_map/ppermute | solution.py:244
  12.8 0.0 collective-permute-start.1
  12.8 0.4 %collective-permute-start = (bf16[2,32,1024]{2,1,0:T(8,128)(2,1)}, bf16[2,32,1024]{2,1,0:T(8,128)(2,1)S(1)}, u32[]{:S(2)}, u32[]{:S(2)}) collective-permute-start(bf16[2,32,1024]{2,1,0:T(8,128)(2,1)} %bitcast.22), channel_id=1, source_target_pairs={{0,4},{4,8},{8,12},{12,16},{16,20},{20,24},{24,28},{28,32},{32,36}... | collective-permute-start | bytes 393224 | tf_op jit(solution)/shard_map/ppermute | solution.py:244
  13.2 0.0 collective-permute-done.3.refs_4_
  13.2 0.6 %collective-permute-start.5 = (bf16[2,32,1024]{2,1,0:T(8,128)(2,1)S(1)}, bf16[2,32,1024]{2,1,0:T(8,128)(2,1)S(1)}, u32[]{:S(2)}, u32[]{:S(2)}) collective-permute-start(bf16[2,32,1024]{2,1,0:T(8,128)(2,1)S(1)} %collective-permute-done.3.refs_4_), channel_id=1, source_target_pairs={{0,1},{1,0},{2,3},{3,2},{4,5},{5,4},{6,7},{7,6},{8,9},{9,8},{10,11... | collective-permute-start | bytes 393224 | tf_op jit(solution)/shard_map/ppermute | solution.py:248
  13.7 0.0 copy-start.1
  13.7 0.1 pad_add_fusion.spot
  13.8 0.0 copy-start.2
  13.8 0.6 %copy-done.1 = s32[64,3]{0,1:T(4,128)S(1)} copy-done((s32[64,3]{0,1:T(4,128)S(1)}, s32[64,3]{0,1:T(4,128)}, u32[]{:S(2)}) %copy-start.1) | copy-done | bytes 792
  14.4 0.1 copy-done.2
  14.5 1.5 %shard_map.37 = (bf16[2,256,256]{2,1,0:T(8,128)(2,1)S(1)}, bf16[2,256,256]{2,1,0:T(8,128)(2,1)S(1)}, bf16[8,256,256]{2,1,0:T(8,128)(2,1)S(1)}, bf16[8,256,256]{2...) custom-call(s32[3,64]{1,0:T(4,128)S(1)} %bitcast.24, s32[64]{0:T(128)S(1)} %copy-done.2, ...), custom_call_target="tpu_custom_call" | custom-call | flops 1000000 | bytes 6000000 | tf_op jit(solution)/shard_map/pallas_call | solution.py:104
  16.0 0.0 collective-permute-done.4.refs_5_
  16.0 0.0 collective-permute-done.2.refs_2_
  16.0 4.8 %collective-permute-done.1.refs_1_ = bf16[2,32,1024]{2,1,0:T(8,128)(2,1)S(1)} collective-permute-done((bf16[2,32,1024]{2,1,0:T(8,128)(2,1)}, bf16[2,32,1024]{2,1,0:T(8,128)(2,1)S(1)}, u32[]{:S(2)}, u32[]{:S(2)}) %collective-permute-start.1) | collective-permute-done | bytes 131104 | tf_op jit(solution)/shard_map/ppermute | solution.py:244
  20.8 1.2 %collective-permute-done.refs_0_ = bf16[2,32,1024]{2,1,0:T(8,128)(2,1)S(1)} collective-permute-done((bf16[2,32,1024]{2,1,0:T(8,128)(2,1)}, bf16[2,32,1024]{2,1,0:T(8,128)(2,1)S(1)}, u32[]{:S(2)}, u32[]{:S(2)}) %collective-permute-start) | collective-permute-done | bytes 131104 | tf_op jit(solution)/shard_map/ppermute | solution.py:244
  22.0 0.0 collective-permute-done.5.refs_6_
  22.0 0.0 copy-start
  22.0 0.9 %copy-done = bf16[1,1,2,32,1024]{4,3,2,1,0:T(8,128)(2,1)S(1)} copy-done((bf16[1,1,2,32,1024]{4,3,2,1,0:T(8,128)(2,1)S(1)}, bf16[1,1,2,32,1024]{4,3,2,1,0:T(8,128)(2,1)}, u32[]{:S(2)}) %copy-start) | copy-done | bytes 131096
  22.9 3.7 %shard_map.38 = (bf16[2,32,1024]{2,1,0:T(8,128)(2,1)S(1)}, bf16[2,32,1024]{2,1,0:T(8,128)(2,1)S(1)}, bf16[2,32,1024]{2,1,0:T(8,128)(2,1)S(1)}, f32[2,2,32,1024]{3,2,1,0:T(8,128)S(1)}, f32[2,2,32,1024]{3,2,1,0:T(8,128)S(1)}) custom-call(bf16[2,32,1024]{2,1,0:T(8,128)(2,1)S(1)} %collective-permute-done.refs_0_, ...), custom_call_target="tpu_custom_call" | custom-call | flops 6000000000 | bytes 6000000 | tf_op jit(solution)/shard_map/pallas_call | solution.py:227
  26.7 1.2 %collective-permute-start.6 = (bf16[2,2,32,1024]{3,2,1,0:T(8,128)(2,1)S(1)}, bf16[2,2,32,1024]{3,2,1,0:T(8,128)(2,1)S(1)}, u32[]{:S(2)}, u32[]{:S(2)}) collective-permute-start(bf16[2,2,32,1024]{3,2,1,0:T(8,128)(2,1)S(1)} %convert_element_type.29), channel_id=1, source_target_pairs={{0,1},{1,0},{2,3},{3,2},{4,5},{5,4},{6,7},{7,6},{8,9},{9,8},{10,11... | collective-permute-start | bytes 786440 | tf_op jit(solution)/shard_map/ppermute | solution.py:248
  27.8 0.7 %collective-permute-start.8 = (bf16[2,32,1024]{2,1,0:T(8,128)(2,1)S(1)}, bf16[2,32,1024]{2,1,0:T(8,128)(2,1)S(1)}, u32[]{:S(2)}, u32[]{:S(2)}) collective-permute-start(bf16[2,32,1024]{2,1,0:T(8,128)(2,1)S(1)} %get-tuple-element.24), channel_id=1, source_target_pairs={{0,252},{4,0},{8,4},{12,8},{16,12},{20,16},{24,20},{28,24},{32,28}... | collective-permute-start | bytes 393224 | tf_op jit(solution)/shard_map/ppermute | solution.py:244
  28.6 1.1 %collective-permute-start.9 = (bf16[2,32,1024]{2,1,0:T(8,128)(2,1)S(1)}, bf16[2,32,1024]{2,1,0:T(8,128)(2,1)S(1)}, u32[]{:S(2)}, u32[]{:S(2)}) collective-permute-start(bf16[2,32,1024]{2,1,0:T(8,128)(2,1)S(1)} %get-tuple-element.25), channel_id=1, source_target_pairs={{0,244},{4,248},{8,252},{12,0},{16,4},{20,8},{24,12},{28,16},{32,2... | collective-permute-start | bytes 393224 | tf_op jit(solution)/shard_map/ppermute | solution.py:244
  29.7 2.7 %collective-permute-start.10 = (bf16[2,32,1024]{2,1,0:T(8,128)(2,1)S(1)}, bf16[2,32,1024]{2,1,0:T(8,128)(2,1)S(1)}, u32[]{:S(2)}, u32[]{:S(2)}) collective-permute-start(bf16[2,32,1024]{2,1,0:T(8,128)(2,1)S(1)} %get-tuple-element.26), channel_id=1, source_target_pairs={{0,8},{4,12},{8,16},{12,20},{16,24},{20,28},{24,32},{28,36},{32,40... | collective-permute-start | bytes 393224 | tf_op jit(solution)/shard_map/ppermute | solution.py:244
  32.4 0.0 collective-permute-done.6
  32.5 1.8 %collective-permute-start.7 = (bf16[2,32,1024]{2,1,0:T(8,128)(2,1)S(1)}, bf16[2,32,1024]{2,1,0:T(8,128)(2,1)S(1)}, u32[]{:S(2)}, u32[]{:S(2)}) collective-permute-start(bf16[2,32,1024]{2,1,0:T(8,128)(2,1)S(1)} %fusion.4), channel_id=1, source_target_pairs={{0,2},{1,3},{2,0},{3,1},{4,6},{5,7},{6,4},{7,5},{8,10},{9,11},{10,... | collective-permute-start | bytes 393224 | tf_op jit(solution)/shard_map/ppermute | solution.py:248
  34.3 0.0 collective-permute-done.8
  34.3 0.3 collective-permute-done.9
  34.5 4.1 %collective-permute-done.10 = bf16[2,32,1024]{2,1,0:T(8,128)(2,1)S(1)} collective-permute-done((bf16[2,32,1024]{2,1,0:T(8,128)(2,1)S(1)}, bf16[2,32,1024]{2,1,0:T(8,128)(2,1)S(1)}, u32[]{:S(2)}, u32[]{:S(2)}) %collective-permute-start.10) | collective-permute-done | bytes 131104 | tf_op jit(solution)/shard_map/ppermute | solution.py:244
  38.6 0.0 collective-permute-done.7
  38.6 0.8 %fusion.3 = f32[1,1,2,32,1024]{4,3,2,1,0:T(8,128)} fusion(bf16[2,32,1024]{2,1,0:T(8,128)(2,1)S(1)} %collective-permute-done.10, bf16[2,32,1024]{2,1,0:T(8,128)(2,1)S(1)} %collective-permute-done.9, bf16[2,32,1024]{2,1,0:T(8,128)(2,1)S(1)} %collective-permute-done.8, bf16[2,32,1024]{2,1,0:T(8,128)(2,1)S(1)} %collective-permute-done.7, ...), kind=kLoop, calls=%fused_computation.4 | loop fusion | flops 655360 | bytes 1179648 | tf_op jit(solution)/shard_map/broadcast_in_dim | solution.py:266
  (2 shorter events, 0.1 us)
Async XLA Ops:
  0.0 13.2 %collective-permute-start.3 = (bf16[2,32,1024]{2,1,0:T(8,128)(2,1)}, bf16[2,32,1024]{2,1,0:T(8,128)(2,1)S(1)}, u32[]{:S(2)}, u32[]{:S(2)}) collective-permute-start(bf16[2,32,1024]{2,1,0:T(8,128)(2,1)} %bitcast.18), channel_id=1, source_target_pairs={{0,2},{1,3},{2,0},{3,1},{4,6},{5,7},{6,4},{7,5},{8,10},{9,11},{10,... | collective-permute-start | bytes 393224 | tf_op jit(solution)/shard_map/ppermute | solution.py:248
  3.6 12.4 %collective-permute-start.4 = (bf16[2,32,1024]{2,1,0:T(8,128)(2,1)}, bf16[2,32,1024]{2,1,0:T(8,128)(2,1)S(1)}, u32[]{:S(2)}, u32[]{:S(2)}) collective-permute-start(bf16[2,32,1024]{2,1,0:T(8,128)(2,1)} %bitcast.19), channel_id=1, source_target_pairs={{0,1},{1,0},{2,3},{3,2},{4,5},{5,4},{6,7},{7,6},{8,9},{9,8},{10,11... | collective-permute-start | bytes 393224 | tf_op jit(solution)/shard_map/ppermute | solution.py:248
  4.5 11.5 %collective-permute-start.2 = (bf16[2,32,1024]{2,1,0:T(8,128)(2,1)}, bf16[2,32,1024]{2,1,0:T(8,128)(2,1)S(1)}, u32[]{:S(2)}, u32[]{:S(2)}) collective-permute-start(bf16[2,32,1024]{2,1,0:T(8,128)(2,1)} %bitcast.20), channel_id=1, source_target_pairs={{0,248},{4,252},{8,0},{12,4},{16,8},{20,12},{24,16},{28,20},{32,24... | collective-permute-start | bytes 393224 | tf_op jit(solution)/shard_map/ppermute | solution.py:244
  12.8 8.0 %collective-permute-start.1 = (bf16[2,32,1024]{2,1,0:T(8,128)(2,1)}, bf16[2,32,1024]{2,1,0:T(8,128)(2,1)S(1)}, u32[]{:S(2)}, u32[]{:S(2)}) collective-permute-start(bf16[2,32,1024]{2,1,0:T(8,128)(2,1)} %bitcast.21), channel_id=1, source_target_pairs={{0,12},{4,16},{8,20},{12,24},{16,28},{20,32},{24,36},{28,40},{32,4... | collective-permute-start | bytes 393224 | tf_op jit(solution)/shard_map/ppermute | solution.py:244
  12.8 9.2 %collective-permute-start = (bf16[2,32,1024]{2,1,0:T(8,128)(2,1)}, bf16[2,32,1024]{2,1,0:T(8,128)(2,1)S(1)}, u32[]{:S(2)}, u32[]{:S(2)}) collective-permute-start(bf16[2,32,1024]{2,1,0:T(8,128)(2,1)} %bitcast.22), channel_id=1, source_target_pairs={{0,4},{4,8},{8,12},{12,16},{16,20},{20,24},{24,28},{28,32},{32,36}... | collective-permute-start | bytes 393224 | tf_op jit(solution)/shard_map/ppermute | solution.py:244
  13.2 8.8 %collective-permute-start.5 = (bf16[2,32,1024]{2,1,0:T(8,128)(2,1)S(1)}, bf16[2,32,1024]{2,1,0:T(8,128)(2,1)S(1)}, u32[]{:S(2)}, u32[]{:S(2)}) collective-permute-start(bf16[2,32,1024]{2,1,0:T(8,128)(2,1)S(1)} %collective-permute-done.3.refs_4_), channel_id=1, source_target_pairs={{0,1},{1,0},{2,3},{3,2},{4,5},{5,4},{6,7},{7,6},{8,9},{9,8},{10,11... | collective-permute-start | bytes 393224 | tf_op jit(solution)/shard_map/ppermute | solution.py:248
  13.7 0.7 %copy-start.1 = (s32[64,3]{0,1:T(4,128)S(1)}, s32[64,3]{0,1:T(4,128)}, u32[]{:S(2)}) copy-start(s32[64,3]{0,1:T(4,128)} %param.4) | copy-start | bytes 2308
  13.8 0.7 %copy-start.2 = (s32[64]{0:T(128)S(1)}, s32[64]{0:T(128)}, u32[]{:S(2)}) copy-start(s32[64]{0:T(128)} %occupied.1) | copy-start | bytes 772
  22.0 0.9 %copy-start = (bf16[1,1,2,32,1024]{4,3,2,1,0:T(8,128)(2,1)S(1)}, bf16[1,1,2,32,1024]{4,3,2,1,0:T(8,128)(2,1)}, u32[]{:S(2)}) copy-start(bf16[1,1,2,32,1024]{4,3,2,1,0:T(8,128)(2,1)} %param.3) | copy-start | bytes 393220
  26.7 5.8 %collective-permute-start.6 = (bf16[2,2,32,1024]{3,2,1,0:T(8,128)(2,1)S(1)}, bf16[2,2,32,1024]{3,2,1,0:T(8,128)(2,1)S(1)}, u32[]{:S(2)}, u32[]{:S(2)}) collective-permute-start(bf16[2,2,32,1024]{3,2,1,0:T(8,128)(2,1)S(1)} %convert_element_type.29), channel_id=1, source_target_pairs={{0,1},{1,0},{2,3},{3,2},{4,5},{5,4},{6,7},{7,6},{8,9},{9,8},{10,11... | collective-permute-start | bytes 786440 | tf_op jit(solution)/shard_map/ppermute | solution.py:248
  27.8 6.4 %collective-permute-start.8 = (bf16[2,32,1024]{2,1,0:T(8,128)(2,1)S(1)}, bf16[2,32,1024]{2,1,0:T(8,128)(2,1)S(1)}, u32[]{:S(2)}, u32[]{:S(2)}) collective-permute-start(bf16[2,32,1024]{2,1,0:T(8,128)(2,1)S(1)} %get-tuple-element.24), channel_id=1, source_target_pairs={{0,252},{4,0},{8,4},{12,8},{16,12},{20,16},{24,20},{28,24},{32,28}... | collective-permute-start | bytes 393224 | tf_op jit(solution)/shard_map/ppermute | solution.py:244
  28.6 6.0 %collective-permute-start.9 = (bf16[2,32,1024]{2,1,0:T(8,128)(2,1)S(1)}, bf16[2,32,1024]{2,1,0:T(8,128)(2,1)S(1)}, u32[]{:S(2)}, u32[]{:S(2)}) collective-permute-start(bf16[2,32,1024]{2,1,0:T(8,128)(2,1)S(1)} %get-tuple-element.25), channel_id=1, source_target_pairs={{0,244},{4,248},{8,252},{12,0},{16,4},{20,8},{24,12},{28,16},{32,2... | collective-permute-start | bytes 393224 | tf_op jit(solution)/shard_map/ppermute | solution.py:244
  29.7 8.9 %collective-permute-start.10 = (bf16[2,32,1024]{2,1,0:T(8,128)(2,1)S(1)}, bf16[2,32,1024]{2,1,0:T(8,128)(2,1)S(1)}, u32[]{:S(2)}, u32[]{:S(2)}) collective-permute-start(bf16[2,32,1024]{2,1,0:T(8,128)(2,1)S(1)} %get-tuple-element.26), channel_id=1, source_target_pairs={{0,8},{4,12},{8,16},{12,20},{16,24},{20,28},{24,32},{28,36},{32,40... | collective-permute-start | bytes 393224 | tf_op jit(solution)/shard_map/ppermute | solution.py:244
  32.5 6.2 %collective-permute-start.7 = (bf16[2,32,1024]{2,1,0:T(8,128)(2,1)S(1)}, bf16[2,32,1024]{2,1,0:T(8,128)(2,1)S(1)}, u32[]{:S(2)}, u32[]{:S(2)}) collective-permute-start(bf16[2,32,1024]{2,1,0:T(8,128)(2,1)S(1)} %fusion.4), channel_id=1, source_target_pairs={{0,2},{1,3},{2,0},{3,1},{4,6},{5,7},{6,4},{7,5},{8,10},{9,11},{10,... | collective-permute-start | bytes 393224 | tf_op jit(solution)/shard_map/ppermute | solution.py:248

commit v3 on v2

--- a/solution.py
+++ b/solution.py
@@ -9,7 +9,7 @@
 from jax.sharding import PartitionSpec as P
 
 KMESH = 8
-SHIFTS = (1, 3, -2)
+SHIFTS = (-2, 1, 3)
 GRID = 32
 LANES = 128
 CELL = 20.52
@@ -29,16 +29,25 @@
     return lax.dot_general(left, right, (dims, ((), ())), preferred_element_type=jnp.float32)
 
 
-def stage_kernel(kpoints, occupied, spot, forward_x, inverse_x, forward_yz, inverse_yz, screened, weights):
+def stage_kernel(kpoints, occupied, spot, band, held, forward_x, inverse_x, forward_yz, inverse_yz, screened, weights):
+    held[...] = band[...]
     turn = 2 * math.pi / GRID
     square = (LANES, LANES)
     row = lax.broadcasted_iota(jnp.int32, square, 0)
     column = lax.broadcasted_iota(jnp.int32, square, 1)
     row_high, column_high = lax.shift_right_logical(row, 5), lax.shift_right_logical(column, 5)
 
+    def cosine_of(turns):
+        turns = jnp.abs(jnp.bitwise_and(turns + GRID // 2, GRID - 1) - GRID // 2)
+        folded = jnp.minimum(turns, GRID // 2 - turns).astype(jnp.float32)
+        square = folded * folded * (turn * turn)
+        series = 1.0
+        for order in (10, 8, 6, 4, 2):
+            series = 1.0 - square * series * (1.0 / (order * (order - 1)))
+        return jnp.where(turns > GRID // 4, -series, series)
+
     def wave(turns):
-        turns = (jnp.bitwise_and(turns + GRID // 2, GRID - 1) - GRID // 2).astype(jnp.float32) * turn
-        return jnp.cos(turns), jnp.sin(turns)
+        return cosine_of(turns), cosine_of(turns - GRID // 4)
 
     def put(table, at, upper, lower):
         table[at, :LANES] = jnp.concatenate(upper, axis=1).astype(table.dtype)
@@ -98,12 +107,13 @@
         weights[flip] = occupancy(own, slot ^ flip)
 
 
-def staged(kpoints, occupied, spot):
+def staged(kpoints, occupied, spot, band):
     smem = pl.BlockSpec(memory_space=pltpu.SMEM)
     vmem = pl.BlockSpec(memory_space=pltpu.VMEM)
     return pl.pallas_call(
         stage_kernel,
         out_shape=[
+            jax.ShapeDtypeStruct(band.shape, band.dtype),
             jax.ShapeDtypeStruct((2, 256, 256), jnp.bfloat16),
             jax.ShapeDtypeStruct((2, 256, 256), jnp.bfloat16),
             jax.ShapeDtypeStruct((8, 256, 256), jnp.bfloat16),
@@ -111,14 +121,14 @@
             jax.ShapeDtypeStruct((len(SHIFTS), 8, GRID, LANES), jnp.float32),
             jax.ShapeDtypeStruct((4 + len(SHIFTS), 1, LANES), jnp.float32),
         ],
-        in_specs=[smem] * 3,
-        out_specs=[vmem] * 6,
+        in_specs=[smem] * 3 + [vmem],
+        out_specs=[vmem] * 7,
         compiler_params=pltpu.CompilerParams(vmem_limit_bytes=VMEM_BYTES),
         cost_estimate=pl.CostEstimate(flops=10**6, bytes_accessed=6 * 10**6, transcendentals=0),
-    )(kpoints, occupied, spot)
-
-
-def pair_kernel(ats, flips, has_sums, has_mates, *refs):
+    )(kpoints, occupied, spot, band)
+
+
+def pair_kernel(ats, flips, has_sums, *refs):
     groups = len(flips)
     refs = list(refs)
 
@@ -127,10 +137,9 @@
         del refs[:n]
         return taken
 
+    bands = [take(2) for _ in range(groups)]
     mates = take(len(ats))
-    bands = [take(2) for _ in range(groups)]
     sums_in = take(groups) if has_sums else None
-    mates_in = take(len(ats)) if has_mates else None
     forward_x, inverse_x, forward_yz, inverse_yz, screened, weights = take(6)
     mates_out = take(len(ats))
     sums = take(groups)
@@ -185,8 +194,11 @@
         waves = [dot(inverse_x[b], back[b, job]) for job in range(len(jobs))]
         for a in range(4):
             cut = block(2 * a + b)
-            mate_total = [[m[0, :, cut], m[1, :, cut]] if has_mates else [0.0, 0.0] for m in mates_in or ats]
-            band_total = [[[s[i, 0, :, cut], s[i, 1, :, cut]] if has_sums else [0.0, 0.0] for i in range(2)] for s in sums_in or flips]
+            mate_total = [[0.0, 0.0] for _ in ats]
+            if has_sums:
+                band_total = [[[s[i, c, :, cut] for c in range(2)] for i in range(2)] for s in sums_in]
+            else:
+                band_total = [[[0.0, 0.0] for _ in range(2)] for _ in flips]
             for job, (m, g) in enumerate(jobs):
                 mate_weight = weights[4 + ats[m]]
                 mate_re = mates[m][0, :, cut].astype(jnp.float32) * mate_weight
@@ -216,16 +228,16 @@
                         sums[g][i, c, :, cut] = band_total[g][i][c].astype(sums[g].dtype)
 
 
-def pair_terms(ats, flips, mates, bands, tables, sums=(), mate_sums=(), types=(jnp.bfloat16, jnp.float32)):
+def pair_terms(ats, flips, mates, bands, tables, sums=(), types=(jnp.float32, jnp.float32)):
     groups = len(bands)
     jobs = len(ats) * groups
     vmem = pl.BlockSpec(memory_space=pltpu.VMEM)
     field = mates[0].shape
-    operands = [*mates, *[band for group in bands for band in group], *sums, *mate_sums, *tables]
-    out_shape = [jax.ShapeDtypeStruct(field, types[0])] * len(ats)
-    out_shape += [jax.ShapeDtypeStruct((2,) + field, types[1])] * groups
+    operands = [*[band for group in bands for band in group], *mates, *sums, *tables]
+    out_shape = [jax.ShapeDtypeStruct(field, jnp.bfloat16)] * len(ats)
+    out_shape += [jax.ShapeDtypeStruct((2,) + field, kind) for kind in types]
     return pl.pallas_call(
-        functools.partial(pair_kernel, ats, flips, len(sums) > 0, len(mate_sums) > 0),
+        functools.partial(pair_kernel, ats, flips, len(sums) > 0),
         out_shape=out_shape,
         in_specs=[vmem] * len(operands),
         out_specs=[vmem] * len(out_shape),
@@ -251,16 +263,18 @@
 def on_device(orbitals, kpoints, occupied):
     own = orbitals[0, 0]
     spot = jnp.stack([lax.axis_index("ka"), lax.axis_index("ba")])
-    tables = staged(kpoints.T, occupied, spot)
-    near = (own, swapped(own, 2))
-    far = (swapped(own, 1), swapped(near[1], 1))
+    held, *tables = staged(kpoints.T, occupied, spot, own)
+    across = swapped(own, 2)
+    near = (held, across)
+    far = (swapped(own, 1), swapped(across, 1))
     mates = [passed_along(own, step) for step in SHIFTS]
-    near_flips, far_flips = (0, 2), (1, 3)
-    *terms, near_sum, far_sum = pair_terms((0, 1, 2), (near_flips, far_flips), mates, (near, far), tables)
-    from_core = swapped(far_sum.astype(jnp.bfloat16), 1)
-    across = swapped((near_sum[1] + from_core[1].astype(jnp.float32)).astype(jnp.bfloat16), 2)
-    back = [passed_along(term, -step) for term, step in zip(terms, SHIFTS)]
-    total = near_sum[0] + from_core[0].astype(jnp.float32) + across.astype(jnp.float32)
+    flips = ((0, 2), (1, 3))
+    last = (jnp.float32, jnp.bfloat16)
+    *terms, near_sum, far_sum = pair_terms((0, 1, 2), flips, mates, (near, far), tables, types=last)
+    from_core = swapped(far_sum, 1)
+    along = swapped((near_sum[1] + from_core[1].astype(jnp.float32)).astype(jnp.bfloat16), 2)
+    back = [passed_along(terms[at], -SHIFTS[at]) for at in (0, 1, 2)]
+    total = near_sum[0] + from_core[0].astype(jnp.float32) + along.astype(jnp.float32)
     for returned in back:
         total = total + returned.astype(jnp.float32)
     return total[None, None]

time: 39.5 us -> 38.2 us (0.967)
  the two profiles are of different devices: /device:TPU:1 before, /device:TPU:225 now
where the time goes in v3:
time: 38.2 us; the launch traced here: 38.1 us
  starting transfers between devices  19.1 us (50%)
  waiting for transfers between devices  11.5 us (30%)
  Pallas kernels  4.96 us (13%)
  local copies, waits for them, and re-layouts  1.56 us (4%)
  other arithmetic  0.92 us (2%)
    ppermute x6, starting transfers between devices, passed_along(): lax.ppermute(value, 'ka', [(i, (i + by) % count) for i in range(count)])  10.4 us
    ppermute x5, starting transfers between devices, swapped(): lax.ppermute(value, 'ba', [(i, i ^ flip) for i in range(lax.axis_size('ba...  8.69 us
    ppermute x6, waiting for transfers between devices, passed_along(): lax.ppermute(value, 'ka', [(i, (i + by) % count) for i in range(count)])  6.4 us
    ppermute x5, waiting for transfers between devices, swapped(): lax.ppermute(value, 'ba', [(i, i ^ flip) for i in range(lax.axis_size('ba...  5.08 us
    pallas_call x1, Pallas kernels, pair_terms(): pl.pallas_call(functools.partial(pair_kernel, ats, flips, len(sums) > 0),...  3.7 us
    unnamed x6, local copies, waits for them, and re-layouts  1.56 us
    pallas_call x1, Pallas kernels, staged(): pl.pallas_call(stage_kernel, out_shape=[jax.ShapeDtypeStruct(band.shape,...  1.26 us
    broadcast_in_dim x1, other arithmetic, on_device(): return total[None, None]  0.81 us
  transfers between devices with their start and end apart: 11, of which 4 were waited for; matrix products, arithmetic and copies ran while one was open for 0% of the time, Pallas kernels for 3%

profile of v3, /device:TPU:225, one launch (start us, length us, event | category | flops | bytes accessed | tf_op | source)
XLA Modules:
  0.0 38.1 jit_solution(16888450781416185609)
XLA Ops:
  0.0 2.7 %collective-permute-start = (bf16[2,32,1024]{2,1,0:T(8,128)(2,1)}, bf16[2,32,1024]{2,1,0:T(8,128)(2,1)S(1)}, u32[]{:S(2)}, u32[]{:S(2)}) collective-permute-start(bf16[2,32,1024]{2,1,0:T(8,128)(2,1)} %bitcast.18), channel_id=1, source_target_pairs={{0,2},{1,3},{2,0},{3,1},{4,6},{5,7},{6,4},{7,5},{8,10},{9,11},{10,... | collective-permute-start | bytes 393224 | tf_op jit(solution)/shard_map/ppermute | solution.py:260
  2.7 2.7 %collective-permute-start.5 = (bf16[2,32,1024]{2,1,0:T(8,128)(2,1)}, bf16[2,32,1024]{2,1,0:T(8,128)(2,1)S(1)}, u32[]{:S(2)}, u32[]{:S(2)}) collective-permute-start(bf16[2,32,1024]{2,1,0:T(8,128)(2,1)} %bitcast.19), channel_id=1, source_target_pairs={{0,12},{4,16},{8,20},{12,24},{16,28},{20,32},{24,36},{28,40},{32,4... | collective-permute-start | bytes 393224 | tf_op jit(solution)/shard_map/ppermute | solution.py:256
  5.5 0.0 collective-permute-start.4
  5.5 3.4 %collective-permute-start.3 = (bf16[2,32,1024]{2,1,0:T(8,128)(2,1)}, bf16[2,32,1024]{2,1,0:T(8,128)(2,1)S(1)}, u32[]{:S(2)}, u32[]{:S(2)}) collective-permute-start(bf16[2,32,1024]{2,1,0:T(8,128)(2,1)} %bitcast.21), channel_id=1, source_target_pairs={{0,248},{4,252},{8,0},{12,4},{16,8},{20,12},{24,16},{28,20},{32,24... | collective-permute-start | bytes 393224 | tf_op jit(solution)/shard_map/ppermute | solution.py:256
  8.9 1.8 %collective-permute-start.1 = (bf16[2,32,1024]{2,1,0:T(8,128)(2,1)}, bf16[2,32,1024]{2,1,0:T(8,128)(2,1)S(1)}, u32[]{:S(2)}, u32[]{:S(2)}) collective-permute-start(bf16[2,32,1024]{2,1,0:T(8,128)(2,1)} %bitcast.22), channel_id=1, source_target_pairs={{0,1},{1,0},{2,3},{3,2},{4,5},{5,4},{6,7},{7,6},{8,9},{9,8},{10,11... | collective-permute-start | bytes 393224 | tf_op jit(solution)/shard_map/ppermute | solution.py:260
  10.7 0.0 collective-permute-done.refs_1_
  10.7 0.0 collective-permute-start.2
  10.7 0.0 copy-start.1
  10.7 0.1 pad_add_fusion.spot
  10.8 0.0 copy-start.2
  10.8 0.6 %copy-done.1 = s32[64,3]{0,1:T(4,128)S(1)} copy-done((s32[64,3]{0,1:T(4,128)S(1)}, s32[64,3]{0,1:T(4,128)}, u32[]{:S(2)}) %copy-start.1) | copy-done | bytes 792
  11.4 0.1 copy-done.2
  11.5 0.0 copy-start
  11.5 0.9 %copy-done = bf16[1,1,2,32,1024]{4,3,2,1,0:T(8,128)(2,1)S(1)} copy-done((bf16[1,1,2,32,1024]{4,3,2,1,0:T(8,128)(2,1)S(1)}, bf16[1,1,2,32,1024]{4,3,2,1,0:T(8,128)(2,1)}, u32[]{:S(2)}) %copy-start) | copy-done | bytes 131096
  12.4 1.3 %shard_map.37 = (bf16[2,32,1024]{2,1,0:T(8,128)(2,1)S(1)}, bf16[2,256,256]{2,1,0:T(8,128)(2,1)S(1)}, bf16[2,256,256]{2,1,0:T(8,128)(2,1)S(1)}, bf16[8,256,256]{2...) custom-call(s32[3,64]{1,0:T(4,128)S(1)} %bitcast.24, ...), custom_call_target="tpu_custom_call" | custom-call | flops 1000000 | bytes 6000000 | tf_op jit(solution)/shard_map/pallas_call | solution.py:113
  13.6 0.0 collective-permute-done.5.refs_6_
  13.6 0.9 %collective-permute-done.4.refs_5_ = bf16[2,32,1024]{2,1,0:T(8,128)(2,1)S(1)} collective-permute-done((bf16[2,32,1024]{2,1,0:T(8,128)(2,1)}, bf16[2,32,1024]{2,1,0:T(8,128)(2,1)S(1)}, u32[]{:S(2)}, u32[]{:S(2)}) %collective-permute-start.4) | collective-permute-done | bytes 131104 | tf_op jit(solution)/shard_map/ppermute | solution.py:256
  14.6 0.0 collective-permute-done.3.refs_4_
  14.6 0.0 collective-permute-done.1.refs_2_
  14.6 0.0 collective-permute-done.2.refs_3_
  14.6 3.7 %shard_map.38 = (bf16[2,32,1024]{2,1,0:T(8,128)(2,1)S(1)}, bf16[2,32,1024]{2,1,0:T(8,128)(2,1)S(1)}, bf16[2,32,1024]{2,1,0:T(8,128)(2,1)S(1)}, f32[2,2,32,1024]{...) custom-call(bf16[2,32,1024]{2,1,0:T(8,128)(2,1)S(1)} %get-tuple-element.17.refs_0_, ...), custom_call_target="tpu_custom_call" | custom-call | flops 6000000000 | bytes 6000000 | tf_op jit(solution)/shard_map/pallas_call | solution.py:239
  18.3 2.3 %collective-permute-start.6 = (bf16[2,2,32,1024]{3,2,1,0:T(8,128)(2,1)S(1)}, bf16[2,2,32,1024]{3,2,1,0:T(8,128)(2,1)S(1)}, u32[]{:S(2)}, u32[]{:S(2)}) collective-permute-start(bf16[2,2,32,1024]{3,2,1,0:T(8,128)(2,1)S(1)} %get-tuple-element.25), channel_id=1, source_target_pairs={{0,1},{1,0},{2,3},{3,2},{4,5},{5,4},{6,7},{7,6},{8,9},{9,8},{10,11... | collective-permute-start | bytes 786440 | tf_op jit(solution)/shard_map/ppermute | solution.py:260
  20.6 0.0 collective-permute-start.8
  20.6 3.7 %collective-permute-start.9 = (bf16[2,32,1024]{2,1,0:T(8,128)(2,1)S(1)}, bf16[2,32,1024]{2,1,0:T(8,128)(2,1)S(1)}, u32[]{:S(2)}, u32[]{:S(2)}) collective-permute-start(bf16[2,32,1024]{2,1,0:T(8,128)(2,1)S(1)} %get-tuple-element.27), channel_id=1, source_target_pairs={{0,252},{4,0},{8,4},{12,8},{16,12},{20,16},{24,20},{28,24},{32,28}... | collective-permute-start | bytes 393224 | tf_op jit(solution)/shard_map/ppermute | solution.py:256
  24.3 0.5 %collective-permute-start.10 = (bf16[2,32,1024]{2,1,0:T(8,128)(2,1)S(1)}, bf16[2,32,1024]{2,1,0:T(8,128)(2,1)S(1)}, u32[]{:S(2)}, u32[]{:S(2)}) collective-permute-start(bf16[2,32,1024]{2,1,0:T(8,128)(2,1)S(1)} %get-tuple-element.28), channel_id=1, source_target_pairs={{0,244},{4,248},{8,252},{12,0},{16,4},{20,8},{24,12},{28,16},{32,2... | collective-permute-start | bytes 393224 | tf_op jit(solution)/shard_map/ppermute | solution.py:256
  24.8 0.0 collective-permute-done.6
  24.8 1.9 %collective-permute-start.7 = (bf16[2,32,1024]{2,1,0:T(8,128)(2,1)S(1)}, bf16[2,32,1024]{2,1,0:T(8,128)(2,1)S(1)}, u32[]{:S(2)}, u32[]{:S(2)}) collective-permute-start(bf16[2,32,1024]{2,1,0:T(8,128)(2,1)S(1)} %fusion.4), channel_id=1, source_target_pairs={{0,2},{1,3},{2,0},{3,1},{4,6},{5,7},{6,4},{7,5},{8,10},{9,11},{10,... | collective-permute-start | bytes 393224 | tf_op jit(solution)/shard_map/ppermute | solution.py:260
  26.7 2.2 %collective-permute-done.8 = bf16[2,32,1024]{2,1,0:T(8,128)(2,1)S(1)} collective-permute-done((bf16[2,32,1024]{2,1,0:T(8,128)(2,1)S(1)}, bf16[2,32,1024]{2,1,0:T(8,128)(2,1)S(1)}, u32[]{:S(2)}, u32[]{:S(2)}) %collective-permute-start.8) | collective-permute-done | bytes 131104 | tf_op jit(solution)/shard_map/ppermute | solution.py:256
  28.9 0.0 collective-permute-done.9
  28.9 3.2 %collective-permute-done.10 = bf16[2,32,1024]{2,1,0:T(8,128)(2,1)S(1)} collective-permute-done((bf16[2,32,1024]{2,1,0:T(8,128)(2,1)S(1)}, bf16[2,32,1024]{2,1,0:T(8,128)(2,1)S(1)}, u32[]{:S(2)}, u32[]{:S(2)}) %collective-permute-start.10) | collective-permute-done | bytes 131104 | tf_op jit(solution)/shard_map/ppermute | solution.py:256
  32.2 5.1 %collective-permute-done.7 = bf16[2,32,1024]{2,1,0:T(8,128)(2,1)S(1)} collective-permute-done((bf16[2,32,1024]{2,1,0:T(8,128)(2,1)S(1)}, bf16[2,32,1024]{2,1,0:T(8,128)(2,1)S(1)}, u32[]{:S(2)}, u32[]{:S(2)}) %collective-permute-start.7) | collective-permute-done | bytes 131104 | tf_op jit(solution)/shard_map/ppermute | solution.py:260
  37.2 0.8 %fusion.3 = f32[1,1,2,32,1024]{4,3,2,1,0:T(8,128)} fusion(bf16[2,32,1024]{2,1,0:T(8,128)(2,1)S(1)} %collective-permute-done.10, bf16[2,32,1024]{2,1,0:T(8,128)(2,1)S(1)} %collective-permute-done.9, bf16[2,32,1024]{2,1,0:T(8,128)(2,1)S(1)} %collective-permute-done.8, bf16[2,32,1024]{2,1,0:T(8,128)(2,1)S(1)} %collective-permute-done.7, ...), kind=kLoop, calls=%fused_computation.4 | loop fusion | flops 655360 | bytes 1179648 | tf_op jit(solution)/shard_map/broadcast_in_dim | solution.py:280
  (1 shorter events, 0.0 us)
Async XLA Ops:
  0.0 10.7 %collective-permute-start = (bf16[2,32,1024]{2,1,0:T(8,128)(2,1)}, bf16[2,32,1024]{2,1,0:T(8,128)(2,1)S(1)}, u32[]{:S(2)}, u32[]{:S(2)}) collective-permute-start(bf16[2,32,1024]{2,1,0:T(8,128)(2,1)} %bitcast.18), channel_id=1, source_target_pairs={{0,2},{1,3},{2,0},{3,1},{4,6},{5,7},{6,4},{7,5},{8,10},{9,11},{10,... | collective-permute-start | bytes 393224 | tf_op jit(solution)/shard_map/ppermute | solution.py:260
  2.7 10.9 %collective-permute-start.5 = (bf16[2,32,1024]{2,1,0:T(8,128)(2,1)}, bf16[2,32,1024]{2,1,0:T(8,128)(2,1)S(1)}, u32[]{:S(2)}, u32[]{:S(2)}) collective-permute-start(bf16[2,32,1024]{2,1,0:T(8,128)(2,1)} %bitcast.19), channel_id=1, source_target_pairs={{0,12},{4,16},{8,20},{12,24},{16,28},{20,32},{24,36},{28,40},{32,4... | collective-permute-start | bytes 393224 | tf_op jit(solution)/shard_map/ppermute | solution.py:256
  5.5 9.1 %collective-permute-start.4 = (bf16[2,32,1024]{2,1,0:T(8,128)(2,1)}, bf16[2,32,1024]{2,1,0:T(8,128)(2,1)S(1)}, u32[]{:S(2)}, u32[]{:S(2)}) collective-permute-start(bf16[2,32,1024]{2,1,0:T(8,128)(2,1)} %bitcast.20), channel_id=1, source_target_pairs={{0,4},{4,8},{8,12},{12,16},{16,20},{20,24},{24,28},{28,32},{32,36}... | collective-permute-start | bytes 393224 | tf_op jit(solution)/shard_map/ppermute | solution.py:256
  5.5 9.1 %collective-permute-start.3 = (bf16[2,32,1024]{2,1,0:T(8,128)(2,1)}, bf16[2,32,1024]{2,1,0:T(8,128)(2,1)S(1)}, u32[]{:S(2)}, u32[]{:S(2)}) collective-permute-start(bf16[2,32,1024]{2,1,0:T(8,128)(2,1)} %bitcast.21), channel_id=1, source_target_pairs={{0,248},{4,252},{8,0},{12,4},{16,8},{20,12},{24,16},{28,20},{32,24... | collective-permute-start | bytes 393224 | tf_op jit(solution)/shard_map/ppermute | solution.py:256
  8.9 5.6 %collective-permute-start.1 = (bf16[2,32,1024]{2,1,0:T(8,128)(2,1)}, bf16[2,32,1024]{2,1,0:T(8,128)(2,1)S(1)}, u32[]{:S(2)}, u32[]{:S(2)}) collective-permute-start(bf16[2,32,1024]{2,1,0:T(8,128)(2,1)} %bitcast.22), channel_id=1, source_target_pairs={{0,1},{1,0},{2,3},{3,2},{4,5},{5,4},{6,7},{7,6},{8,9},{9,8},{10,11... | collective-permute-start | bytes 393224 | tf_op jit(solution)/shard_map/ppermute | solution.py:260
  10.7 3.9 %collective-permute-start.2 = (bf16[2,32,1024]{2,1,0:T(8,128)(2,1)S(1)}, bf16[2,32,1024]{2,1,0:T(8,128)(2,1)S(1)}, u32[]{:S(2)}, u32[]{:S(2)}) collective-permute-start(bf16[2,32,1024]{2,1,0:T(8,128)(2,1)S(1)} %collective-permute-done.refs_1_), channel_id=1, source_target_pairs={{0,1},{1,0},{2,3},{3,2},{4,5},{5,4},{6,7},{7,6},{8,9},{9,8},{10,11... | collective-permute-start | bytes 393224 | tf_op jit(solution)/shard_map/ppermute | solution.py:260
  10.7 0.7 %copy-start.1 = (s32[64,3]{0,1:T(4,128)S(1)}, s32[64,3]{0,1:T(4,128)}, u32[]{:S(2)}) copy-start(s32[64,3]{0,1:T(4,128)} %param.4) | copy-start | bytes 2308
  10.8 0.7 %copy-start.2 = (s32[64]{0:T(128)S(1)}, s32[64]{0:T(128)}, u32[]{:S(2)}) copy-start(s32[64]{0:T(128)} %occupied.1) | copy-start | bytes 772
  11.5 0.9 %copy-start = (bf16[1,1,2,32,1024]{4,3,2,1,0:T(8,128)(2,1)S(1)}, bf16[1,1,2,32,1024]{4,3,2,1,0:T(8,128)(2,1)}, u32[]{:S(2)}) copy-start(bf16[1,1,2,32,1024]{4,3,2,1,0:T(8,128)(2,1)} %param.3) | copy-start | bytes 393220
  18.3 6.5 %collective-permute-start.6 = (bf16[2,2,32,1024]{3,2,1,0:T(8,128)(2,1)S(1)}, bf16[2,2,32,1024]{3,2,1,0:T(8,128)(2,1)S(1)}, u32[]{:S(2)}, u32[]{:S(2)}) collective-permute-start(bf16[2,2,32,1024]{3,2,1,0:T(8,128)(2,1)S(1)} %get-tuple-element.25), channel_id=1, source_target_pairs={{0,1},{1,0},{2,3},{3,2},{4,5},{5,4},{6,7},{7,6},{8,9},{9,8},{10,11... | collective-permute-start | bytes 786440 | tf_op jit(solution)/shard_map/ppermute | solution.py:260
  20.6 8.4 %collective-permute-start.8 = (bf16[2,32,1024]{2,1,0:T(8,128)(2,1)S(1)}, bf16[2,32,1024]{2,1,0:T(8,128)(2,1)S(1)}, u32[]{:S(2)}, u32[]{:S(2)}) collective-permute-start(bf16[2,32,1024]{2,1,0:T(8,128)(2,1)S(1)} %get-tuple-element.26), channel_id=1, source_target_pairs={{0,8},{4,12},{8,16},{12,20},{16,24},{20,28},{24,32},{28,36},{32,40... | collective-permute-start | bytes 393224 | tf_op jit(solution)/shard_map/ppermute | solution.py:256
  20.6 8.4 %collective-permute-start.9 = (bf16[2,32,1024]{2,1,0:T(8,128)(2,1)S(1)}, bf16[2,32,1024]{2,1,0:T(8,128)(2,1)S(1)}, u32[]{:S(2)}, u32[]{:S(2)}) collective-permute-start(bf16[2,32,1024]{2,1,0:T(8,128)(2,1)S(1)} %get-tuple-element.27), channel_id=1, source_target_pairs={{0,252},{4,0},{8,4},{12,8},{16,12},{20,16},{24,20},{28,24},{32,28}... | collective-permute-start | bytes 393224 | tf_op jit(solution)/shard_map/ppermute | solution.py:256
  24.3 7.9 %collective-permute-start.10 = (bf16[2,32,1024]{2,1,0:T(8,128)(2,1)S(1)}, bf16[2,32,1024]{2,1,0:T(8,128)(2,1)S(1)}, u32[]{:S(2)}, u32[]{:S(2)}) collective-permute-start(bf16[2,32,1024]{2,1,0:T(8,128)(2,1)S(1)} %get-tuple-element.28), channel_id=1, source_target_pairs={{0,244},{4,248},{8,252},{12,0},{16,4},{20,8},{24,12},{28,16},{32,2... | collective-permute-start | bytes 393224 | tf_op jit(solution)/shard_map/ppermute | solution.py:256
  24.8 12.4 %collective-permute-start.7 = (bf16[2,32,1024]{2,1,0:T(8,128)(2,1)S(1)}, bf16[2,32,1024]{2,1,0:T(8,128)(2,1)S(1)}, u32[]{:S(2)}, u32[]{:S(2)}) collective-permute-start(bf16[2,32,1024]{2,1,0:T(8,128)(2,1)S(1)} %fusion.4), channel_id=1, source_target_pairs={{0,2},{1,3},{2,0},{3,1},{4,6},{5,7},{6,4},{7,5},{8,10},{9,11},{10,... | collective-permute-start | bytes 393224 | tf_op jit(solution)/shard_map/ppermute | solution.py:260

commit v4 on v3

v4 whole, which is shorter than its diff:
```python
import functools
import math

import jax
import jax.numpy as jnp
from jax import lax
from jax.experimental import pallas as pl
from jax.experimental.pallas import tpu as pltpu
from jax.sharding import PartitionSpec as P

KMESH = 8
SHIFTS = ((2, 2, -3, -1), (3, 1, -1, -3), (-3, -1, 2, 2))
GRID = 32
LANES = 128
CELL = 20.52
SCREENING = 0.05
BANDS = 4
FLIPS = (0, 2, 1, 3)
VMEM_BYTES = 32 * 1024 * 1024


def block(index):
    return slice(index * LANES, (index + 1) * LANES)


def rows(index):
    return slice(index * GRID, (index + 1) * GRID)


def dot(left, right, dims=((1,), (0,))):
    return lax.dot_general(left, right, (dims, ((), ())), preferred_element_type=jnp.float32)


def table_kernel(forward_x, inverse_x, forward_yz, inverse_yz):
    turn = 2 * math.pi / GRID
    square = (LANES, LANES)
    row = lax.broadcasted_iota(jnp.int32, square, 0)
    column = lax.broadcasted_iota(jnp.int32, square, 1)
    row_high, column_high = lax.shift_right_logical(row, 5), lax.shift_right_logical(column, 5)

    def cosine_of(turns):
        turns = jnp.abs(jnp.bitwise_and(turns + GRID // 2, GRID - 1) - GRID // 2)
        folded = jnp.minimum(turns, GRID // 2 - turns).astype(jnp.float32)
        square = folded * folded * (turn * turn)
        series = 1.0
        for order in (10, 8, 6, 4, 2):
            series = 1.0 - square * series * (1.0 / (order * (order - 1)))
        return jnp.where(turns > GRID // 4, -series, series)

    def wave(turns):
        return cosine_of(turns), cosine_of(turns - GRID // 4)

    def put(table, at, upper, lower):
        table[at, :LANES] = jnp.concatenate(upper, axis=1).astype(table.dtype)
        table[at, LANES:] = jnp.concatenate(lower, axis=1).astype(table.dtype)

    low = jnp.bitwise_and(row, GRID - 1) * jnp.bitwise_and(column, GRID - 1)
    cosine, sine = wave(8 * row_high * column_high + low)
    row_cosine, row_sine = wave(row_high)
    column_cosine, column_sine = wave(column_high)
    down = across = (cosine, sine)
    for k1 in range(8):
        put(forward_yz, k1, (down[0], -down[1]), (down[1], down[0]))
        put(inverse_yz, k1, (across[0], across[1]), (-across[1], across[0]))
        if k1 % 4 == 0:
            put(forward_x, k1 // 4, (down[0], down[1]), (-down[1], down[0]))
            put(inverse_x, k1 // 4, (across[0], -across[1]), (across[1], across[0]))
        down = (
            down[0] * row_cosine - down[1] * row_sine,
            down[0] * row_sine + down[1] * row_cosine,
        )
        across = (
            across[0] * column_cosine - across[1] * column_sine,
            across[0] * column_sine + across[1] * column_cosine,
        )


def point_kernel(kpoints, occupied, spot, screened, weights):
    count = kpoints.shape[1]
    own = spot[0]
    slot = spot[1]
    unit = 2 * math.pi / CELL
    shape = (GRID, LANES)
    lane = lax.broadcasted_iota(jnp.int32, shape, 1)
    high = lax.shift_right_logical(lane, 5) * 8

    def centred(index):
        return (jnp.bitwise_and(index + GRID // 2, GRID - 1) - GRID // 2).astype(jnp.float32)

    def occupancy(point, band):
        return jnp.full((1, LANES), jnp.where(band < occupied[point], -1.0, 0.0), jnp.float32)

    grid_x = centred(lax.broadcasted_iota(jnp.int32, shape, 0))
    grid_z = centred(jnp.bitwise_and(lane, GRID - 1))
    for at, shifts in enumerate(SHIFTS):
        step = shifts[0]
        for turn in range(1, len(shifts)):
            step = jnp.where(lax.rem(own, len(shifts)) == turn, shifts[turn], step)
        other = lax.rem(own - step + count, count)
        later, earlier = jnp.where(step > 0, own, other), jnp.where(step > 0, other, own)
        along = []
        for i in range(3):
            apart = lax.rem(kpoints[i, later] - kpoints[i, earlier] + KMESH // 2 + KMESH, KMESH)
            along.append((apart - KMESH // 2).astype(jnp.float32) / KMESH)
        at_x = (grid_x + along[0]) * unit
        at_z = (grid_z + along[2]) * unit
        flat = at_x * at_x + at_z * at_z + SCREENING
        for k1 in range(8):
            at_y = (centred(high + k1) + along[1]) * unit
            screened[at, k1] = (math.pi / GRID**3) / (flat + at_y * at_y)
        weights[4 + at] = occupancy(other, slot)
        sign = jnp.where(step > 0, 1.0, -1.0)
        weights[7 + at] = jnp.full((1, LANES), sign, jnp.float32)
    for flip in range(4):
        weights[flip] = occupancy(own, slot ^ flip)


def tables_of(kpoints, occupied, spot):
    smem = pl.BlockSpec(memory_space=pltpu.SMEM)
    vmem = pl.BlockSpec(memory_space=pltpu.VMEM)
    params = pltpu.CompilerParams(vmem_limit_bytes=VMEM_BYTES)
    tables = pl.pallas_call(
        table_kernel,
        out_shape=[jax.ShapeDtypeStruct((count, 256, 256), jnp.bfloat16) for count in (2, 2, 8, 8)],
        out_specs=[vmem] * 4,
        compiler_params=params,
        cost_estimate=pl.CostEstimate(flops=2 * 10**9, bytes_accessed=3 * 10**6, transcendentals=0),
    )()
    points = pl.pallas_call(
        point_kernel,
        out_shape=[
            jax.ShapeDtypeStruct((len(SHIFTS), 8, GRID, LANES), jnp.float32),
            jax.ShapeDtypeStruct((4 + 2 * len(SHIFTS), 1, LANES), jnp.float32),
        ],
        in_specs=[smem] * 3,
        out_specs=[vmem] * 2,
        compiler_params=params,
        cost_estimate=pl.CostEstimate(flops=10**8, bytes_accessed=10**5, transcendentals=0),
    )(kpoints, occupied, spot)
    return (*tables, *points)


def pair_kernel(*refs):
    bands, mates = refs[:4], refs[4:7]
    forward_x, inverse_x, forward_yz, inverse_yz, screened, weights = refs[7:13]
    mates_out = refs[13:16]
    sums = [refs[16], refs[17], refs[18].at[0], refs[18].at[1]]
    wide, mid, back = refs[19:]
    signs = [weights[7 + m] for m in range(len(SHIFTS))]

    for b in range(2):
        for a in range(4):
            cut = block(2 * a + b)
            for n in range(BANDS):
                band_re = bands[n][0, :, cut].astype(jnp.float32)
                band_im = bands[n][1, :, cut].astype(jnp.float32)
                for m in range(len(SHIFTS)):
                    job, i = 2 * m + n // 2, n % 2
                    mate_re = mates[m][0, :, cut].astype(jnp.float32)
                    mate_im = mates[m][1, :, cut].astype(jnp.float32)
                    value_re = mate_re * band_re + mate_im * band_im
                    value_im = (mate_re * band_im - mate_im * band_re) * signs[m]
                    wide[b, job, rows(a), block(i)] = value_re.astype(jnp.bfloat16)
                    wide[b, job, rows(4 + a), block(i)] = value_im.astype(jnp.bfloat16)

    for job in range(2 * len(SHIFTS)):
        even = dot(forward_x[0], wide[0, job])
        odd = dot(forward_x[1], wide[1, job])
        plus = (even + odd).astype(jnp.bfloat16)
        minus = (even - odd).astype(jnp.bfloat16)
        for i in range(2):
            for e in range(4):
                for c in range(2):
                    mid[e, rows(2 * job + i), block(c)] = plus[rows(4 * c + e), block(i)]
                    mid[e + 4, rows(2 * job + i), block(c)] = minus[rows(4 * c + e), block(i)]

    for e in range(4):
        halves = []
        for k1 in (e, e + 4):
            third = dot(mid[k1], forward_yz[k1])
            factor = []
            for m in range(len(SHIFTS)):
                factor += [jnp.concatenate([screened[m, k1]] * 2, axis=1)] * BANDS
            factor = jnp.concatenate(factor, axis=0)
            halves.append(dot((third * factor).astype(jnp.bfloat16), inverse_yz[k1]))
        for b in range(2):
            joined = (halves[0] - halves[1] if b else halves[0] + halves[1]).astype(jnp.bfloat16)
            for job in range(2 * len(SHIFTS)):
                for i in range(2):
                    for c in range(2):
                        back[b, job, rows(4 * c + e), block(i)] = joined[rows(2 * job + i), block(c)]

    for b in range(2):
        waves = [dot(inverse_x[b], back[b, job]) for job in range(2 * len(SHIFTS))]
        for a in range(4):
            cut = block(2 * a + b)
            mate_total = [[0.0, 0.0] for _ in mates]
            band_total = [[0.0, 0.0] for _ in bands]
            for m in range(len(SHIFTS)):
                mate_re = mates[m][0, :, cut].astype(jnp.float32) * weights[4 + m]
                mate_im = mates[m][1, :, cut].astype(jnp.float32) * weights[4 + m]
                for n in range(BANDS):
                    band_re = bands[n][0, :, cut].astype(jnp.float32) * weights[FLIPS[n]]
                    band_im = bands[n][1, :, cut].astype(jnp.float32) * weights[FLIPS[n]]
                    wave_re = waves[2 * m + n // 2][rows(a), block(n % 2)]
                    wave_im = waves[2 * m + n // 2][rows(4 + a), block(n % 2)] * signs[m]
                    band_total[n][0] += mate_re * wave_re - mate_im * wave_im
                    band_total[n][1] += mate_re * wave_im + mate_im * wave_re
                    mate_total[m][0] += band_re * wave_re + band_im * wave_im
                    mate_total[m][1] += band_im * wave_re - band_re * wave_im
            for c in range(2):
                for m in range(len(SHIFTS)):
                    mates_out[m][c, :, cut] = mate_total[m][c].astype(mates_out[m].dtype)
                for n in range(BANDS):
                    sums[n][c, :, cut] = band_total[n][c].astype(sums[n].dtype)


def pair_terms(bands, mates, tables, short=jnp.bfloat16):
    vmem = pl.BlockSpec(memory_space=pltpu.VMEM)
    field = mates[0].shape
    jobs = 2 * len(SHIFTS)
    operands = [*bands, *mates, *tables]
    out_shape = [jax.ShapeDtypeStruct(field, kind) for kind in (short,) * len(SHIFTS) + (jnp.float32,) * 2]
    out_shape.append(jax.ShapeDtypeStruct((2,) + field, short))
    return pl.pallas_call(
        pair_kernel,
        out_shape=out_shape,
        in_specs=[vmem] * len(operands),
        out_specs=[vmem] * len(out_shape),
        scratch_shapes=[
            pltpu.VMEM((2, jobs, 256, 256), jnp.bfloat16),
            pltpu.VMEM((8, jobs * 2 * GRID, 256), jnp.bfloat16),
            pltpu.VMEM((2, jobs, 256, 256), jnp.bfloat16),
        ],
        compiler_params=pltpu.CompilerParams(vmem_limit_bytes=VMEM_BYTES),
        cost_estimate=pl.CostEstimate(flops=6 * 10**9, bytes_accessed=6 * 10**6, transcendentals=0),
    )(*operands)


def passed_along(value, shifts, back=False):
    count = lax.axis_size("ka")
    pairs = [((k - shifts[k % len(shifts)]) % count, k) for k in range(count)]
    if back:
        pairs = [(to, start) for start, to in pairs]
    return lax.ppermute(value, "ka", pairs)


def swapped(value, flip):
    return lax.ppermute(value, "ba", [(i, i ^ flip) for i in range(lax.axis_size("ba"))])


def on_device(orbitals, kpoints, occupied):
    own = orbitals[0, 0]
    spot = jnp.stack([lax.axis_index("ka"), lax.axis_index("ba")])
    tables = tables_of(kpoints.T, occupied, spot)
    across = swapped(own, 2)
    bands = (own, across, swapped(own, 1), swapped(across, 1))
    mates = [passed_along(own, shifts) for shifts in SHIFTS]
    *terms, own_sum, across_sum, far_sum = pair_terms(bands, mates, tables)
    beside, beyond = swapped(far_sum, 1)
    leaving = (across_sum + beyond.astype(jnp.float32)).astype(jnp.bfloat16)
    total = own_sum + beside.astype(jnp.float32) + swapped(leaving, 2).astype(jnp.float32)
    for at in (0, 1, 2):
        total = total + passed_along(terms[at], SHIFTS[at], back=True).astype(jnp.float32)
    return total[None, None]


def solution(mesh):
    in_specs = (P("ka", "ba", None, None, None), P(), P())
    out_specs = P("ka", "ba", None, None, None)
    return jax.shard_map(
        on_device, mesh=mesh, in_specs=in_specs, out_specs=out_specs, check_vma=False
    )
```

time: 38.2 us -> 36.5 us (0.955)
  the two profiles are of different devices: /device:TPU:225 before, /device:TPU:8 now
where the time goes in v4:
time: 36.5 us; the launch traced here: 36.4 us
  starting transfers between devices  20.5 us (56%)
  waiting for transfers between devices  9.38 us (26%)
  Pallas kernels  4.84 us (13%)
  other arithmetic  0.9 us (2%)
  local copies, waits for them, and re-layouts  0.66 us (2%)
    ppermute x6, starting transfers between devices, passed_along(): return lax.ppermute(value, 'ka', pairs)  15.5 us
    ppermute x6, waiting for transfers between devices, passed_along(): return lax.ppermute(value, 'ka', pairs)  9.37 us
    ppermute x5, starting transfers between devices, swapped(): lax.ppermute(value, 'ba', [(i, i ^ flip) for i in range(lax.axis_size('ba...  5.03 us
    pallas_call x1, Pallas kernels, pair_terms(): pl.pallas_call(pair_kernel, out_shape=out_shape, in_specs=[vmem] * len(op...  3.55 us
    broadcast_in_dim x1, other arithmetic, on_device(): return total[None, None]  0.8 us
  transfers between devices with their start and end apart: 11, of which 4 were waited for; matrix products, arithmetic and copies ran while one was open for 0% of the time, Pallas kernels for 4%

profile of v4, /device:TPU:8, one launch (start us, length us, event | category | flops | bytes accessed | tf_op | source)
XLA Modules:
  0.0 36.4 jit_solution(17007048833648624890)
XLA Ops:
  0.0 3.0 %collective-permute-start = (bf16[2,32,1024]{2,1,0:T(8,128)(2,1)}, bf16[2,32,1024]{2,1,0:T(8,128)(2,1)S(1)}, u32[]{:S(2)}, u32[]{:S(2)}) collective-permute-start(bf16[2,32,1024]{2,1,0:T(8,128)(2,1)} %bitcast.16), channel_id=1, source_target_pairs={{0,2},{1,3},{2,0},{3,1},{4,6},{5,7},{6,4},{7,5},{8,10},{9,11},{10,... | collective-permute-start | bytes 393224 | tf_op jit(solution)/shard_map/ppermute | solution.py:249
  3.0 2.3 %collective-permute-start.5 = (bf16[2,32,1024]{2,1,0:T(8,128)(2,1)}, bf16[2,32,1024]{2,1,0:T(8,128)(2,1)S(1)}, u32[]{:S(2)}, u32[]{:S(2)}) collective-permute-start(bf16[2,32,1024]{2,1,0:T(8,128)(2,1)} %bitcast.17), channel_id=1, source_target_pairs={{12,0},{8,4},{0,8},{4,12},{28,16},{24,20},{16,24},{20,28},{44,32},... | collective-permute-start | bytes 393224 | tf_op jit(solution)/shard_map/ppermute | solution.py:245
  5.3 1.4 %collective-permute-start.4 = (bf16[2,32,1024]{2,1,0:T(8,128)(2,1)}, bf16[2,32,1024]{2,1,0:T(8,128)(2,1)S(1)}, u32[]{:S(2)}, u32[]{:S(2)}) collective-permute-start(bf16[2,32,1024]{2,1,0:T(8,128)(2,1)} %bitcast.18), channel_id=1, source_target_pairs={{244,0},{0,4},{12,8},{24,12},{4,16},{16,20},{28,24},{40,28},{20,32... | collective-permute-start | bytes 393224 | tf_op jit(solution)/shard_map/ppermute | solution.py:245
  6.7 5.6 %collective-permute-start.3 = (bf16[2,32,1024]{2,1,0:T(8,128)(2,1)}, bf16[2,32,1024]{2,1,0:T(8,128)(2,1)S(1)}, u32[]{:S(2)}, u32[]{:S(2)}) collective-permute-start(bf16[2,32,1024]{2,1,0:T(8,128)(2,1)} %bitcast.19), channel_id=1, source_target_pairs={{248,0},{252,4},{20,8},{16,12},{8,16},{12,20},{36,24},{32,28},{24,... | collective-permute-start | bytes 393224 | tf_op jit(solution)/shard_map/ppermute | solution.py:245
  12.3 0.0 collective-permute-start.1
  12.3 0.0 copy-start.1
  12.3 0.1 pad_add_fusion.spot
  12.4 0.0 copy-start.2
  12.4 0.6 %copy-done.1 = s32[64,3]{0,1:T(4,128)S(1)} copy-done((s32[64,3]{0,1:T(4,128)S(1)}, s32[64,3]{0,1:T(4,128)}, u32[]{:S(2)}) %copy-start.1) | copy-done | bytes 792
  13.0 0.1 copy-done.2
  13.0 0.7 %shard_map.38 = (f32[3,8,32,128]{3,2,1,0:T(8,128)S(1)}, f32[10,1,128]{2,1,0:T(1,128)S(1)}) custom-call(s32[3,64]{1,0:T(4,128)S(1)} %bitcast.22, s32[64]{0:T(128)S(1)} %copy-done.2, s32[2]{0:T(128)S(1)} %pad_add_fusion.spot), custom_call_target="tpu_custom_call" | custom-call | flops 100000000 | bytes 100000 | tf_op jit(solution)/shard_map/pallas_call | solution.py:129
  13.7 0.0 copy-start
  13.7 0.0 collective-permute-done.refs_1_
  13.7 0.6 %collective-permute-start.2 = (bf16[2,32,1024]{2,1,0:T(8,128)(2,1)S(1)}, bf16[2,32,1024]{2,1,0:T(8,128)(2,1)S(1)}, u32[]{:S(2)}, u32[]{:S(2)}) collective-permute-start(bf16[2,32,1024]{2,1,0:T(8,128)(2,1)S(1)} %collective-permute-done.refs_1_), channel_id=1, source_target_pairs={{0,1},{1,0},{2,3},{3,2},{4,5},{5,4},{6,7},{7,6},{8,9},{9,8},{10,11... | collective-permute-start | bytes 393224 | tf_op jit(solution)/shard_map/ppermute | solution.py:249
  14.3 0.6 %shard_map.37 = (bf16[2,256,256]{2,1,0:T(8,128)(2,1)S(1)}, bf16[2,256,256]{2,1,0:T(8,128)(2,1)S(1)}, bf16[8,256,256]{2,1,0:T(8,128)(2,1)S(1)}, bf16[8,256,256]{2,1,0:T(8,128)(2,1)S(1)}) custom-call(), custom_call_target="tpu_custom_call" | custom-call | flops 2000000000 | bytes 3000000 | tf_op jit(solution)/shard_map/pallas_call | solution.py:122
  15.0 0.0 collective-permute-done.5.refs_6_
  15.0 0.0 collective-permute-done.4.refs_5_
  15.0 1.4 %collective-permute-done.3.refs_4_ = bf16[2,32,1024]{2,1,0:T(8,128)(2,1)S(1)} collective-permute-done((bf16[2,32,1024]{2,1,0:T(8,128)(2,1)}, bf16[2,32,1024]{2,1,0:T(8,128)(2,1)S(1)}, u32[]{:S(2)}, u32[]{:S(2)}) %collective-permute-start.3) | collective-permute-done | bytes 131104 | tf_op jit(solution)/shard_map/ppermute | solution.py:245
  16.4 0.0 collective-permute-done.1.refs_2_
  16.4 0.0 collective-permute-done.2.refs_3_
  16.4 0.0 copy-done
  16.4 3.6 %shard_map.39 = (bf16[2,32,1024]{2,1,0:T(8,128)(2,1)S(1)}, bf16[2,32,1024]{2,1,0:T(8,128)(2,1)S(1)}, bf16[2,32,1024]{2,1,0:T(8,128)(2,1)S(1)}, f32[2,32,1024]{2,...) custom-call(bf16[2,32,1024]{2,1,0:T(8,128)(2,1)S(1)} %bitcast.21, ...), custom_call_target="tpu_custom_call" | custom-call | flops 6000000000 | bytes 6000000 | tf_op jit(solution)/shard_map/pallas_call | solution.py:225
  20.0 0.1 collective-permute-start.6
  20.1 5.1 %collective-permute-start.8 = (bf16[2,32,1024]{2,1,0:T(8,128)(2,1)S(1)}, bf16[2,32,1024]{2,1,0:T(8,128)(2,1)S(1)}, u32[]{:S(2)}, u32[]{:S(2)}) collective-permute-start(bf16[2,32,1024]{2,1,0:T(8,128)(2,1)S(1)} %get-tuple-element.26), channel_id=1, source_target_pairs={{0,248},{4,252},{8,20},{12,16},{16,8},{20,12},{24,36},{28,32},{32,... | collective-permute-start | bytes 393224 | tf_op jit(solution)/shard_map/ppermute | solution.py:245
  25.2 1.1 %collective-permute-start.9 = (bf16[2,32,1024]{2,1,0:T(8,128)(2,1)S(1)}, bf16[2,32,1024]{2,1,0:T(8,128)(2,1)S(1)}, u32[]{:S(2)}, u32[]{:S(2)}) collective-permute-start(bf16[2,32,1024]{2,1,0:T(8,128)(2,1)S(1)} %get-tuple-element.27), channel_id=1, source_target_pairs={{0,244},{4,0},{8,12},{12,24},{16,4},{20,16},{24,28},{28,40},{32,20... | collective-permute-start | bytes 393224 | tf_op jit(solution)/shard_map/ppermute | solution.py:245
  26.3 0.0 collective-permute-start.10
  26.3 0.0 collective-permute-done.6
  26.3 1.3 %collective-permute-start.7 = (bf16[2,32,1024]{2,1,0:T(8,128)(2,1)S(1)}, bf16[2,32,1024]{2,1,0:T(8,128)(2,1)S(1)}, u32[]{:S(2)}, u32[]{:S(2)}) collective-permute-start(bf16[2,32,1024]{2,1,0:T(8,128)(2,1)S(1)} %fusion), channel_id=1, source_target_pairs={{0,2},{1,3},{2,0},{3,1},{4,6},{5,7},{6,4},{7,5},{8,10},{9,11},{10,... | collective-permute-start | bytes 393224 | tf_op jit(solution)/shard_map/ppermute | solution.py:249
  27.7 1.3 %collective-permute-done.8 = bf16[2,32,1024]{2,1,0:T(8,128)(2,1)S(1)} collective-permute-done((bf16[2,32,1024]{2,1,0:T(8,128)(2,1)S(1)}, bf16[2,32,1024]{2,1,0:T(8,128)(2,1)S(1)}, u32[]{:S(2)}, u32[]{:S(2)}) %collective-permute-start.8) | collective-permute-done | bytes 131104 | tf_op jit(solution)/shard_map/ppermute | solution.py:245
  29.0 3.4 %collective-permute-done.9 = bf16[2,32,1024]{2,1,0:T(8,128)(2,1)S(1)} collective-permute-done((bf16[2,32,1024]{2,1,0:T(8,128)(2,1)S(1)}, bf16[2,32,1024]{2,1,0:T(8,128)(2,1)S(1)}, u32[]{:S(2)}, u32[]{:S(2)}) %collective-permute-start.9) | collective-permute-done | bytes 131104 | tf_op jit(solution)/shard_map/ppermute | solution.py:245
  32.4 3.2 %collective-permute-done.10 = bf16[2,32,1024]{2,1,0:T(8,128)(2,1)S(1)} collective-permute-done((bf16[2,32,1024]{2,1,0:T(8,128)(2,1)S(1)}, bf16[2,32,1024]{2,1,0:T(8,128)(2,1)S(1)}, u32[]{:S(2)}, u32[]{:S(2)}) %collective-permute-start.10) | collective-permute-done | bytes 131104 | tf_op jit(solution)/shard_map/ppermute | solution.py:245
  35.6 0.0 collective-permute-done.7
  35.6 0.8 %fusion.5 = f32[1,1,2,32,1024]{4,3,2,1,0:T(8,128)} fusion(f32[2,32,1024]{2,1,0:T(8,128)S(1)} %get-tuple-element.23, bf16[2,32,1024]{2,1,0:T(8,128)(2,1)S(1)} %collective-permute-done.10, bf16[2,32,1024]{2,1,0:T(8,128)(2,1)S(1)} %collective-permute-done.9, bf16[2,32,1024]{2,1,0:T(8,128)(2,1)S(1)} %collective-permute-done.8, ...), kind=kLoop, calls=%fused_computation.7 | loop fusion | flops 655360 | bytes 1179648 | tf_op jit(solution)/shard_map/broadcast_in_dim | solution.py:265
  (1 shorter events, 0.0 us)
Async XLA Ops:
  0.0 13.7 %collective-permute-start = (bf16[2,32,1024]{2,1,0:T(8,128)(2,1)}, bf16[2,32,1024]{2,1,0:T(8,128)(2,1)S(1)}, u32[]{:S(2)}, u32[]{:S(2)}) collective-permute-start(bf16[2,32,1024]{2,1,0:T(8,128)(2,1)} %bitcast.16), channel_id=1, source_target_pairs={{0,2},{1,3},{2,0},{3,1},{4,6},{5,7},{6,4},{7,5},{8,10},{9,11},{10,... | collective-permute-start | bytes 393224 | tf_op jit(solution)/shard_map/ppermute | solution.py:249
  3.0 11.9 %collective-permute-start.5 = (bf16[2,32,1024]{2,1,0:T(8,128)(2,1)}, bf16[2,32,1024]{2,1,0:T(8,128)(2,1)S(1)}, u32[]{:S(2)}, u32[]{:S(2)}) collective-permute-start(bf16[2,32,1024]{2,1,0:T(8,128)(2,1)} %bitcast.17), channel_id=1, source_target_pairs={{12,0},{8,4},{0,8},{4,12},{28,16},{24,20},{16,24},{20,28},{44,32},... | collective-permute-start | bytes 393224 | tf_op jit(solution)/shard_map/ppermute | solution.py:245
  5.3 9.7 %collective-permute-start.4 = (bf16[2,32,1024]{2,1,0:T(8,128)(2,1)}, bf16[2,32,1024]{2,1,0:T(8,128)(2,1)S(1)}, u32[]{:S(2)}, u32[]{:S(2)}) collective-permute-start(bf16[2,32,1024]{2,1,0:T(8,128)(2,1)} %bitcast.18), channel_id=1, source_target_pairs={{244,0},{0,4},{12,8},{24,12},{4,16},{16,20},{28,24},{40,28},{20,32... | collective-permute-start | bytes 393224 | tf_op jit(solution)/shard_map/ppermute | solution.py:245
  6.7 9.7 %collective-permute-start.3 = (bf16[2,32,1024]{2,1,0:T(8,128)(2,1)}, bf16[2,32,1024]{2,1,0:T(8,128)(2,1)S(1)}, u32[]{:S(2)}, u32[]{:S(2)}) collective-permute-start(bf16[2,32,1024]{2,1,0:T(8,128)(2,1)} %bitcast.19), channel_id=1, source_target_pairs={{248,0},{252,4},{20,8},{16,12},{8,16},{12,20},{36,24},{32,28},{24,... | collective-permute-start | bytes 393224 | tf_op jit(solution)/shard_map/ppermute | solution.py:245
  12.3 4.1 %collective-permute-start.1 = (bf16[2,32,1024]{2,1,0:T(8,128)(2,1)}, bf16[2,32,1024]{2,1,0:T(8,128)(2,1)S(1)}, u32[]{:S(2)}, u32[]{:S(2)}) collective-permute-start(bf16[2,32,1024]{2,1,0:T(8,128)(2,1)} %bitcast.20), channel_id=1, source_target_pairs={{0,1},{1,0},{2,3},{3,2},{4,5},{5,4},{6,7},{7,6},{8,9},{9,8},{10,11... | collective-permute-start | bytes 393224 | tf_op jit(solution)/shard_map/ppermute | solution.py:249
  12.3 0.7 %copy-start.1 = (s32[64,3]{0,1:T(4,128)S(1)}, s32[64,3]{0,1:T(4,128)}, u32[]{:S(2)}) copy-start(s32[64,3]{0,1:T(4,128)} %param.4) | copy-start | bytes 2308
  12.4 0.7 %copy-start.2 = (s32[64]{0:T(128)S(1)}, s32[64]{0:T(128)}, u32[]{:S(2)}) copy-start(s32[64]{0:T(128)} %occupied.1) | copy-start | bytes 772
  13.7 2.7 %copy-start = (bf16[1,1,2,32,1024]{4,3,2,1,0:T(8,128)(2,1)S(1)}, bf16[1,1,2,32,1024]{4,3,2,1,0:T(8,128)(2,1)}, u32[]{:S(2)}) copy-start(bf16[1,1,2,32,1024]{4,3,2,1,0:T(8,128)(2,1)} %param.3) | copy-start | bytes 393220
  13.7 2.6 %collective-permute-start.2 = (bf16[2,32,1024]{2,1,0:T(8,128)(2,1)S(1)}, bf16[2,32,1024]{2,1,0:T(8,128)(2,1)S(1)}, u32[]{:S(2)}, u32[]{:S(2)}) collective-permute-start(bf16[2,32,1024]{2,1,0:T(8,128)(2,1)S(1)} %collective-permute-done.refs_1_), channel_id=1, source_target_pairs={{0,1},{1,0},{2,3},{3,2},{4,5},{5,4},{6,7},{7,6},{8,9},{9,8},{10,11... | collective-permute-start | bytes 393224 | tf_op jit(solution)/shard_map/ppermute | solution.py:249
  20.0 6.3 %collective-permute-start.6 = (bf16[2,2,32,1024]{3,2,1,0:T(8,128)(2,1)S(1)}, bf16[2,2,32,1024]{3,2,1,0:T(8,128)(2,1)S(1)}, u32[]{:S(2)}, u32[]{:S(2)}) collective-permute-start(bf16[2,2,32,1024]{3,2,1,0:T(8,128)(2,1)S(1)} %get-tuple-element.24), channel_id=1, source_target_pairs={{0,1},{1,0},{2,3},{3,2},{4,5},{5,4},{6,7},{7,6},{8,9},{9,8},{10,11... | collective-permute-start | bytes 786440 | tf_op jit(solution)/shard_map/ppermute | solution.py:249
  20.1 8.9 %collective-permute-start.8 = (bf16[2,32,1024]{2,1,0:T(8,128)(2,1)S(1)}, bf16[2,32,1024]{2,1,0:T(8,128)(2,1)S(1)}, u32[]{:S(2)}, u32[]{:S(2)}) collective-permute-start(bf16[2,32,1024]{2,1,0:T(8,128)(2,1)S(1)} %get-tuple-element.26), channel_id=1, source_target_pairs={{0,248},{4,252},{8,20},{12,16},{16,8},{20,12},{24,36},{28,32},{32,... | collective-permute-start | bytes 393224 | tf_op jit(solution)/shard_map/ppermute | solution.py:245
  25.2 7.2 %collective-permute-start.9 = (bf16[2,32,1024]{2,1,0:T(8,128)(2,1)S(1)}, bf16[2,32,1024]{2,1,0:T(8,128)(2,1)S(1)}, u32[]{:S(2)}, u32[]{:S(2)}) collective-permute-start(bf16[2,32,1024]{2,1,0:T(8,128)(2,1)S(1)} %get-tuple-element.27), channel_id=1, source_target_pairs={{0,244},{4,0},{8,12},{12,24},{16,4},{20,16},{24,28},{28,40},{32,20... | collective-permute-start | bytes 393224 | tf_op jit(solution)/shard_map/ppermute | solution.py:245
  26.3 9.3 %collective-permute-start.10 = (bf16[2,32,1024]{2,1,0:T(8,128)(2,1)S(1)}, bf16[2,32,1024]{2,1,0:T(8,128)(2,1)S(1)}, u32[]{:S(2)}, u32[]{:S(2)}) collective-permute-start(bf16[2,32,1024]{2,1,0:T(8,128)(2,1)S(1)} %get-tuple-element.28), channel_id=1, source_target_pairs={{0,12},{4,8},{8,0},{12,4},{16,28},{20,24},{24,16},{28,20},{32,44},... | collective-permute-start | bytes 393224 | tf_op jit(solution)/shard_map/ppermute | solution.py:245
  26.3 9.3 %collective-permute-start.7 = (bf16[2,32,1024]{2,1,0:T(8,128)(2,1)S(1)}, bf16[2,32,1024]{2,1,0:T(8,128)(2,1)S(1)}, u32[]{:S(2)}, u32[]{:S(2)}) collective-permute-start(bf16[2,32,1024]{2,1,0:T(8,128)(2,1)S(1)} %fusion), channel_id=1, source_target_pairs={{0,2},{1,3},{2,0},{3,1},{4,6},{5,7},{6,4},{7,5},{8,10},{9,11},{10,... | collective-permute-start | bytes 393224 | tf_op jit(solution)/shard_map/ppermute | solution.py:249

commit v5 on v4

--- a/solution.py
+++ b/solution.py
@@ -260,7 +260,7 @@
     beside, beyond = swapped(far_sum, 1)
     leaving = (across_sum + beyond.astype(jnp.float32)).astype(jnp.bfloat16)
     total = own_sum + beside.astype(jnp.float32) + swapped(leaving, 2).astype(jnp.float32)
-    for at in (0, 1, 2):
+    for at in (0, 2, 1):
         total = total + passed_along(terms[at], SHIFTS[at], back=True).astype(jnp.float32)
     return total[None, None]
 

time: 36.5 us -> 35.7 us (0.978)
  the two profiles are of different devices: /device:TPU:8 before, /device:TPU:6 now
where the time goes in v5:
time: 35.7 us; the launch traced here: 35.6 us
  starting transfers between devices  15.5 us (43%)
  waiting for transfers between devices  13.7 us (38%)
  Pallas kernels  4.84 us (14%)
  other arithmetic  0.9 us (3%)
  local copies, waits for them, and re-layouts  0.66 us (2%)
    ppermute x6, starting transfers between devices, passed_along(): return lax.ppermute(value, 'ka', pairs)  11 us
    ppermute x6, waiting for transfers between devices, passed_along(): return lax.ppermute(value, 'ka', pairs)  9.96 us
    ppermute x5, starting transfers between devices, swapped(): lax.ppermute(value, 'ba', [(i, i ^ flip) for i in range(lax.axis_size('ba...  4.48 us
    ppermute x5, waiting for transfers between devices, swapped(): lax.ppermute(value, 'ba', [(i, i ^ flip) for i in range(lax.axis_size('ba...  3.72 us
    pallas_call x1, Pallas kernels, pair_terms(): pl.pallas_call(pair_kernel, out_shape=out_shape, in_specs=[vmem] * len(op...  3.55 us
    broadcast_in_dim x1, other arithmetic, on_device(): return total[None, None]  0.8 us
  transfers between devices with their start and end apart: 11, of which 5 were waited for; matrix products, arithmetic and copies ran while one was open for 0% of the time, Pallas kernels for 4%

profile of v5, /device:TPU:6, one launch (start us, length us, event | category | flops | bytes accessed | tf_op | source)
XLA Modules:
  0.0 35.6 jit_solution(15261350751132410015)
XLA Ops:
  0.0 1.4 %collective-permute-start = (bf16[2,32,1024]{2,1,0:T(8,128)(2,1)}, bf16[2,32,1024]{2,1,0:T(8,128)(2,1)S(1)}, u32[]{:S(2)}, u32[]{:S(2)}) collective-permute-start(bf16[2,32,1024]{2,1,0:T(8,128)(2,1)} %bitcast.16), channel_id=1, source_target_pairs={{0,2},{1,3},{2,0},{3,1},{4,6},{5,7},{6,4},{7,5},{8,10},{9,11},{10,... | collective-permute-start | bytes 393224 | tf_op jit(solution)/shard_map/ppermute | solution.py:249
  1.4 3.2 %collective-permute-start.5 = (bf16[2,32,1024]{2,1,0:T(8,128)(2,1)}, bf16[2,32,1024]{2,1,0:T(8,128)(2,1)S(1)}, u32[]{:S(2)}, u32[]{:S(2)}) collective-permute-start(bf16[2,32,1024]{2,1,0:T(8,128)(2,1)} %bitcast.17), channel_id=1, source_target_pairs={{12,0},{8,4},{0,8},{4,12},{28,16},{24,20},{16,24},{20,28},{44,32},... | collective-permute-start | bytes 393224 | tf_op jit(solution)/shard_map/ppermute | solution.py:245
  4.6 0.7 %collective-permute-start.4 = (bf16[2,32,1024]{2,1,0:T(8,128)(2,1)}, bf16[2,32,1024]{2,1,0:T(8,128)(2,1)S(1)}, u32[]{:S(2)}, u32[]{:S(2)}) collective-permute-start(bf16[2,32,1024]{2,1,0:T(8,128)(2,1)} %bitcast.18), channel_id=1, source_target_pairs={{244,0},{0,4},{12,8},{24,12},{4,16},{16,20},{28,24},{40,28},{20,32... | collective-permute-start | bytes 393224 | tf_op jit(solution)/shard_map/ppermute | solution.py:245
  5.3 0.5 %collective-permute-start.3 = (bf16[2,32,1024]{2,1,0:T(8,128)(2,1)}, bf16[2,32,1024]{2,1,0:T(8,128)(2,1)S(1)}, u32[]{:S(2)}, u32[]{:S(2)}) collective-permute-start(bf16[2,32,1024]{2,1,0:T(8,128)(2,1)} %bitcast.19), channel_id=1, source_target_pairs={{248,0},{252,4},{20,8},{16,12},{8,16},{12,20},{36,24},{32,28},{24,... | collective-permute-start | bytes 393224 | tf_op jit(solution)/shard_map/ppermute | solution.py:245
  5.7 0.0 collective-permute-start.1
  5.8 0.0 copy-start.1
  5.8 0.1 pad_add_fusion.spot
  5.8 0.0 copy-start.2
  5.8 0.6 %copy-done.1 = s32[64,3]{0,1:T(4,128)S(1)} copy-done((s32[64,3]{0,1:T(4,128)S(1)}, s32[64,3]{0,1:T(4,128)}, u32[]{:S(2)}) %copy-start.1) | copy-done | bytes 792
  6.4 0.1 copy-done.2
  6.5 0.7 %shard_map.38 = (f32[3,8,32,128]{3,2,1,0:T(8,128)S(1)}, f32[10,1,128]{2,1,0:T(1,128)S(1)}) custom-call(s32[3,64]{1,0:T(4,128)S(1)} %bitcast.22, s32[64]{0:T(128)S(1)} %copy-done.2, s32[2]{0:T(128)S(1)} %pad_add_fusion.spot), custom_call_target="tpu_custom_call" | custom-call | flops 100000000 | bytes 100000 | tf_op jit(solution)/shard_map/pallas_call | solution.py:129
  7.2 0.0 copy-start
  7.2 0.0 collective-permute-done.refs_1_
  7.2 0.6 %collective-permute-start.2 = (bf16[2,32,1024]{2,1,0:T(8,128)(2,1)S(1)}, bf16[2,32,1024]{2,1,0:T(8,128)(2,1)S(1)}, u32[]{:S(2)}, u32[]{:S(2)}) collective-permute-start(bf16[2,32,1024]{2,1,0:T(8,128)(2,1)S(1)} %collective-permute-done.refs_1_), channel_id=1, source_target_pairs={{0,1},{1,0},{2,3},{3,2},{4,5},{5,4},{6,7},{7,6},{8,9},{9,8},{10,11... | collective-permute-start | bytes 393224 | tf_op jit(solution)/shard_map/ppermute | solution.py:249
  7.8 0.6 %shard_map.37 = (bf16[2,256,256]{2,1,0:T(8,128)(2,1)S(1)}, bf16[2,256,256]{2,1,0:T(8,128)(2,1)S(1)}, bf16[8,256,256]{2,1,0:T(8,128)(2,1)S(1)}, bf16[8,256,256]{2,1,0:T(8,128)(2,1)S(1)}) custom-call(), custom_call_target="tpu_custom_call" | custom-call | flops 2000000000 | bytes 3000000 | tf_op jit(solution)/shard_map/pallas_call | solution.py:122
  8.4 0.4 %collective-permute-done.5.refs_6_ = bf16[2,32,1024]{2,1,0:T(8,128)(2,1)S(1)} collective-permute-done((bf16[2,32,1024]{2,1,0:T(8,128)(2,1)}, bf16[2,32,1024]{2,1,0:T(8,128)(2,1)S(1)}, u32[]{:S(2)}, u32[]{:S(2)}) %collective-permute-start.5) | collective-permute-done | bytes 131104 | tf_op jit(solution)/shard_map/ppermute | solution.py:245
  8.8 4.4 %collective-permute-done.4.refs_5_ = bf16[2,32,1024]{2,1,0:T(8,128)(2,1)S(1)} collective-permute-done((bf16[2,32,1024]{2,1,0:T(8,128)(2,1)}, bf16[2,32,1024]{2,1,0:T(8,128)(2,1)S(1)}, u32[]{:S(2)}, u32[]{:S(2)}) %collective-permute-start.4) | collective-permute-done | bytes 131104 | tf_op jit(solution)/shard_map/ppermute | solution.py:245
  13.2 2.2 %collective-permute-done.3.refs_4_ = bf16[2,32,1024]{2,1,0:T(8,128)(2,1)S(1)} collective-permute-done((bf16[2,32,1024]{2,1,0:T(8,128)(2,1)}, bf16[2,32,1024]{2,1,0:T(8,128)(2,1)S(1)}, u32[]{:S(2)}, u32[]{:S(2)}) %collective-permute-start.3) | collective-permute-done | bytes 131104 | tf_op jit(solution)/shard_map/ppermute | solution.py:245
  15.5 0.0 collective-permute-done.1.refs_2_
  15.5 0.0 collective-permute-done.2.refs_3_
  15.5 0.0 copy-done
  15.5 3.5 %shard_map.39 = (bf16[2,32,1024]{2,1,0:T(8,128)(2,1)S(1)}, bf16[2,32,1024]{2,1,0:T(8,128)(2,1)S(1)}, bf16[2,32,1024]{2,1,0:T(8,128)(2,1)S(1)}, f32[2,32,1024]{2,...) custom-call(bf16[2,32,1024]{2,1,0:T(8,128)(2,1)S(1)} %bitcast.21, ...), custom_call_target="tpu_custom_call" | custom-call | flops 6000000000 | bytes 6000000 | tf_op jit(solution)/shard_map/pallas_call | solution.py:225
  19.1 0.1 collective-permute-start.6
  19.2 4.1 %collective-permute-start.8 = (bf16[2,32,1024]{2,1,0:T(8,128)(2,1)S(1)}, bf16[2,32,1024]{2,1,0:T(8,128)(2,1)S(1)}, u32[]{:S(2)}, u32[]{:S(2)}) collective-permute-start(bf16[2,32,1024]{2,1,0:T(8,128)(2,1)S(1)} %get-tuple-element.26), channel_id=1, source_target_pairs={{0,248},{4,252},{8,20},{12,16},{16,8},{20,12},{24,36},{28,32},{32,... | collective-permute-start | bytes 393224 | tf_op jit(solution)/shard_map/ppermute | solution.py:245
  23.3 0.0 collective-permute-start.9
  23.3 2.5 %collective-permute-start.10 = (bf16[2,32,1024]{2,1,0:T(8,128)(2,1)S(1)}, bf16[2,32,1024]{2,1,0:T(8,128)(2,1)S(1)}, u32[]{:S(2)}, u32[]{:S(2)}) collective-permute-start(bf16[2,32,1024]{2,1,0:T(8,128)(2,1)S(1)} %get-tuple-element.28), channel_id=1, source_target_pairs={{0,244},{4,0},{8,12},{12,24},{16,4},{20,16},{24,28},{28,40},{32,20... | collective-permute-start | bytes 393224 | tf_op jit(solution)/shard_map/ppermute | solution.py:245
  25.8 0.0 collective-permute-done.6
  25.8 2.4 %collective-permute-start.7 = (bf16[2,32,1024]{2,1,0:T(8,128)(2,1)S(1)}, bf16[2,32,1024]{2,1,0:T(8,128)(2,1)S(1)}, u32[]{:S(2)}, u32[]{:S(2)}) collective-permute-start(bf16[2,32,1024]{2,1,0:T(8,128)(2,1)S(1)} %fusion), channel_id=1, source_target_pairs={{0,2},{1,3},{2,0},{3,1},{4,6},{5,7},{6,4},{7,5},{8,10},{9,11},{10,... | collective-permute-start | bytes 393224 | tf_op jit(solution)/shard_map/ppermute | solution.py:249
  28.2 0.0 collective-permute-done.8
  28.2 2.9 %collective-permute-done.9 = bf16[2,32,1024]{2,1,0:T(8,128)(2,1)S(1)} collective-permute-done((bf16[2,32,1024]{2,1,0:T(8,128)(2,1)S(1)}, bf16[2,32,1024]{2,1,0:T(8,128)(2,1)S(1)}, u32[]{:S(2)}, u32[]{:S(2)}) %collective-permute-start.9) | collective-permute-done | bytes 131104 | tf_op jit(solution)/shard_map/ppermute | solution.py:245
  31.1 0.0 collective-permute-done.10
  31.1 3.7 %collective-permute-done.7 = bf16[2,32,1024]{2,1,0:T(8,128)(2,1)S(1)} collective-permute-done((bf16[2,32,1024]{2,1,0:T(8,128)(2,1)S(1)}, bf16[2,32,1024]{2,1,0:T(8,128)(2,1)S(1)}, u32[]{:S(2)}, u32[]{:S(2)}) %collective-permute-start.7) | collective-permute-done | bytes 131104 | tf_op jit(solution)/shard_map/ppermute | solution.py:249
  34.8 0.8 %fusion.5 = f32[1,1,2,32,1024]{4,3,2,1,0:T(8,128)} fusion(f32[2,32,1024]{2,1,0:T(8,128)S(1)} %get-tuple-element.23, bf16[2,32,1024]{2,1,0:T(8,128)(2,1)S(1)} %collective-permute-done.10, bf16[2,32,1024]{2,1,0:T(8,128)(2,1)S(1)} %collective-permute-done.9, bf16[2,32,1024]{2,1,0:T(8,128)(2,1)S(1)} %collective-permute-done.8, ...), kind=kLoop, calls=%fused_computation.7 | loop fusion | flops 655360 | bytes 1179648 | tf_op jit(solution)/shard_map/broadcast_in_dim | solution.py:265
  (1 shorter events, 0.0 us)
Async XLA Ops:
  0.0 7.2 %collective-permute-start = (bf16[2,32,1024]{2,1,0:T(8,128)(2,1)}, bf16[2,32,1024]{2,1,0:T(8,128)(2,1)S(1)}, u32[]{:S(2)}, u32[]{:S(2)}) collective-permute-start(bf16[2,32,1024]{2,1,0:T(8,128)(2,1)} %bitcast.16), channel_id=1, source_target_pairs={{0,2},{1,3},{2,0},{3,1},{4,6},{5,7},{6,4},{7,5},{8,10},{9,11},{10,... | collective-permute-start | bytes 393224 | tf_op jit(solution)/shard_map/ppermute | solution.py:249
  1.4 7.4 %collective-permute-start.5 = (bf16[2,32,1024]{2,1,0:T(8,128)(2,1)}, bf16[2,32,1024]{2,1,0:T(8,128)(2,1)S(1)}, u32[]{:S(2)}, u32[]{:S(2)}) collective-permute-start(bf16[2,32,1024]{2,1,0:T(8,128)(2,1)} %bitcast.17), channel_id=1, source_target_pairs={{12,0},{8,4},{0,8},{4,12},{28,16},{24,20},{16,24},{20,28},{44,32},... | collective-permute-start | bytes 393224 | tf_op jit(solution)/shard_map/ppermute | solution.py:245
  4.6 8.6 %collective-permute-start.4 = (bf16[2,32,1024]{2,1,0:T(8,128)(2,1)}, bf16[2,32,1024]{2,1,0:T(8,128)(2,1)S(1)}, u32[]{:S(2)}, u32[]{:S(2)}) collective-permute-start(bf16[2,32,1024]{2,1,0:T(8,128)(2,1)} %bitcast.18), channel_id=1, source_target_pairs={{244,0},{0,4},{12,8},{24,12},{4,16},{16,20},{28,24},{40,28},{20,32... | collective-permute-start | bytes 393224 | tf_op jit(solution)/shard_map/ppermute | solution.py:245
  5.3 10.2 %collective-permute-start.3 = (bf16[2,32,1024]{2,1,0:T(8,128)(2,1)}, bf16[2,32,1024]{2,1,0:T(8,128)(2,1)S(1)}, u32[]{:S(2)}, u32[]{:S(2)}) collective-permute-start(bf16[2,32,1024]{2,1,0:T(8,128)(2,1)} %bitcast.19), channel_id=1, source_target_pairs={{248,0},{252,4},{20,8},{16,12},{8,16},{12,20},{36,24},{32,28},{24,... | collective-permute-start | bytes 393224 | tf_op jit(solution)/shard_map/ppermute | solution.py:245
  5.7 9.7 %collective-permute-start.1 = (bf16[2,32,1024]{2,1,0:T(8,128)(2,1)}, bf16[2,32,1024]{2,1,0:T(8,128)(2,1)S(1)}, u32[]{:S(2)}, u32[]{:S(2)}) collective-permute-start(bf16[2,32,1024]{2,1,0:T(8,128)(2,1)} %bitcast.20), channel_id=1, source_target_pairs={{0,1},{1,0},{2,3},{3,2},{4,5},{5,4},{6,7},{7,6},{8,9},{9,8},{10,11... | collective-permute-start | bytes 393224 | tf_op jit(solution)/shard_map/ppermute | solution.py:249
  5.8 0.7 %copy-start.1 = (s32[64,3]{0,1:T(4,128)S(1)}, s32[64,3]{0,1:T(4,128)}, u32[]{:S(2)}) copy-start(s32[64,3]{0,1:T(4,128)} %param.4) | copy-start | bytes 2308
  5.8 0.7 %copy-start.2 = (s32[64]{0:T(128)S(1)}, s32[64]{0:T(128)}, u32[]{:S(2)}) copy-start(s32[64]{0:T(128)} %occupied.1) | copy-start | bytes 772
  7.2 8.3 %copy-start = (bf16[1,1,2,32,1024]{4,3,2,1,0:T(8,128)(2,1)S(1)}, bf16[1,1,2,32,1024]{4,3,2,1,0:T(8,128)(2,1)}, u32[]{:S(2)}) copy-start(bf16[1,1,2,32,1024]{4,3,2,1,0:T(8,128)(2,1)} %param.3) | copy-start | bytes 393220
  7.2 8.3 %collective-permute-start.2 = (bf16[2,32,1024]{2,1,0:T(8,128)(2,1)S(1)}, bf16[2,32,1024]{2,1,0:T(8,128)(2,1)S(1)}, u32[]{:S(2)}, u32[]{:S(2)}) collective-permute-start(bf16[2,32,1024]{2,1,0:T(8,128)(2,1)S(1)} %collective-permute-done.refs_1_), channel_id=1, source_target_pairs={{0,1},{1,0},{2,3},{3,2},{4,5},{5,4},{6,7},{7,6},{8,9},{9,8},{10,11... | collective-permute-start | bytes 393224 | tf_op jit(solution)/shard_map/ppermute | solution.py:249
  19.1 6.8 %collective-permute-start.6 = (bf16[2,2,32,1024]{3,2,1,0:T(8,128)(2,1)S(1)}, bf16[2,2,32,1024]{3,2,1,0:T(8,128)(2,1)S(1)}, u32[]{:S(2)}, u32[]{:S(2)}) collective-permute-start(bf16[2,2,32,1024]{3,2,1,0:T(8,128)(2,1)S(1)} %get-tuple-element.24), channel_id=1, source_target_pairs={{0,1},{1,0},{2,3},{3,2},{4,5},{5,4},{6,7},{7,6},{8,9},{9,8},{10,11... | collective-permute-start | bytes 786440 | tf_op jit(solution)/shard_map/ppermute | solution.py:249
  19.2 9.1 %collective-permute-start.8 = (bf16[2,32,1024]{2,1,0:T(8,128)(2,1)S(1)}, bf16[2,32,1024]{2,1,0:T(8,128)(2,1)S(1)}, u32[]{:S(2)}, u32[]{:S(2)}) collective-permute-start(bf16[2,32,1024]{2,1,0:T(8,128)(2,1)S(1)} %get-tuple-element.26), channel_id=1, source_target_pairs={{0,248},{4,252},{8,20},{12,16},{16,8},{20,12},{24,36},{28,32},{32,... | collective-permute-start | bytes 393224 | tf_op jit(solution)/shard_map/ppermute | solution.py:245
  23.3 7.8 %collective-permute-start.9 = (bf16[2,32,1024]{2,1,0:T(8,128)(2,1)S(1)}, bf16[2,32,1024]{2,1,0:T(8,128)(2,1)S(1)}, u32[]{:S(2)}, u32[]{:S(2)}) collective-permute-start(bf16[2,32,1024]{2,1,0:T(8,128)(2,1)S(1)} %get-tuple-element.27), channel_id=1, source_target_pairs={{0,12},{4,8},{8,0},{12,4},{16,28},{20,24},{24,16},{28,20},{32,44},... | collective-permute-start | bytes 393224 | tf_op jit(solution)/shard_map/ppermute | solution.py:245
  23.3 7.8 %collective-permute-start.10 = (bf16[2,32,1024]{2,1,0:T(8,128)(2,1)S(1)}, bf16[2,32,1024]{2,1,0:T(8,128)(2,1)S(1)}, u32[]{:S(2)}, u32[]{:S(2)}) collective-permute-start(bf16[2,32,1024]{2,1,0:T(8,128)(2,1)S(1)} %get-tuple-element.28), channel_id=1, source_target_pairs={{0,244},{4,0},{8,12},{12,24},{16,4},{20,16},{24,28},{28,40},{32,20... | collective-permute-start | bytes 393224 | tf_op jit(solution)/shard_map/ppermute | solution.py:245
  25.8 9.0 %collective-permute-start.7 = (bf16[2,32,1024]{2,1,0:T(8,128)(2,1)S(1)}, bf16[2,32,1024]{2,1,0:T(8,128)(2,1)S(1)}, u32[]{:S(2)}, u32[]{:S(2)}) collective-permute-start(bf16[2,32,1024]{2,1,0:T(8,128)(2,1)S(1)} %fusion), channel_id=1, source_target_pairs={{0,2},{1,3},{2,0},{3,1},{4,6},{5,7},{6,4},{7,5},{8,10},{9,11},{10,... | collective-permute-start | bytes 393224 | tf_op jit(solution)/shard_map/ppermute | solution.py:249

commit v6 on v5

--- a/solution.py
+++ b/solution.py
@@ -174,15 +174,14 @@
                     mid[e, rows(2 * job + i), block(c)] = plus[rows(4 * c + e), block(i)]
                     mid[e + 4, rows(2 * job + i), block(c)] = minus[rows(4 * c + e), block(i)]
 
+    for k1 in range(8):
+        factor = []
+        for m in range(len(SHIFTS)):
+            factor += [jnp.concatenate([screened[m, k1]] * 2, axis=1)] * BANDS
+        factor = jnp.concatenate(factor, axis=0)
+        mid[k1] = (dot(mid[k1], forward_yz[k1]) * factor).astype(jnp.bfloat16)
     for e in range(4):
-        halves = []
-        for k1 in (e, e + 4):
-            third = dot(mid[k1], forward_yz[k1])
-            factor = []
-            for m in range(len(SHIFTS)):
-                factor += [jnp.concatenate([screened[m, k1]] * 2, axis=1)] * BANDS
-            factor = jnp.concatenate(factor, axis=0)
-            halves.append(dot((third * factor).astype(jnp.bfloat16), inverse_yz[k1]))
+        halves = [dot(mid[k1], inverse_yz[k1]) for k1 in (e, e + 4)]
         for b in range(2):
             joined = (halves[0] - halves[1] if b else halves[0] + halves[1]).astype(jnp.bfloat16)
             for job in range(2 * len(SHIFTS)):

time: 35.7 us -> 35.6 us (level)
  no operation moved by 1% of the time
where the time goes in v6:
time: 35.6 us; the launch traced here: 35.5 us
  starting transfers between devices  15.5 us (44%)
  waiting for transfers between devices  13.7 us (38%)
  Pallas kernels  4.77 us (13%)
  other arithmetic  0.9 us (3%)
  local copies, waits for them, and re-layouts  0.66 us (2%)
    ppermute x6, starting transfers between devices, passed_along(): return lax.ppermute(value, 'ka', pairs)  11 us
    ppermute x6, waiting for transfers between devices, passed_along(): return lax.ppermute(value, 'ka', pairs)  9.96 us
    ppermute x5, starting transfers between devices, swapped(): lax.ppermute(value, 'ba', [(i, i ^ flip) for i in range(lax.axis_size('ba...  4.49 us
    ppermute x5, waiting for transfers between devices, swapped(): lax.ppermute(value, 'ba', [(i, i ^ flip) for i in range(lax.axis_size('ba...  3.71 us
    pallas_call x1, Pallas kernels, pair_terms(): pl.pallas_call(pair_kernel, out_shape=out_shape, in_specs=[vmem] * len(op...  3.47 us
    broadcast_in_dim x1, other arithmetic, on_device(): return total[None, None]  0.8 us
  transfers between devices with their start and end apart: 11, of which 5 were waited for; matrix products, arithmetic and copies ran while one was open for 0% of the time, Pallas kernels for 4%

profile of v6, /device:TPU:6, one launch (start us, length us, event | category | flops | bytes accessed | tf_op | source)
XLA Modules:
  0.0 35.5 jit_solution(14548753394993867053)
XLA Ops:
  0.0 1.4 %collective-permute-start = (bf16[2,32,1024]{2,1,0:T(8,128)(2,1)}, bf16[2,32,1024]{2,1,0:T(8,128)(2,1)S(1)}, u32[]{:S(2)}, u32[]{:S(2)}) collective-permute-start(bf16[2,32,1024]{2,1,0:T(8,128)(2,1)} %bitcast.16), channel_id=1, source_target_pairs={{0,2},{1,3},{2,0},{3,1},{4,6},{5,7},{6,4},{7,5},{8,10},{9,11},{10,... | collective-permute-start | bytes 393224 | tf_op jit(solution)/shard_map/ppermute | solution.py:248
  1.4 3.2 %collective-permute-start.5 = (bf16[2,32,1024]{2,1,0:T(8,128)(2,1)}, bf16[2,32,1024]{2,1,0:T(8,128)(2,1)S(1)}, u32[]{:S(2)}, u32[]{:S(2)}) collective-permute-start(bf16[2,32,1024]{2,1,0:T(8,128)(2,1)} %bitcast.17), channel_id=1, source_target_pairs={{12,0},{8,4},{0,8},{4,12},{28,16},{24,20},{16,24},{20,28},{44,32},... | collective-permute-start | bytes 393224 | tf_op jit(solution)/shard_map/ppermute | solution.py:244
  4.6 0.7 %collective-permute-start.4 = (bf16[2,32,1024]{2,1,0:T(8,128)(2,1)}, bf16[2,32,1024]{2,1,0:T(8,128)(2,1)S(1)}, u32[]{:S(2)}, u32[]{:S(2)}) collective-permute-start(bf16[2,32,1024]{2,1,0:T(8,128)(2,1)} %bitcast.18), channel_id=1, source_target_pairs={{244,0},{0,4},{12,8},{24,12},{4,16},{16,20},{28,24},{40,28},{20,32... | collective-permute-start | bytes 393224 | tf_op jit(solution)/shard_map/ppermute | solution.py:244
  5.3 0.5 %collective-permute-start.3 = (bf16[2,32,1024]{2,1,0:T(8,128)(2,1)}, bf16[2,32,1024]{2,1,0:T(8,128)(2,1)S(1)}, u32[]{:S(2)}, u32[]{:S(2)}) collective-permute-start(bf16[2,32,1024]{2,1,0:T(8,128)(2,1)} %bitcast.19), channel_id=1, source_target_pairs={{248,0},{252,4},{20,8},{16,12},{8,16},{12,20},{36,24},{32,28},{24,... | collective-permute-start | bytes 393224 | tf_op jit(solution)/shard_map/ppermute | solution.py:244
  5.7 0.0 collective-permute-start.1
  5.8 0.0 copy-start.1
  5.8 0.1 pad_add_fusion.spot
  5.8 0.0 copy-start.2
  5.8 0.6 %copy-done.1 = s32[64,3]{0,1:T(4,128)S(1)} copy-done((s32[64,3]{0,1:T(4,128)S(1)}, s32[64,3]{0,1:T(4,128)}, u32[]{:S(2)}) %copy-start.1) | copy-done | bytes 792
  6.4 0.1 copy-done.2
  6.5 0.7 %shard_map.38 = (f32[3,8,32,128]{3,2,1,0:T(8,128)S(1)}, f32[10,1,128]{2,1,0:T(1,128)S(1)}) custom-call(s32[3,64]{1,0:T(4,128)S(1)} %bitcast.22, s32[64]{0:T(128)S(1)} %copy-done.2, s32[2]{0:T(128)S(1)} %pad_add_fusion.spot), custom_call_target="tpu_custom_call" | custom-call | flops 100000000 | bytes 100000 | tf_op jit(solution)/shard_map/pallas_call | solution.py:129
  7.2 0.0 copy-start
  7.2 0.0 collective-permute-done.refs_1_
  7.2 0.6 %collective-permute-start.2 = (bf16[2,32,1024]{2,1,0:T(8,128)(2,1)S(1)}, bf16[2,32,1024]{2,1,0:T(8,128)(2,1)S(1)}, u32[]{:S(2)}, u32[]{:S(2)}) collective-permute-start(bf16[2,32,1024]{2,1,0:T(8,128)(2,1)S(1)} %collective-permute-done.refs_1_), channel_id=1, source_target_pairs={{0,1},{1,0},{2,3},{3,2},{4,5},{5,4},{6,7},{7,6},{8,9},{9,8},{10,11... | collective-permute-start | bytes 393224 | tf_op jit(solution)/shard_map/ppermute | solution.py:248
  7.8 0.6 %shard_map.37 = (bf16[2,256,256]{2,1,0:T(8,128)(2,1)S(1)}, bf16[2,256,256]{2,1,0:T(8,128)(2,1)S(1)}, bf16[8,256,256]{2,1,0:T(8,128)(2,1)S(1)}, bf16[8,256,256]{2,1,0:T(8,128)(2,1)S(1)}) custom-call(), custom_call_target="tpu_custom_call" | custom-call | flops 2000000000 | bytes 3000000 | tf_op jit(solution)/shard_map/pallas_call | solution.py:122
  8.4 0.4 %collective-permute-done.5.refs_6_ = bf16[2,32,1024]{2,1,0:T(8,128)(2,1)S(1)} collective-permute-done((bf16[2,32,1024]{2,1,0:T(8,128)(2,1)}, bf16[2,32,1024]{2,1,0:T(8,128)(2,1)S(1)}, u32[]{:S(2)}, u32[]{:S(2)}) %collective-permute-start.5) | collective-permute-done | bytes 131104 | tf_op jit(solution)/shard_map/ppermute | solution.py:244
  8.8 4.4 %collective-permute-done.4.refs_5_ = bf16[2,32,1024]{2,1,0:T(8,128)(2,1)S(1)} collective-permute-done((bf16[2,32,1024]{2,1,0:T(8,128)(2,1)}, bf16[2,32,1024]{2,1,0:T(8,128)(2,1)S(1)}, u32[]{:S(2)}, u32[]{:S(2)}) %collective-permute-start.4) | collective-permute-done | bytes 131104 | tf_op jit(solution)/shard_map/ppermute | solution.py:244
  13.2 2.2 %collective-permute-done.3.refs_4_ = bf16[2,32,1024]{2,1,0:T(8,128)(2,1)S(1)} collective-permute-done((bf16[2,32,1024]{2,1,0:T(8,128)(2,1)}, bf16[2,32,1024]{2,1,0:T(8,128)(2,1)S(1)}, u32[]{:S(2)}, u32[]{:S(2)}) %collective-permute-start.3) | collective-permute-done | bytes 131104 | tf_op jit(solution)/shard_map/ppermute | solution.py:244
  15.5 0.0 collective-permute-done.1.refs_2_
  15.5 0.0 collective-permute-done.2.refs_3_
  15.5 0.0 copy-done
  15.5 3.5 %shard_map.39 = (bf16[2,32,1024]{2,1,0:T(8,128)(2,1)S(1)}, bf16[2,32,1024]{2,1,0:T(8,128)(2,1)S(1)}, bf16[2,32,1024]{2,1,0:T(8,128)(2,1)S(1)}, f32[2,32,1024]{2,...) custom-call(bf16[2,32,1024]{2,1,0:T(8,128)(2,1)S(1)} %bitcast.21, ...), custom_call_target="tpu_custom_call" | custom-call | flops 6000000000 | bytes 6000000 | tf_op jit(solution)/shard_map/pallas_call | solution.py:224
  19.0 0.1 collective-permute-start.6
  19.1 4.1 %collective-permute-start.8 = (bf16[2,32,1024]{2,1,0:T(8,128)(2,1)S(1)}, bf16[2,32,1024]{2,1,0:T(8,128)(2,1)S(1)}, u32[]{:S(2)}, u32[]{:S(2)}) collective-permute-start(bf16[2,32,1024]{2,1,0:T(8,128)(2,1)S(1)} %get-tuple-element.26), channel_id=1, source_target_pairs={{0,248},{4,252},{8,20},{12,16},{16,8},{20,12},{24,36},{28,32},{32,... | collective-permute-start | bytes 393224 | tf_op jit(solution)/shard_map/ppermute | solution.py:244
  23.2 0.0 collective-permute-start.9
  23.2 2.5 %collective-permute-start.10 = (bf16[2,32,1024]{2,1,0:T(8,128)(2,1)S(1)}, bf16[2,32,1024]{2,1,0:T(8,128)(2,1)S(1)}, u32[]{:S(2)}, u32[]{:S(2)}) collective-permute-start(bf16[2,32,1024]{2,1,0:T(8,128)(2,1)S(1)} %get-tuple-element.28), channel_id=1, source_target_pairs={{0,244},{4,0},{8,12},{12,24},{16,4},{20,16},{24,28},{28,40},{32,20... | collective-permute-start | bytes 393224 | tf_op jit(solution)/shard_map/ppermute | solution.py:244
  25.7 0.0 collective-permute-done.6
  25.8 2.4 %collective-permute-start.7 = (bf16[2,32,1024]{2,1,0:T(8,128)(2,1)S(1)}, bf16[2,32,1024]{2,1,0:T(8,128)(2,1)S(1)}, u32[]{:S(2)}, u32[]{:S(2)}) collective-permute-start(bf16[2,32,1024]{2,1,0:T(8,128)(2,1)S(1)} %fusion), channel_id=1, source_target_pairs={{0,2},{1,3},{2,0},{3,1},{4,6},{5,7},{6,4},{7,5},{8,10},{9,11},{10,... | collective-permute-start | bytes 393224 | tf_op jit(solution)/shard_map/ppermute | solution.py:248
  28.2 0.0 collective-permute-done.8
  28.2 2.9 %collective-permute-done.9 = bf16[2,32,1024]{2,1,0:T(8,128)(2,1)S(1)} collective-permute-done((bf16[2,32,1024]{2,1,0:T(8,128)(2,1)S(1)}, bf16[2,32,1024]{2,1,0:T(8,128)(2,1)S(1)}, u32[]{:S(2)}, u32[]{:S(2)}) %collective-permute-start.9) | collective-permute-done | bytes 131104 | tf_op jit(solution)/shard_map/ppermute | solution.py:244
  31.0 0.0 collective-permute-done.10
  31.0 3.7 %collective-permute-done.7 = bf16[2,32,1024]{2,1,0:T(8,128)(2,1)S(1)} collective-permute-done((bf16[2,32,1024]{2,1,0:T(8,128)(2,1)S(1)}, bf16[2,32,1024]{2,1,0:T(8,128)(2,1)S(1)}, u32[]{:S(2)}, u32[]{:S(2)}) %collective-permute-start.7) | collective-permute-done | bytes 131104 | tf_op jit(solution)/shard_map/ppermute | solution.py:248
  34.7 0.8 %fusion.5 = f32[1,1,2,32,1024]{4,3,2,1,0:T(8,128)} fusion(f32[2,32,1024]{2,1,0:T(8,128)S(1)} %get-tuple-element.23, bf16[2,32,1024]{2,1,0:T(8,128)(2,1)S(1)} %collective-permute-done.10, bf16[2,32,1024]{2,1,0:T(8,128)(2,1)S(1)} %collective-permute-done.9, bf16[2,32,1024]{2,1,0:T(8,128)(2,1)S(1)} %collective-permute-done.8, ...), kind=kLoop, calls=%fused_computation.7 | loop fusion | flops 655360 | bytes 1179648 | tf_op jit(solution)/shard_map/broadcast_in_dim | solution.py:264
  (1 shorter events, 0.0 us)
Async XLA Ops:
  0.0 7.2 %collective-permute-start = (bf16[2,32,1024]{2,1,0:T(8,128)(2,1)}, bf16[2,32,1024]{2,1,0:T(8,128)(2,1)S(1)}, u32[]{:S(2)}, u32[]{:S(2)}) collective-permute-start(bf16[2,32,1024]{2,1,0:T(8,128)(2,1)} %bitcast.16), channel_id=1, source_target_pairs={{0,2},{1,3},{2,0},{3,1},{4,6},{5,7},{6,4},{7,5},{8,10},{9,11},{10,... | collective-permute-start | bytes 393224 | tf_op jit(solution)/shard_map/ppermute | solution.py:248
  1.4 7.4 %collective-permute-start.5 = (bf16[2,32,1024]{2,1,0:T(8,128)(2,1)}, bf16[2,32,1024]{2,1,0:T(8,128)(2,1)S(1)}, u32[]{:S(2)}, u32[]{:S(2)}) collective-permute-start(bf16[2,32,1024]{2,1,0:T(8,128)(2,1)} %bitcast.17), channel_id=1, source_target_pairs={{12,0},{8,4},{0,8},{4,12},{28,16},{24,20},{16,24},{20,28},{44,32},... | collective-permute-start | bytes 393224 | tf_op jit(solution)/shard_map/ppermute | solution.py:244
  4.6 8.6 %collective-permute-start.4 = (bf16[2,32,1024]{2,1,0:T(8,128)(2,1)}, bf16[2,32,1024]{2,1,0:T(8,128)(2,1)S(1)}, u32[]{:S(2)}, u32[]{:S(2)}) collective-permute-start(bf16[2,32,1024]{2,1,0:T(8,128)(2,1)} %bitcast.18), channel_id=1, source_target_pairs={{244,0},{0,4},{12,8},{24,12},{4,16},{16,20},{28,24},{40,28},{20,32... | collective-permute-start | bytes 393224 | tf_op jit(solution)/shard_map/ppermute | solution.py:244
  5.3 10.2 %collective-permute-start.3 = (bf16[2,32,1024]{2,1,0:T(8,128)(2,1)}, bf16[2,32,1024]{2,1,0:T(8,128)(2,1)S(1)}, u32[]{:S(2)}, u32[]{:S(2)}) collective-permute-start(bf16[2,32,1024]{2,1,0:T(8,128)(2,1)} %bitcast.19), channel_id=1, source_target_pairs={{248,0},{252,4},{20,8},{16,12},{8,16},{12,20},{36,24},{32,28},{24,... | collective-permute-start | bytes 393224 | tf_op jit(solution)/shard_map/ppermute | solution.py:244
  5.7 9.7 %collective-permute-start.1 = (bf16[2,32,1024]{2,1,0:T(8,128)(2,1)}, bf16[2,32,1024]{2,1,0:T(8,128)(2,1)S(1)}, u32[]{:S(2)}, u32[]{:S(2)}) collective-permute-start(bf16[2,32,1024]{2,1,0:T(8,128)(2,1)} %bitcast.20), channel_id=1, source_target_pairs={{0,1},{1,0},{2,3},{3,2},{4,5},{5,4},{6,7},{7,6},{8,9},{9,8},{10,11... | collective-permute-start | bytes 393224 | tf_op jit(solution)/shard_map/ppermute | solution.py:248
  5.8 0.7 %copy-start.1 = (s32[64,3]{0,1:T(4,128)S(1)}, s32[64,3]{0,1:T(4,128)}, u32[]{:S(2)}) copy-start(s32[64,3]{0,1:T(4,128)} %param.4) | copy-start | bytes 2308
  5.8 0.7 %copy-start.2 = (s32[64]{0:T(128)S(1)}, s32[64]{0:T(128)}, u32[]{:S(2)}) copy-start(s32[64]{0:T(128)} %occupied.1) | copy-start | bytes 772
  7.2 8.3 %copy-start = (bf16[1,1,2,32,1024]{4,3,2,1,0:T(8,128)(2,1)S(1)}, bf16[1,1,2,32,1024]{4,3,2,1,0:T(8,128)(2,1)}, u32[]{:S(2)}) copy-start(bf16[1,1,2,32,1024]{4,3,2,1,0:T(8,128)(2,1)} %param.3) | copy-start | bytes 393220
  7.2 8.3 %collective-permute-start.2 = (bf16[2,32,1024]{2,1,0:T(8,128)(2,1)S(1)}, bf16[2,32,1024]{2,1,0:T(8,128)(2,1)S(1)}, u32[]{:S(2)}, u32[]{:S(2)}) collective-permute-start(bf16[2,32,1024]{2,1,0:T(8,128)(2,1)S(1)} %collective-permute-done.refs_1_), channel_id=1, source_target_pairs={{0,1},{1,0},{2,3},{3,2},{4,5},{5,4},{6,7},{7,6},{8,9},{9,8},{10,11... | collective-permute-start | bytes 393224 | tf_op jit(solution)/shard_map/ppermute | solution.py:248
  19.0 6.8 %collective-permute-start.6 = (bf16[2,2,32,1024]{3,2,1,0:T(8,128)(2,1)S(1)}, bf16[2,2,32,1024]{3,2,1,0:T(8,128)(2,1)S(1)}, u32[]{:S(2)}, u32[]{:S(2)}) collective-permute-start(bf16[2,2,32,1024]{3,2,1,0:T(8,128)(2,1)S(1)} %get-tuple-element.24), channel_id=1, source_target_pairs={{0,1},{1,0},{2,3},{3,2},{4,5},{5,4},{6,7},{7,6},{8,9},{9,8},{10,11... | collective-permute-start | bytes 786440 | tf_op jit(solution)/shard_map/ppermute | solution.py:248
  19.1 9.1 %collective-permute-start.8 = (bf16[2,32,1024]{2,1,0:T(8,128)(2,1)S(1)}, bf16[2,32,1024]{2,1,0:T(8,128)(2,1)S(1)}, u32[]{:S(2)}, u32[]{:S(2)}) collective-permute-start(bf16[2,32,1024]{2,1,0:T(8,128)(2,1)S(1)} %get-tuple-element.26), channel_id=1, source_target_pairs={{0,248},{4,252},{8,20},{12,16},{16,8},{20,12},{24,36},{28,32},{32,... | collective-permute-start | bytes 393224 | tf_op jit(solution)/shard_map/ppermute | solution.py:244
  23.2 7.8 %collective-permute-start.9 = (bf16[2,32,1024]{2,1,0:T(8,128)(2,1)S(1)}, bf16[2,32,1024]{2,1,0:T(8,128)(2,1)S(1)}, u32[]{:S(2)}, u32[]{:S(2)}) collective-permute-start(bf16[2,32,1024]{2,1,0:T(8,128)(2,1)S(1)} %get-tuple-element.27), channel_id=1, source_target_pairs={{0,12},{4,8},{8,0},{12,4},{16,28},{20,24},{24,16},{28,20},{32,44},... | collective-permute-start | bytes 393224 | tf_op jit(solution)/shard_map/ppermute | solution.py:244
  23.2 7.8 %collective-permute-start.10 = (bf16[2,32,1024]{2,1,0:T(8,128)(2,1)S(1)}, bf16[2,32,1024]{2,1,0:T(8,128)(2,1)S(1)}, u32[]{:S(2)}, u32[]{:S(2)}) collective-permute-start(bf16[2,32,1024]{2,1,0:T(8,128)(2,1)S(1)} %get-tuple-element.28), channel_id=1, source_target_pairs={{0,244},{4,0},{8,12},{12,24},{16,4},{20,16},{24,28},{28,40},{32,20... | collective-permute-start | bytes 393224 | tf_op jit(solution)/shard_map/ppermute | solution.py:244
  25.8 9.0 %collective-permute-start.7 = (bf16[2,32,1024]{2,1,0:T(8,128)(2,1)S(1)}, bf16[2,32,1024]{2,1,0:T(8,128)(2,1)S(1)}, u32[]{:S(2)}, u32[]{:S(2)}) collective-permute-start(bf16[2,32,1024]{2,1,0:T(8,128)(2,1)S(1)} %fusion), channel_id=1, source_target_pairs={{0,2},{1,3},{2,0},{3,1},{4,6},{5,7},{6,4},{7,5},{8,10},{9,11},{10,... | collective-permute-start | bytes 393224 | tf_op jit(solution)/shard_map/ppermute | solution.py:248

commit v7 on v6

--- a/solution.py
+++ b/solution.py
@@ -124,7 +124,7 @@
         out_shape=[jax.ShapeDtypeStruct((count, 256, 256), jnp.bfloat16) for count in (2, 2, 8, 8)],
         out_specs=[vmem] * 4,
         compiler_params=params,
-        cost_estimate=pl.CostEstimate(flops=2 * 10**9, bytes_accessed=3 * 10**6, transcendentals=0),
+        cost_estimate=pl.CostEstimate(flops=10**8, bytes_accessed=10**5, transcendentals=0),
     )()
     points = pl.pallas_call(
         point_kernel,
@@ -135,7 +135,7 @@
         in_specs=[smem] * 3,
         out_specs=[vmem] * 2,
         compiler_params=params,
-        cost_estimate=pl.CostEstimate(flops=10**8, bytes_accessed=10**5, transcendentals=0),
+        cost_estimate=pl.CostEstimate(flops=2 * 10**9, bytes_accessed=10**5, transcendentals=0),
     )(kpoints, occupied, spot)
     return (*tables, *points)
 
@@ -147,21 +147,19 @@
     sums = [refs[16], refs[17], refs[18].at[0], refs[18].at[1]]
     wide, mid, back = refs[19:]
     signs = [weights[7 + m] for m in range(len(SHIFTS))]
+    short_signs = [sign.astype(jnp.bfloat16) for sign in signs]
 
     for b in range(2):
         for a in range(4):
             cut = block(2 * a + b)
             for n in range(BANDS):
-                band_re = bands[n][0, :, cut].astype(jnp.float32)
-                band_im = bands[n][1, :, cut].astype(jnp.float32)
+                band_re, band_im = bands[n][0, :, cut], bands[n][1, :, cut]
                 for m in range(len(SHIFTS)):
                     job, i = 2 * m + n // 2, n % 2
-                    mate_re = mates[m][0, :, cut].astype(jnp.float32)
-                    mate_im = mates[m][1, :, cut].astype(jnp.float32)
-                    value_re = mate_re * band_re + mate_im * band_im
-                    value_im = (mate_re * band_im - mate_im * band_re) * signs[m]
-                    wide[b, job, rows(a), block(i)] = value_re.astype(jnp.bfloat16)
-                    wide[b, job, rows(4 + a), block(i)] = value_im.astype(jnp.bfloat16)
+                    mate_re, mate_im = mates[m][0, :, cut], mates[m][1, :, cut]
+                    value_im = mate_re * band_im - mate_im * band_re
+                    wide[b, job, rows(a), block(i)] = mate_re * band_re + mate_im * band_im
+                    wide[b, job, rows(4 + a), block(i)] = value_im * short_signs[m]
 
     for job in range(2 * len(SHIFTS)):
         even = dot(forward_x[0], wide[0, job])

time: 35.6 us -> 35.7 us (level)
  waiting for transfers between devices: 13.7 us -> 14.8 us
  starting transfers between devices: 15.5 us -> 14.9 us
  local copies, waits for them, and re-layouts: 0.66 us -> 0.11 us
    ppermute x6, waiting for transfers between devices: 9.96 us -> 10.6 us  [passed_along(): return lax.ppermute(value, 'ka', pairs)]
    unnamed x6, local copies, waits for them, and re-layouts: 0.66 us -> 0.11 us
    ppermute x5, starting transfers between devices: 4.49 us -> 3.95 us  [swapped(): lax.ppermute(value, 'ba', [(i, i ^ flip) for i in range(lax.axis_size('ba...]
    ppermute x5, waiting for transfers between devices: 3.71 us -> 4.21 us  [swapped(): lax.ppermute(value, 'ba', [(i, i ^ flip) for i in range(lax.axis_size('ba...]
  transfers between devices with their start and end apart: 11 -> 11, of which waited for: 5 -> 6; matrix products, arithmetic and copies ran while one was open for 0% -> 0% of each run, Pallas kernels for 4% -> 4%
where the time goes in v7:
time: 35.7 us; the launch traced here: 35.6 us
  starting transfers between devices  14.9 us (42%)
  waiting for transfers between devices  14.8 us (41%)
  Pallas kernels  4.78 us (13%)
  other arithmetic  0.9 us (3%)
    ppermute x6, starting transfers between devices, passed_along(): return lax.ppermute(value, 'ka', pairs)  11 us
    ppermute x6, waiting for transfers between devices, passed_along(): return lax.ppermute(value, 'ka', pairs)  10.6 us
    ppermute x5, waiting for transfers between devices, swapped(): lax.ppermute(value, 'ba', [(i, i ^ flip) for i in range(lax.axis_size('ba...  4.21 us
    ppermute x5, starting transfers between devices, swapped(): lax.ppermute(value, 'ba', [(i, i ^ flip) for i in range(lax.axis_size('ba...  3.95 us
    pallas_call x1, Pallas kernels, pair_terms(): pl.pallas_call(pair_kernel, out_shape=out_shape, in_specs=[vmem] * len(op...  3.48 us
    broadcast_in_dim x1, other arithmetic, on_device(): return total[None, None]  0.8 us
  transfers between devices with their start and end apart: 11, of which 6 were waited for; matrix products, arithmetic and copies ran while one was open for 0% of the time, Pallas kernels for 4%

profile of v7, /device:TPU:6, one launch (start us, length us, event | category | flops | bytes accessed | tf_op | source)
XLA Modules:
  0.0 35.6 jit_solution(3647201701221788634)
XLA Ops:
  0.0 1.4 %collective-permute-start = (bf16[2,32,1024]{2,1,0:T(8,128)(2,1)}, bf16[2,32,1024]{2,1,0:T(8,128)(2,1)S(1)}, u32[]{:S(2)}, u32[]{:S(2)}) collective-permute-start(bf16[2,32,1024]{2,1,0:T(8,128)(2,1)} %bitcast.16), channel_id=1, source_target_pairs={{0,2},{1,3},{2,0},{3,1},{4,6},{5,7},{6,4},{7,5},{8,10},{9,11},{10,... | collective-permute-start | bytes 393224 | tf_op jit(solution)/shard_map/ppermute | solution.py:246
  1.4 3.2 %collective-permute-start.5 = (bf16[2,32,1024]{2,1,0:T(8,128)(2,1)}, bf16[2,32,1024]{2,1,0:T(8,128)(2,1)S(1)}, u32[]{:S(2)}, u32[]{:S(2)}) collective-permute-start(bf16[2,32,1024]{2,1,0:T(8,128)(2,1)} %bitcast.17), channel_id=1, source_target_pairs={{12,0},{8,4},{0,8},{4,12},{28,16},{24,20},{16,24},{20,28},{44,32},... | collective-permute-start | bytes 393224 | tf_op jit(solution)/shard_map/ppermute | solution.py:242
  4.6 0.7 %collective-permute-start.4 = (bf16[2,32,1024]{2,1,0:T(8,128)(2,1)}, bf16[2,32,1024]{2,1,0:T(8,128)(2,1)S(1)}, u32[]{:S(2)}, u32[]{:S(2)}) collective-permute-start(bf16[2,32,1024]{2,1,0:T(8,128)(2,1)} %bitcast.18), channel_id=1, source_target_pairs={{244,0},{0,4},{12,8},{24,12},{4,16},{16,20},{28,24},{40,28},{20,32... | collective-permute-start | bytes 393224 | tf_op jit(solution)/shard_map/ppermute | solution.py:242
  5.3 0.5 %collective-permute-start.3 = (bf16[2,32,1024]{2,1,0:T(8,128)(2,1)}, bf16[2,32,1024]{2,1,0:T(8,128)(2,1)S(1)}, u32[]{:S(2)}, u32[]{:S(2)}) collective-permute-start(bf16[2,32,1024]{2,1,0:T(8,128)(2,1)} %bitcast.19), channel_id=1, source_target_pairs={{248,0},{252,4},{20,8},{16,12},{8,16},{12,20},{36,24},{32,28},{24,... | collective-permute-start | bytes 393224 | tf_op jit(solution)/shard_map/ppermute | solution.py:242
  5.7 0.0 collective-permute-start.1
  5.8 0.6 %shard_map.37 = (bf16[2,256,256]{2,1,0:T(8,128)(2,1)S(1)}, bf16[2,256,256]{2,1,0:T(8,128)(2,1)S(1)}, bf16[8,256,256]{2,1,0:T(8,128)(2,1)S(1)}, bf16[8,256,256]{2,1,0:T(8,128)(2,1)S(1)}) custom-call(), custom_call_target="tpu_custom_call" | custom-call | flops 100000000 | bytes 100000 | tf_op jit(solution)/shard_map/pallas_call | solution.py:122
  6.4 0.0 copy-start.1
  6.4 0.1 pad_add_fusion.spot
  6.5 0.0 copy-start.2
  6.5 0.5 %collective-permute-done.refs_1_ = bf16[2,32,1024]{2,1,0:T(8,128)(2,1)S(1)} collective-permute-done((bf16[2,32,1024]{2,1,0:T(8,128)(2,1)}, bf16[2,32,1024]{2,1,0:T(8,128)(2,1)S(1)}, u32[]{:S(2)}, u32[]{:S(2)}) %collective-permute-start) | collective-permute-done | bytes 131104 | tf_op jit(solution)/shard_map/ppermute | solution.py:246
  7.0 0.1 collective-permute-start.2
  7.0 0.0 copy-done.1
  7.1 0.1 copy-done.2
  7.1 0.0 copy-start
  7.1 0.7 %shard_map.38 = (f32[3,8,32,128]{3,2,1,0:T(8,128)S(1)}, f32[10,1,128]{2,1,0:T(1,128)S(1)}) custom-call(s32[3,64]{1,0:T(4,128)S(1)} %bitcast.22, s32[64]{0:T(128)S(1)} %copy-done.2, s32[2]{0:T(128)S(1)} %pad_add_fusion.spot), custom_call_target="tpu_custom_call" | custom-call | flops 2000000000 | bytes 100000 | tf_op jit(solution)/shard_map/pallas_call | solution.py:129
  7.8 1.0 %collective-permute-done.5.refs_6_ = bf16[2,32,1024]{2,1,0:T(8,128)(2,1)S(1)} collective-permute-done((bf16[2,32,1024]{2,1,0:T(8,128)(2,1)}, bf16[2,32,1024]{2,1,0:T(8,128)(2,1)S(1)}, u32[]{:S(2)}, u32[]{:S(2)}) %collective-permute-start.5) | collective-permute-done | bytes 131104 | tf_op jit(solution)/shard_map/ppermute | solution.py:242
  8.8 4.4 %collective-permute-done.4.refs_5_ = bf16[2,32,1024]{2,1,0:T(8,128)(2,1)S(1)} collective-permute-done((bf16[2,32,1024]{2,1,0:T(8,128)(2,1)}, bf16[2,32,1024]{2,1,0:T(8,128)(2,1)S(1)}, u32[]{:S(2)}, u32[]{:S(2)}) %collective-permute-start.4) | collective-permute-done | bytes 131104 | tf_op jit(solution)/shard_map/ppermute | solution.py:242
  13.2 2.2 %collective-permute-done.3.refs_4_ = bf16[2,32,1024]{2,1,0:T(8,128)(2,1)S(1)} collective-permute-done((bf16[2,32,1024]{2,1,0:T(8,128)(2,1)}, bf16[2,32,1024]{2,1,0:T(8,128)(2,1)S(1)}, u32[]{:S(2)}, u32[]{:S(2)}) %collective-permute-start.3) | collective-permute-done | bytes 131104 | tf_op jit(solution)/shard_map/ppermute | solution.py:242
  15.5 0.0 collective-permute-done.1.refs_2_
  15.5 0.0 collective-permute-done.2.refs_3_
  15.5 0.0 copy-done
  15.5 3.5 %shard_map.39 = (bf16[2,32,1024]{2,1,0:T(8,128)(2,1)S(1)}, bf16[2,32,1024]{2,1,0:T(8,128)(2,1)S(1)}, bf16[2,32,1024]{2,1,0:T(8,128)(2,1)S(1)}, f32[2,32,1024]{2,...) custom-call(bf16[2,32,1024]{2,1,0:T(8,128)(2,1)S(1)} %bitcast.21, ...), custom_call_target="tpu_custom_call" | custom-call | flops 6000000000 | bytes 6000000 | tf_op jit(solution)/shard_map/pallas_call | solution.py:222
  19.0 0.1 collective-permute-start.6
  19.1 4.1 %collective-permute-start.8 = (bf16[2,32,1024]{2,1,0:T(8,128)(2,1)S(1)}, bf16[2,32,1024]{2,1,0:T(8,128)(2,1)S(1)}, u32[]{:S(2)}, u32[]{:S(2)}) collective-permute-start(bf16[2,32,1024]{2,1,0:T(8,128)(2,1)S(1)} %get-tuple-element.26), channel_id=1, source_target_pairs={{0,248},{4,252},{8,20},{12,16},{16,8},{20,12},{24,36},{28,32},{32,... | collective-permute-start | bytes 393224 | tf_op jit(solution)/shard_map/ppermute | solution.py:242
  23.2 0.0 collective-permute-start.9
  23.2 2.5 %collective-permute-start.10 = (bf16[2,32,1024]{2,1,0:T(8,128)(2,1)S(1)}, bf16[2,32,1024]{2,1,0:T(8,128)(2,1)S(1)}, u32[]{:S(2)}, u32[]{:S(2)}) collective-permute-start(bf16[2,32,1024]{2,1,0:T(8,128)(2,1)S(1)} %get-tuple-element.28), channel_id=1, source_target_pairs={{0,244},{4,0},{8,12},{12,24},{16,4},{20,16},{24,28},{28,40},{32,20... | collective-permute-start | bytes 393224 | tf_op jit(solution)/shard_map/ppermute | solution.py:242
  25.8 0.0 collective-permute-done.6
  25.8 2.4 %collective-permute-start.7 = (bf16[2,32,1024]{2,1,0:T(8,128)(2,1)S(1)}, bf16[2,32,1024]{2,1,0:T(8,128)(2,1)S(1)}, u32[]{:S(2)}, u32[]{:S(2)}) collective-permute-start(bf16[2,32,1024]{2,1,0:T(8,128)(2,1)S(1)} %fusion), channel_id=1, source_target_pairs={{0,2},{1,3},{2,0},{3,1},{4,6},{5,7},{6,4},{7,5},{8,10},{9,11},{10,... | collective-permute-start | bytes 393224 | tf_op jit(solution)/shard_map/ppermute | solution.py:246
  28.2 0.0 collective-permute-done.8
  28.2 2.9 %collective-permute-done.9 = bf16[2,32,1024]{2,1,0:T(8,128)(2,1)S(1)} collective-permute-done((bf16[2,32,1024]{2,1,0:T(8,128)(2,1)S(1)}, bf16[2,32,1024]{2,1,0:T(8,128)(2,1)S(1)}, u32[]{:S(2)}, u32[]{:S(2)}) %collective-permute-start.9) | collective-permute-done | bytes 131104 | tf_op jit(solution)/shard_map/ppermute | solution.py:242
  31.1 0.0 collective-permute-done.10
  31.1 3.7 %collective-permute-done.7 = bf16[2,32,1024]{2,1,0:T(8,128)(2,1)S(1)} collective-permute-done((bf16[2,32,1024]{2,1,0:T(8,128)(2,1)S(1)}, bf16[2,32,1024]{2,1,0:T(8,128)(2,1)S(1)}, u32[]{:S(2)}, u32[]{:S(2)}) %collective-permute-start.7) | collective-permute-done | bytes 131104 | tf_op jit(solution)/shard_map/ppermute | solution.py:246
  34.8 0.8 %fusion.5 = f32[1,1,2,32,1024]{4,3,2,1,0:T(8,128)} fusion(f32[2,32,1024]{2,1,0:T(8,128)S(1)} %get-tuple-element.23, bf16[2,32,1024]{2,1,0:T(8,128)(2,1)S(1)} %collective-permute-done.10, bf16[2,32,1024]{2,1,0:T(8,128)(2,1)S(1)} %collective-permute-done.9, bf16[2,32,1024]{2,1,0:T(8,128)(2,1)S(1)} %collective-permute-done.8, ...), kind=kLoop, calls=%fused_computation.7 | loop fusion | flops 655360 | bytes 1179648 | tf_op jit(solution)/shard_map/broadcast_in_dim | solution.py:262
  (1 shorter events, 0.0 us)
Async XLA Ops:
  0.0 7.0 %collective-permute-start = (bf16[2,32,1024]{2,1,0:T(8,128)(2,1)}, bf16[2,32,1024]{2,1,0:T(8,128)(2,1)S(1)}, u32[]{:S(2)}, u32[]{:S(2)}) collective-permute-start(bf16[2,32,1024]{2,1,0:T(8,128)(2,1)} %bitcast.16), channel_id=1, source_target_pairs={{0,2},{1,3},{2,0},{3,1},{4,6},{5,7},{6,4},{7,5},{8,10},{9,11},{10,... | collective-permute-start | bytes 393224 | tf_op jit(solution)/shard_map/ppermute | solution.py:246
  1.4 7.4 %collective-permute-start.5 = (bf16[2,32,1024]{2,1,0:T(8,128)(2,1)}, bf16[2,32,1024]{2,1,0:T(8,128)(2,1)S(1)}, u32[]{:S(2)}, u32[]{:S(2)}) collective-permute-start(bf16[2,32,1024]{2,1,0:T(8,128)(2,1)} %bitcast.17), channel_id=1, source_target_pairs={{12,0},{8,4},{0,8},{4,12},{28,16},{24,20},{16,24},{20,28},{44,32},... | collective-permute-start | bytes 393224 | tf_op jit(solution)/shard_map/ppermute | solution.py:242
  4.6 8.6 %collective-permute-start.4 = (bf16[2,32,1024]{2,1,0:T(8,128)(2,1)}, bf16[2,32,1024]{2,1,0:T(8,128)(2,1)S(1)}, u32[]{:S(2)}, u32[]{:S(2)}) collective-permute-start(bf16[2,32,1024]{2,1,0:T(8,128)(2,1)} %bitcast.18), channel_id=1, source_target_pairs={{244,0},{0,4},{12,8},{24,12},{4,16},{16,20},{28,24},{40,28},{20,32... | collective-permute-start | bytes 393224 | tf_op jit(solution)/shard_map/ppermute | solution.py:242
  5.3 10.2 %collective-permute-start.3 = (bf16[2,32,1024]{2,1,0:T(8,128)(2,1)}, bf16[2,32,1024]{2,1,0:T(8,128)(2,1)S(1)}, u32[]{:S(2)}, u32[]{:S(2)}) collective-permute-start(bf16[2,32,1024]{2,1,0:T(8,128)(2,1)} %bitcast.19), channel_id=1, source_target_pairs={{248,0},{252,4},{20,8},{16,12},{8,16},{12,20},{36,24},{32,28},{24,... | collective-permute-start | bytes 393224 | tf_op jit(solution)/shard_map/ppermute | solution.py:242
  5.7 9.7 %collective-permute-start.1 = (bf16[2,32,1024]{2,1,0:T(8,128)(2,1)}, bf16[2,32,1024]{2,1,0:T(8,128)(2,1)S(1)}, u32[]{:S(2)}, u32[]{:S(2)}) collective-permute-start(bf16[2,32,1024]{2,1,0:T(8,128)(2,1)} %bitcast.20), channel_id=1, source_target_pairs={{0,1},{1,0},{2,3},{3,2},{4,5},{5,4},{6,7},{7,6},{8,9},{9,8},{10,11... | collective-permute-start | bytes 393224 | tf_op jit(solution)/shard_map/ppermute | solution.py:246
  6.4 0.7 %copy-start.1 = (s32[64,3]{0,1:T(4,128)S(1)}, s32[64,3]{0,1:T(4,128)}, u32[]{:S(2)}) copy-start(s32[64,3]{0,1:T(4,128)} %param.4) | copy-start | bytes 2308
  6.5 0.7 %copy-start.2 = (s32[64]{0:T(128)S(1)}, s32[64]{0:T(128)}, u32[]{:S(2)}) copy-start(s32[64]{0:T(128)} %occupied.1) | copy-start | bytes 772
  7.0 8.5 %collective-permute-start.2 = (bf16[2,32,1024]{2,1,0:T(8,128)(2,1)S(1)}, bf16[2,32,1024]{2,1,0:T(8,128)(2,1)S(1)}, u32[]{:S(2)}, u32[]{:S(2)}) collective-permute-start(bf16[2,32,1024]{2,1,0:T(8,128)(2,1)S(1)} %collective-permute-done.refs_1_), channel_id=1, source_target_pairs={{0,1},{1,0},{2,3},{3,2},{4,5},{5,4},{6,7},{7,6},{8,9},{9,8},{10,11... | collective-permute-start | bytes 393224 | tf_op jit(solution)/shard_map/ppermute | solution.py:246
  7.1 8.4 %copy-start = (bf16[1,1,2,32,1024]{4,3,2,1,0:T(8,128)(2,1)S(1)}, bf16[1,1,2,32,1024]{4,3,2,1,0:T(8,128)(2,1)}, u32[]{:S(2)}) copy-start(bf16[1,1,2,32,1024]{4,3,2,1,0:T(8,128)(2,1)} %param.3) | copy-start | bytes 393220
  19.0 6.8 %collective-permute-start.6 = (bf16[2,2,32,1024]{3,2,1,0:T(8,128)(2,1)S(1)}, bf16[2,2,32,1024]{3,2,1,0:T(8,128)(2,1)S(1)}, u32[]{:S(2)}, u32[]{:S(2)}) collective-permute-start(bf16[2,2,32,1024]{3,2,1,0:T(8,128)(2,1)S(1)} %get-tuple-element.24), channel_id=1, source_target_pairs={{0,1},{1,0},{2,3},{3,2},{4,5},{5,4},{6,7},{7,6},{8,9},{9,8},{10,11... | collective-permute-start | bytes 786440 | tf_op jit(solution)/shard_map/ppermute | solution.py:246
  19.1 9.1 %collective-permute-start.8 = (bf16[2,32,1024]{2,1,0:T(8,128)(2,1)S(1)}, bf16[2,32,1024]{2,1,0:T(8,128)(2,1)S(1)}, u32[]{:S(2)}, u32[]{:S(2)}) collective-permute-start(bf16[2,32,1024]{2,1,0:T(8,128)(2,1)S(1)} %get-tuple-element.26), channel_id=1, source_target_pairs={{0,248},{4,252},{8,20},{12,16},{16,8},{20,12},{24,36},{28,32},{32,... | collective-permute-start | bytes 393224 | tf_op jit(solution)/shard_map/ppermute | solution.py:242
  23.2 7.8 %collective-permute-start.9 = (bf16[2,32,1024]{2,1,0:T(8,128)(2,1)S(1)}, bf16[2,32,1024]{2,1,0:T(8,128)(2,1)S(1)}, u32[]{:S(2)}, u32[]{:S(2)}) collective-permute-start(bf16[2,32,1024]{2,1,0:T(8,128)(2,1)S(1)} %get-tuple-element.27), channel_id=1, source_target_pairs={{0,12},{4,8},{8,0},{12,4},{16,28},{20,24},{24,16},{28,20},{32,44},... | collective-permute-start | bytes 393224 | tf_op jit(solution)/shard_map/ppermute | solution.py:242
  23.2 7.8 %collective-permute-start.10 = (bf16[2,32,1024]{2,1,0:T(8,128)(2,1)S(1)}, bf16[2,32,1024]{2,1,0:T(8,128)(2,1)S(1)}, u32[]{:S(2)}, u32[]{:S(2)}) collective-permute-start(bf16[2,32,1024]{2,1,0:T(8,128)(2,1)S(1)} %get-tuple-element.28), channel_id=1, source_target_pairs={{0,244},{4,0},{8,12},{12,24},{16,4},{20,16},{24,28},{28,40},{32,20... | collective-permute-start | bytes 393224 | tf_op jit(solution)/shard_map/ppermute | solution.py:242
  25.8 9.0 %collective-permute-start.7 = (bf16[2,32,1024]{2,1,0:T(8,128)(2,1)S(1)}, bf16[2,32,1024]{2,1,0:T(8,128)(2,1)S(1)}, u32[]{:S(2)}, u32[]{:S(2)}) collective-permute-start(bf16[2,32,1024]{2,1,0:T(8,128)(2,1)S(1)} %fusion), channel_id=1, source_target_pairs={{0,2},{1,3},{2,0},{3,1},{4,6},{5,7},{6,4},{7,5},{8,10},{9,11},{10,... | collective-permute-start | bytes 393224 | tf_op jit(solution)/shard_map/ppermute | solution.py:246
